TPU v7x, 128 devices: a whole 4x4x4 slice. The times are simulated.
128 devices in a mesh: dp: 16 (over x, y_lo, core), seq: 8 (over z, y_hi).
Axes of the slice: x: 4, y: 4 (y_hi: 2, y_lo: 2; y = y_hi * 2 + y_lo), z: 4, core: 2. Of those that a mesh axis runs over, the one named last changes fastest.
Arguments:
- queries: bfloat16 [16, 2048, 2048], P('dp', 'seq'), may hold values from -6 to 6
- keys: bfloat16 [16, 2048, 1024], P('dp', 'seq'), may hold values from -6 to 6
- values: bfloat16 [16, 2048, 1024], P('dp', 'seq'), may hold values from -190 to 190
- segments: int32 [16, 2048], P('dp', 'seq'), may hold values from 0 to 2, never falling along the last dimension, each value on 1 to 1280 neighbouring positions
- cotangent: bfloat16 [16, 2048, 2304], P('dp', 'seq'), may hold values from -6 to 6
- weight: float32 [2048, 2304], P(('dp', 'seq')), may hold values from -0.125 to 0.125
- first_moment: bfloat16 [2048, 2304], P(('dp', 'seq')), may hold values from -1 to 1
- first_scale: float32 [2048, 18], P(('dp', 'seq')), may hold values from 0.3 to 3
- second_moment: bfloat16 [2048, 2304], P(('dp', 'seq')), may hold values from 0.049804688 to 1
- second_scale: float32 [2048, 18], P(('dp', 'seq')), may hold values from 0.3 to 3
Outputs:
- layer_out: bfloat16 [16, 2048, 2304], P('dp', 'seq')
- new_weight: float32 [2048, 2304], P(('dp', 'seq'))
- new_first: bfloat16 [2048, 2304], P(('dp', 'seq'))
- new_first_scale: float32 [2048, 18], P(('dp', 'seq'))
- new_second: bfloat16 [2048, 2304], P(('dp', 'seq'))
- new_second_scale: float32 [2048, 18], P(('dp', 'seq'))
Inputs may be any that keep to these rules, and one draw needn't show every extreme that they name: `segments`: document numbers never fall along a sequence; each sequence holds 3 documents, one of exactly 1280 positions.
All inputs are finite; a program needn't handle non-finite values. Where the computation divides by a largest or mean magnitude, that divisor is 1e-20 or more.
Results may differ from a plain program's by a relative error of at most 0.01.
Values may be sent and summed in bfloat16 or wider, within the bound.
No kernel may reach another device: no remote copies, remote signals or barrier semaphores. Data moves between devices by JAX's collectives and lax.ppermute only.
A program may use at most 128 MiB of HBM per device.

v0:
```python
import math

import jax
import jax.numpy as jnp
from jax import lax
from jax.sharding import Mesh
from jax.sharding import PartitionSpec as P

HEADS = 16
KV_HEADS = 8
HEAD_DIM = 128
DO = 2304
GROUP = 128
QW = 2048
SEQ = ("seq_0", "seq_1")
DP = ("dp_0", "dp_1", "dp_2")
DP_SEQ = ("dp_0", "dp_1", "dp_2", "seq_0", "seq_1")


score_scale = 144.0 ** (-0.5)
soft_cap = 50.0
beta_first = 0.9
beta_second = 0.95
learn_rate = 0.001
decay_rate = 0.1


def side_by_side(arrays, axis, dim, along):
    widths = [math.prod(a.shape[along:]) for a in arrays]
    both = jnp.concatenate(
        [a.reshape(*a.shape[:along], w) for a, w in zip(arrays, widths)], axis=along
    )
    result = lax.all_gather(both, axis, axis=dim, tiled=True)
    parts = jnp.split(result, [sum(widths[:k]) for k in range(1, len(widths))], axis=along)
    return tuple(
        (b.reshape(*result.shape[:along], *a.shape[along:]) for a, b in zip(arrays, parts))
    )


def sent_to_all(x, axis):
    peers = lax.axis_size(axis)
    return lax.all_to_all(jnp.broadcast_to(x[None], (peers, *x.shape)), axis, 0, 0, tiled=True)


def laid_out(parts, dim):
    parts = jnp.moveaxis(parts, 0, dim)
    dims = parts.shape
    return parts.reshape(*dims[:dim], dims[dim] * dims[dim + 1], *dims[dim + 2 :])


def gather_directly(x, axis, dim):
    parts = sent_to_all(x, axis)
    return laid_out(parts, dim)


def split_up(x, dim, peers):
    dims = x.shape
    parts = x.reshape(*dims[:dim], peers, dims[dim] // peers, *dims[dim + 1 :])
    return jnp.moveaxis(parts, dim, 0)


def summed_on_arrival(x, axis, dim):
    parts = split_up(x, dim, lax.axis_size(axis))
    arrived = lax.all_to_all(parts, axis, split_axis=0, concat_axis=0, tiled=True)
    return arrived.astype(jnp.float32).sum(axis=0)


def by_axis(x, axes):
    for axis in axes:
        x = lax.psum(x, axis)
    return x


def quantize(blocks):
    grouped = blocks.astype(jnp.float32).reshape(blocks.shape[0], KV_HEADS, HEAD_DIM)
    scales = (jnp.max(jnp.abs(grouped), axis=-1) + 1e-06).astype(jnp.bfloat16)
    coded = (grouped / scales.astype(jnp.float32)[..., None]).astype(jnp.bfloat16)
    return (coded, scales)


def recover_values(coded, scales):
    return (coded.astype(jnp.float32) * scales.astype(jnp.float32)[..., None]).astype(jnp.bfloat16)


def decode(coded, scales):
    values_f = coded.astype(jnp.float32).reshape(coded.shape[0], -1, GROUP)
    return (scales[..., None] * jnp.sign(values_f) * jnp.sqrt(jnp.abs(values_f))).reshape(
        coded.shape
    )


def encode(moment):
    grouped = moment.reshape(moment.shape[0], -1, GROUP)
    scales = jnp.max(jnp.abs(grouped), axis=-1) + 1e-06
    coded = (grouped * jnp.abs(grouped) / (scales[..., None] * scales[..., None])).astype(
        jnp.bfloat16
    )
    return (coded.reshape(moment.shape), scales)


def local(
    queries,
    keys,
    values,
    segments,
    cotangent,
    weight,
    first_moment,
    first_scale,
    second_moment,
    second_scale,
):
    query_rows = queries[0]
    tokens_here = query_rows.shape[0]
    repeat_heads = HEADS // KV_HEADS
    grouped_queries = query_rows.reshape(tokens_here, KV_HEADS, repeat_heads, HEAD_DIM)
    positions = lax.axis_index(SEQ) * tokens_here + jnp.arange(tokens_here, dtype=jnp.int32)
    own_docs = segments[0]
    key_codes, key_scale_factors = quantize(keys[0])
    value_codes, value_scale_factors = quantize(values[0])
    portion_keys, portion_key_scale, piece_values, piece_vscale, piece_docs = (
        *side_by_side((key_codes, key_scale_factors, value_codes, value_scale_factors), SEQ, 0, 2),
        lax.all_gather(own_docs, SEQ, axis=0, tiled=True),
    )
    count_rows = portion_keys.shape[0]
    key_estimate = recover_values(portion_keys, portion_key_scale)
    value_hat = recover_values(piece_values, piece_vscale)
    scores = (
        jnp.einsum(
            "qgrd,kgd->qgrk", grouped_queries, key_estimate, preferred_element_type=jnp.float32
        )
        * score_scale
    )
    capped = soft_cap * jnp.tanh(scores / soft_cap)
    key_places = jnp.arange(count_rows, dtype=jnp.int32)
    allowed = (own_docs[:, None] == piece_docs[None, :]) & (
        key_places[None, :] <= positions[:, None]
    )
    weights = jnp.where(allowed[:, None, None, :], jnp.exp(capped), jnp.float32(0.0))
    denom = jnp.sum(weights, axis=-1)
    numer = jnp.einsum(
        "qgrk,kgd->qgrd",
        weights.astype(jnp.bfloat16),
        value_hat,
        preferred_element_type=jnp.float32,
    )
    numer, denom = (numer, denom)
    attended = (
        (numer / denom[..., None]).reshape(tokens_here, HEADS * HEAD_DIM).astype(jnp.bfloat16)
    )
    weight_low = weight.astype(jnp.bfloat16)
    group_rows = gather_directly(weight_low, SEQ, 0)
    columns = attended
    projected = jnp.dot(
        columns,
        lax.all_gather(group_rows, DP, axis=0, tiled=True),
        preferred_element_type=jnp.float32,
    )
    layer_out = projected.astype(jnp.bfloat16)[None]
    cot_rows = cotangent[0]
    columns = attended
    group_sum = lax.psum_scatter(
        lax.dot_general(
            columns, cot_rows, (((0,), (0,)), ((), ())), preferred_element_type=jnp.float32
        ).astype(jnp.bfloat16),
        DP,
        scatter_dimension=0,
        tiled=True,
    )
    gradient_matrix = summed_on_arrival(group_sum, SEQ, 0)
    sum_squares = by_axis(jnp.sum(gradient_matrix * gradient_matrix), DP_SEQ)
    rms_value = jnp.sqrt(sum_squares / (QW * DO) + 1e-06)
    clipped = gradient_matrix * jnp.minimum(jnp.float32(1.0), 1.0 / rms_value)
    first = beta_first * decode(first_moment, first_scale) + (1.0 - beta_first) * clipped
    second = (
        beta_second * decode(second_moment, second_scale) + (1.0 - beta_second) * clipped * clipped
    )
    new_weight = weight - learn_rate * (first / (jnp.sqrt(second) + 1e-08) + decay_rate * weight)
    new_first, new_first_scale = encode(first)
    new_second, new_second_scale = encode(second)
    return (layer_out, new_weight, new_first, new_first_scale, new_second, new_second_scale)


def solution(mesh):
    finer = Mesh(mesh.devices.reshape(4, 2, 2, 4, 2), ("dp_0", "dp_1", "dp_2", "seq_0", "seq_1"))
    placed = (
        P(DP, SEQ, None),
        P(DP, SEQ, None),
        P(DP, SEQ, None),
        P(DP, SEQ),
        P(DP, SEQ, None),
        P(DP_SEQ, None),
        P(DP_SEQ, None),
        P(DP_SEQ, None),
        P(DP_SEQ, None),
        P(DP_SEQ, None),
    )
    return jax.shard_map(
        local,
        mesh=finer,
        in_specs=placed,
        out_specs=(
            P(DP, SEQ, None),
            P(DP_SEQ, None),
            P(DP_SEQ, None),
            P(DP_SEQ, None),
            P(DP_SEQ, None),
            P(DP_SEQ, None),
        ),
        check_vma=False,
    )
```

profile of v0, /device:TPU:1, one launch (start us, length us, event | category | flops | bytes accessed | tf_op | source)
XLA Modules:
  0.0 414.0 jit_solution(12219922689015739856)
XLA Ops:
  7.2 0.0 copy-start
  7.2 0.0 copy-start.1
  7.2 0.0 copy-start.8
  7.2 0.0 all-gather.4.cloned.1.call-start
  7.2 1.4 copy.58
  8.6 0.1 fusion.22
  8.8 1.2 copy.61
  10.0 0.1 fusion.24
  10.2 0.2 fusion.23
  10.4 1.2 pad_maximum_fusion
  11.5 0.0 all-gather.4.cloned.1.call-update
  11.6 0.0 reduce-scatter.2.cloned.1.call-start
  11.6 0.0 copy-done.1
  11.6 0.8 reshape_squeeze.3
  12.4 0.0 copy-done.8
  12.4 21.9 %all-gather = s32[1,2048]{1,0:T(1,128)S(1)} all-gather(s32[1,256]{1,0:T(1,128)S(1)} %copy-done.8), channel_id=2, replica_groups=mesh['dp_0'=4,'dp_1'=2,'dp_2'=2,'seq_0'=4,'seq_1'=2] {'seq_0','seq_1'}, dimensions={1}, use_global_device_ids=true | all-gather | bytes 9216 | tf_op jit(solution)/shard_map/all_gather | solution.py:123
  34.3 0.5 fusion.16
  34.8 0.0 copy-start.2
  34.8 95.7 %all-gather.4.cloned.1.call-done = bf16[2048,8,258]{0,2,1:T(8,128)(2,1)} async-done(((bf16[256,8,258]{0,2,1:T(8,128)(2,1)}), bf16[2048,8,258]{0,2,1:T(8,128)(2,1)}) %all-gather.4.cloned.1.call-update) | async-done | bytes 8454160 | tf_op jit(solution)/shard_map/all_gather | solution.py:33
  130.5 1.1 slice_convert_fusion.1
  131.7 16.7 %fusion = (f32[256,8,2]{0,2,1:T(2,128)S(1)}, f32[8,2048,256,2]{2,1,3,0:T(8,128)}) fusion(pred[256,2048]{0,1:T(8,128)(4,1)S(1)} %fusion.16, bf16[256,8,2,128]{3,2,1,0:T(2,128)(2,1)S(1)} %reshape_squeeze.3, bf16[2048,8,258]{0,2,1:T(8,128)(2,1)} %all-gather.4.cloned.1.call-done, f32[2048,8]{0,1:T(8,128)S(1)} %bitcast.85), kind=kOutput, calls=%fused_computation.1 | convolution fusion | flops 2187325440 | bytes 39403520 | tf_op jit(solution)/shard_map/qgrd,kgd->qgrk/dot_general | solution.py:129
  148.4 0.0 copy-done.2
  148.4 17.4 %fusion.15 = bf16[256,8,2,128]{0,3,2,1:T(8,128)(2,1)S(1)} fusion(f32[8,2048,256,2]{2,1,3,0:T(8,128)} %get-tuple-element.27, pred[256,2048]{0,1:T(8,128)(4,1)} %copy-done.2, bf16[2048,8,258]{0,2,1:T(8,128)(2,1)} %all-gather.4.cloned.1.call-done, f32[2048,8]{0,1:T(8,128)S(1)} %bitcast.84, f32[256,8,2]{0,2,1:T(2,128)S(1)} %get-tuple-element.26), kind=kOutput, calls=%fused_computation.18 | convolution fusion | flops 2188378112 | bytes 39403520 | tf_op jit(solution)/shard_map/qgrk,kgd->qgrd/dot_general | solution.py:141
  165.9 0.0 copy-done
  165.9 5.0 %convolution_convert_fusion = bf16[2048,2304]{1,0:T(8,128)(2,1)} fusion(bf16[256,2048]{0,1:T(8,128)(2,1)S(1)} %bitcast.72, bf16[1,256,2304]{2,1,0:T(8,128)(2,1)S(1)} %copy-done), kind=kOutput, calls=%fused_computation.5 | convolution fusion | flops 2420637696 | bytes 11665408 | tf_op jit(solution)/shard_map/dot_general | solution.py:163
  170.9 0.0 copy-start.6
  170.9 0.0 copy-start.7
  170.9 0.0 copy-start.4
  171.0 0.0 copy-start.5
  171.0 0.0 copy-start.3
  171.0 0.0 reduce-scatter.2.cloned.1.call-update
  171.0 0.0 all-gather.6.cloned.1.call-start
  171.0 105.1 %reduce-scatter.2.cloned.1.call-done = bf16[128,2304]{1,0:T(8,128)(2,1)} async-done(((bf16[2048,2304]{1,0:T(8,128)(2,1)}), bf16[128,2304]{1,0:T(8,128)(2,1)}) %reduce-scatter.2.cloned.1.call-update) | async-done | bytes 589840 | tf_op jit(solution)/shard_map/reduce_scatter | solution.py:162
  276.1 17.8 %all_to_all.10 = bf16[8,16,2304]{2,1,0:T(8,128)(2,1)S(1)} all-to-all(bf16[8,16,2304]{2,1,0:T(8,128)(2,1)} %bitcast.83), channel_id=1, replica_groups=mesh['dp_0'=4,'dp_1'=2,'dp_2'=2,'seq_0'=4,'seq_1'=2] {'seq_0','seq_1'}, dimensions={0} | all-to-all | bytes 1179648 | tf_op jit(solution)/shard_map/all_to_all | solution.py:64
  293.9 0.1 convert_reduce_fusion
  294.0 0.6 multiply_reduce_fusion
  294.7 9.4 %psum.35 = f32[]{:T(128)} all-reduce(f32[]{:T(128)} %multiply_reduce_fusion), channel_id=1, replica_groups=mesh['dp_0'=4,'dp_1'=2,'dp_2'=2,'seq_0'=4,'seq_1'=2] {'dp_0'}, use_global_device_ids=true, to_apply=%region_6.7 | all-reduce | flops 1 | bytes 8 | tf_op jit(solution)/shard_map/psum | solution.py:70
  304.1 4.6 %psum.36 = f32[]{:T(128)} all-reduce(f32[]{:T(128)} %psum.35), channel_id=1, replica_groups=mesh['dp_0'=4,'dp_1'=2,'dp_2'=2,'seq_0'=4,'seq_1'=2] {'dp_1'}, use_global_device_ids=true, to_apply=%region_7.8 | all-reduce | flops 1 | bytes 8 | tf_op jit(solution)/shard_map/psum | solution.py:70
  308.7 5.0 %psum.37 = f32[]{:T(128)} all-reduce(f32[]{:T(128)} %psum.36), channel_id=1, replica_groups=mesh['dp_0'=4,'dp_1'=2,'dp_2'=2,'seq_0'=4,'seq_1'=2] {'dp_2'}, use_global_device_ids=true, to_apply=%region_8.9 | all-reduce | flops 1 | bytes 8 | tf_op jit(solution)/shard_map/psum | solution.py:70
  313.7 7.5 %psum.38 = f32[]{:T(128)} all-reduce(f32[]{:T(128)} %psum.37), channel_id=1, replica_groups=mesh['dp_0'=4,'dp_1'=2,'dp_2'=2,'seq_0'=4,'seq_1'=2] {'seq_0'}, use_global_device_ids=true, to_apply=%region_9.10 | all-reduce | flops 1 | bytes 8 | tf_op jit(solution)/shard_map/psum | solution.py:70
  321.2 5.9 %psum.39 = f32[]{:T(128)} all-reduce(f32[]{:T(128)} %psum.38), channel_id=1, replica_groups=mesh['dp_0'=4,'dp_1'=2,'dp_2'=2,'seq_0'=4,'seq_1'=2] {'seq_1'}, use_global_device_ids=true, to_apply=%region_10.11 | all-reduce | flops 1 | bytes 8 | tf_op jit(solution)/shard_map/psum | solution.py:70
  327.8 0.0 copy-done.6
  327.8 0.1 mul.145
  327.9 0.0 copy-done.7
  327.9 0.1 mul.155
  328.0 0.0 copy-done.4
  328.0 0.0 copy-done.5
  328.1 0.2 fusion.47
  328.3 0.1 reduce_max.38
  328.5 0.6 fusion.49
  329.1 0.1 reduce_max.39
  329.2 0.6 fusion.46
  329.8 0.1 div.68
  329.9 0.1 div.71
  330.1 0.0 copy-done.3
  330.1 0.8 fusion.37
  330.9 12.7 %all_to_all.11 = bf16[8,16,2304]{2,1,0:T(8,128)(2,1)} all-to-all(bf16[8,16,2304]{2,1,0:T(8,128)(2,1)S(1)} %broadcast_in_dim.18), channel_id=1, replica_groups=mesh['dp_0'=4,'dp_1'=2,'dp_2'=2,'seq_0'=4,'seq_1'=2] {'seq_0','seq_1'}, dimensions={0} | all-to-all | bytes 1179648 | tf_op jit(solution)/shard_map/all_to_all | solution.py:42
  343.6 0.0 all-gather.6.cloned.1.call-update
  343.6 56.5 %all-gather.6.cloned.1.call-done = bf16[2048,2304]{1,0:T(8,128)(2,1)} async-done(((bf16[128,2304]{1,0:T(8,128)(2,1)}), bf16[2048,2304]{1,0:T(8,128)(2,1)}) %all-gather.6.cloned.1.call-update) | async-done | bytes 9437200 | tf_op jit(solution)/shard_map/all_gather | solution.py:156
  400.2 7.3 %fusion.14 = bf16[1,256,2304]{2,1,0:T(8,128)(2,1)} fusion(bf16[256,2048]{0,1:T(8,128)(2,1)S(1)} %bitcast.73, bf16[2048,2304]{1,0:T(8,128)(2,1)} %all-gather.6.cloned.1.call-done), kind=kOutput, calls=%fused_computation.16 | convolution fusion | flops 2416508928 | bytes 11665408 | tf_op jit(solution)/shard_map/dot_general | solution.py:154
  (10 shorter events, 0.2 us)
Async XLA Ops:
  7.2 158.7 %copy-start = (bf16[1,256,2304]{2,1,0:T(8,128)(2,1)S(1)}, bf16[1,256,2304]{2,1,0:T(8,128)(2,1)}, u32[]{:S(2)}) copy-start(bf16[1,256,2304]{2,1,0:T(8,128)(2,1)} %param.14) | copy-start | bytes 3538948
  7.2 4.4 %copy-start.1 = (bf16[1,256,2048]{2,1,0:T(8,128)(2,1)S(1)}, bf16[1,256,2048]{2,1,0:T(8,128)(2,1)}, u32[]{:S(2)}) copy-start(bf16[1,256,2048]{2,1,0:T(8,128)(2,1)} %param.10) | copy-start | bytes 3145732
  7.2 5.2 %copy-start.8 = (s32[1,256]{1,0:T(1,128)S(1)}, s32[1,256]{1,0:T(1,128)}, u32[]{:S(2)}) copy-start(s32[1,256]{1,0:T(1,128)} %param.13) | copy-start | bytes 3076
  7.2 123.3 %all-gather.4.cloned.1.call-start = ((), (), s32[]{:S(2)}) async-start(), calls=%async_computation.3 | async-start | bytes 9732096 | tf_op jit(solution)/shard_map/all_gather | solution.py:33
  11.6 264.6 %reduce-scatter.2.cloned.1.call-start = ((), (), s32[]{:S(2)}) async-start(), calls=%async_computation.5 | async-start | bytes 10027008 | tf_op jit(solution)/shard_map/reduce_scatter | solution.py:162
  34.8 113.6 %copy-start.2 = (pred[256,2048]{0,1:T(8,128)(4,1)}, pred[256,2048]{0,1:T(8,128)(4,1)S(1)}, u32[]{:S(2)}) copy-start(pred[256,2048]{0,1:T(8,128)(4,1)S(1)} %fusion.16) | copy-start | bytes 1572868
  170.9 156.8 %copy-start.6 = (f32[16,18]{1,0:T(8,128)S(1)}, f32[16,18]{1,0:T(8,128)}, u32[]{:S(2)}) copy-start(f32[16,18]{1,0:T(8,128)} %param.17) | copy-start | bytes 3460
  170.9 157.0 %copy-start.7 = (f32[16,18]{1,0:T(8,128)S(1)}, f32[16,18]{1,0:T(8,128)}, u32[]{:S(2)}) copy-start(f32[16,18]{1,0:T(8,128)} %param.19) | copy-start | bytes 3460
  170.9 157.1 %copy-start.4 = (bf16[16,2304]{1,0:T(8,128)(2,1)S(1)}, bf16[16,2304]{1,0:T(8,128)(2,1)}, u32[]{:S(2)}) copy-start(bf16[16,2304]{1,0:T(8,128)(2,1)} %param.18) | copy-start | bytes 221188
  171.0 157.1 %copy-start.5 = (bf16[16,2304]{1,0:T(8,128)(2,1)S(1)}, bf16[16,2304]{1,0:T(8,128)(2,1)}, u32[]{:S(2)}) copy-start(bf16[16,2304]{1,0:T(8,128)(2,1)} %param.16) | copy-start | bytes 221188
  171.0 159.1 %copy-start.3 = (f32[16,2304]{1,0:T(8,128)S(1)}, f32[16,2304]{1,0:T(8,128)}, u32[]{:S(2)}) copy-start(f32[16,2304]{1,0:T(8,128)} %param.15) | copy-start | bytes 442372
  171.0 229.2 %all-gather.6.cloned.1.call-start = ((), (), s32[]{:S(2)}) async-start(), calls=%async_computation.4 | async-start | bytes 10027008 | tf_op jit(solution)/shard_map/all_gather | solution.py:156
Sparse Core Ops, SparseCore 0:
  11.7 118.8 all-gather.3
  171.1 104.9 reduce-scatter.1
  343.7 56.3 all-gather.5
where the time goes:
time: 414 us
  waiting for transfers between devices  257 us (62%)
  blocking collectives  84.8 us (20%)
  matrix products  46.5 us (11%)
  between operations  14.7 us (4%)
  other arithmetic  6.43 us (2%)
    reduce_scatter x1, waiting for transfers between devices, local(): lax.psum_scatter(lax.dot_general(columns, cot_rows, (((0,), (0,)), ((), (...  105 us
    all_gather x1, waiting for transfers between devices, side_by_side(): result = lax.all_gather(both, axis, axis=dim, tiled=True)  95.7 us
    all_gather x1, waiting for transfers between devices, local(): lax.all_gather(group_rows, DP, axis=0, tiled=True)  56.5 us
    psum x5, blocking collectives, by_axis(): x = lax.psum(x, axis)  32.4 us
    all_gather x1, blocking collectives, local(): lax.all_gather(own_docs, SEQ, axis=0, tiled=True)  21.9 us
    all_to_all x1, blocking collectives, summed_on_arrival(): lax.all_to_all(parts, axis, split_axis=0, concat_axis=0, tiled=True)  17.8 us
    dot_general x1, matrix products, local(): jnp.einsum('qgrk,kgd->qgrd', weights.astype(jnp.bfloat16), value_hat, pre...  17.4 us
    dot_general x1, matrix products, local(): jnp.einsum('qgrd,kgd->qgrk', grouped_queries, key_estimate, preferred_ele...  16.7 us
  transfers between devices with their start and end apart: 3, of which 3 were waited for; matrix products, arithmetic and copies ran while one was open for 0% of the time, Pallas kernels for 0%

commit v1 on v0

v1 whole, which is shorter than its diff:
```python
import jax
import jax.numpy as jnp
from jax import lax
from jax.experimental import pallas as pl
from jax.experimental.pallas import tpu as pltpu
from jax.sharding import Mesh
from jax.sharding import PartitionSpec as P

QW = 2048
DO = 2304
GROUP = 128
TILE = 256
BLOCKS = 8
NOTE = 16
SEQ = ("seq_0", "seq_1")
DP = ("dp_0", "dp_1", "dp_2")
DP_SEQ = ("dp_0", "dp_1", "dp_2", "seq_0", "seq_1")
LOG2E = 1.4426950408889634
VMEM_LIMIT = 48 * 1024 * 1024

score_scale = 144.0 ** (-0.5)
soft_cap = 50.0
beta_first = 0.9
beta_second = 0.95
learn_rate = 0.001
decay_rate = 0.1

F32 = jnp.float32
BF16 = jnp.bfloat16


def params(*semantics):
    return pltpu.CompilerParams(
        vmem_limit_bytes=VMEM_LIMIT,
        dimension_semantics=semantics or None,
    )


def restored(entries):
    wide = entries.astype(F32)
    scale = (jnp.max(jnp.abs(wide), axis=-1, keepdims=True) + 1e-06).astype(BF16).astype(F32)
    coded = (wide / scale).astype(BF16).astype(F32)
    return (coded * scale).astype(BF16)


def pack_kernel(q_ref, k_ref, v_ref, seg_ref, out_ref):
    out_ref[0, :TILE, 0:256] = q_ref[...]
    out_ref[0, :TILE, 256:384] = restored(k_ref[...])
    out_ref[0, :TILE, 384:512] = restored(v_ref[...])
    seg = seg_ref[...]
    below_1 = jnp.sum((seg < 1).astype(F32), axis=-1, keepdims=True)
    below_2 = jnp.sum((seg < 2).astype(F32), axis=-1, keepdims=True)
    out_ref[0, TILE:, 0:256] = jnp.broadcast_to(below_1, (NOTE, 256)).astype(BF16)
    out_ref[0, TILE:, 256:512] = jnp.broadcast_to(below_2, (NOTE, 256)).astype(BF16)


def pack(q, k, v, seg):
    return pl.pallas_call(
        pack_kernel,
        grid=(BLOCKS,),
        in_specs=[
            pl.BlockSpec((TILE, 256), lambda h: (0, h)),
            pl.BlockSpec((TILE, 128), lambda h: (0, h)),
            pl.BlockSpec((TILE, 128), lambda h: (0, h)),
            pl.BlockSpec((1, TILE), lambda h: (0, 0)),
        ],
        out_specs=pl.BlockSpec((1, TILE + NOTE, 512), lambda h: (h, 0, 0)),
        out_shape=jax.ShapeDtypeStruct((BLOCKS, TILE + NOTE, 512), BF16),
        compiler_params=params("arbitrary"),
        name="pack",
    )(q, k, v, seg)


def attend_kernel(in_ref, out_ref, acc, total):
    notes = in_ref[:, TILE : TILE + 8, :].astype(F32).sum(axis=0)
    first_of_1 = jnp.max(notes[:, 0:128]).astype(jnp.int32)
    first_of_2 = jnp.max(notes[:, 256:384]).astype(jnp.int32)

    def first_seen(place):
        return jnp.where(
            place < first_of_1, 0, jnp.where(place < first_of_2, first_of_1, first_of_2)
        )

    key_row = lax.broadcasted_iota(jnp.int32, (TILE, 2 * TILE), 0)
    lane = lax.broadcasted_iota(jnp.int32, (1, 2 * TILE), 1)
    query_col = jnp.where(lane < TILE, lane, lane - TILE)

    for i in range(BLOCKS):
        query = jnp.concatenate([in_ref[i, :TILE, 0:128], in_ref[i, :TILE, 128:256]], axis=0)
        start_row = first_seen(i * TILE + query_col)
        start_low = first_seen(jnp.int32(i * TILE))
        start_high = first_seen(jnp.int32(i * TILE + TILE - 1))
        acc[...] = jnp.zeros_like(acc)
        total[...] = jnp.zeros_like(total)

        def step(j, mask, query=query):
            key = in_ref[j, :TILE, 256:384]
            value = in_ref[j, :TILE, 384:512]
            scores = lax.dot_general(
                key, query, (((1,), (1,)), ((), ())), preferred_element_type=F32
            )
            capped = jnp.tanh(scores * (score_scale / soft_cap))
            weights = jnp.exp2(capped * (soft_cap * LOG2E))
            if mask is not None:
                weights = jnp.where(mask, weights, 0.0)
            total[...] += weights.reshape(TILE // 8, 8, 2 * TILE).sum(axis=0)
            acc[...] += lax.dot_general(
                value, weights.astype(BF16), (((0,), (0,)), ((), ())), preferred_element_type=F32
            )

        low = start_low // TILE
        clear = jnp.minimum((start_high + TILE - 1) // TILE, i)

        @pl.loop(low, clear)
        def _(j):
            step(j, key_row + j * TILE >= start_row)

        @pl.loop(clear, i)
        def _(j):
            step(j, None)

        step(i, (key_row <= query_col) & (key_row + i * TILE >= start_row))

        attended = (acc[...] / jnp.sum(total[...], axis=0, keepdims=True)).astype(BF16)
        for x in range(4):
            for c in range(2):
                out_ref[(x * 2 + c) * BLOCKS + i] = attended[
                    x * 32 : (x + 1) * 32, c * TILE : (c + 1) * TILE
                ]


def attend(packed):
    return pl.pallas_call(
        attend_kernel,
        out_shape=jax.ShapeDtypeStruct((64, 32, TILE), BF16),
        in_specs=[pl.BlockSpec(memory_space=pltpu.VMEM)],
        out_specs=pl.BlockSpec(memory_space=pltpu.VMEM),
        scratch_shapes=[pltpu.VMEM((128, 2 * TILE), F32), pltpu.VMEM((8, 2 * TILE), F32)],
        compiler_params=params(),
        name="attend",
    )(packed)


def gradient_kernel(me_ref, att_ref, *refs):
    cots, out_ref = refs[:8], refs[8]
    x, c = me_ref[0], me_ref[2]
    total = jnp.zeros((256, TILE), F32)
    for core in range(2):
        for k in range(4):
            member = lax.rem(x - k + 4, 4) * 2 + (c if core == 0 else 1 - c)
            total += jnp.dot(
                att_ref[member], cots[core * 4 + k][...], preferred_element_type=F32
            )
    low = total.astype(BF16)
    for fx in range(4):
        for fy in range(2):
            for fh in range(2):
                row = ((fx * 2 + fy) * 2 + fh) * 16
                out_ref[(fy * 4 + fx) * 2 + fh] = low[row : row + 16]


def gradient_rows(me, att, cots):
    return pl.pallas_call(
        gradient_kernel,
        grid_spec=pltpu.PrefetchScalarGridSpec(
            num_scalar_prefetch=1,
            grid=(DO // TILE,),
            in_specs=[pl.BlockSpec((8, 256, TILE), lambda n, me: (0, 0, 0))]
            + [pl.BlockSpec((TILE, TILE), lambda n, me: (0, n))] * 8,
            out_specs=pl.BlockSpec((16, 16, TILE), lambda n, me: (0, 0, n)),
        ),
        out_shape=jax.ShapeDtypeStruct((16, 16, DO), BF16),
        compiler_params=params("arbitrary"),
        name="gradient_rows",
    )(me, att, *cots)


def project_kernel(me_ref, att_ref, *refs):
    rows, out_ref, left = refs[:8], refs[8], refs[9]
    x, c, z = me_ref[0], me_ref[2], me_ref[3]
    y = me_ref[4] * 2 + me_ref[1]

    @pl.when(pl.program_id(0) == 0)
    def _():
        for core in range(2):
            fc = c if core == 0 else 1 - c
            for kx in range(4):
                fx = lax.rem(x - kx + 4, 4)
                blocks = []
                for kz in range(4):
                    fz = lax.rem(z - kz + 4, 4)
                    for ky in range(4):
                        fy = lax.rem(y - ky + 4, 4)
                        low, high = lax.rem(fy, 2), fy // 2
                        blocks.append(att_ref[fz * 2 + fc, fx * 4 + low * 2 + high])
                left[core * 4 + kx] = jnp.concatenate(blocks, axis=0).T

    total = jnp.zeros((TILE, TILE), F32)
    for k in range(8):
        total += jnp.dot(left[k], rows[k][...], preferred_element_type=F32)
    out_ref[0] = total.astype(BF16)


def project(me, att, rows):
    return pl.pallas_call(
        project_kernel,
        grid_spec=pltpu.PrefetchScalarGridSpec(
            num_scalar_prefetch=1,
            grid=(DO // TILE,),
            in_specs=[pl.BlockSpec((8, 16, 16, TILE), lambda n, me: (0, 0, 0, 0))]
            + [pl.BlockSpec((TILE, TILE), lambda n, me: (0, n))] * 8,
            out_specs=pl.BlockSpec((1, TILE, TILE), lambda n, me: (0, 0, n)),
            scratch_shapes=[pltpu.VMEM((8, TILE, TILE), BF16)],
        ),
        out_shape=jax.ShapeDtypeStruct((1, TILE, DO), BF16),
        compiler_params=params("arbitrary"),
        name="project",
    )(me, att, *rows)


def total_kernel(parts_ref, grad_ref, squares_ref):
    total = parts_ref[0].astype(F32)
    for k in range(1, 16):
        total += parts_ref[k].astype(F32)
    grad_ref[...] = total
    squares = jnp.sum(total * total)
    squares_ref[...] = jnp.broadcast_to(squares, squares_ref.shape)


def total_rows(parts):
    return pl.pallas_call(
        total_kernel,
        out_shape=(
            jax.ShapeDtypeStruct((16, DO), F32),
            jax.ShapeDtypeStruct((128, 1, 128), F32),
        ),
        compiler_params=params(),
        name="total_rows",
    )(parts)


def adam_kernel(
    grad_ref, squares_ref, weight_ref, first_ref, fscale_ref, second_ref, sscale_ref,
    new_weight_ref, new_first_ref, new_fscale_ref, new_second_ref, new_sscale_ref,
):
    sum_squares = jnp.sum(squares_ref[:, 0, :]) * (1.0 / 128.0)
    rms = jnp.sqrt(jnp.full((16, GROUP), sum_squares * (1.0 / (QW * DO)) + 1e-06, F32))
    shrink = jnp.minimum(1.0, 1.0 / rms)

    def decode(coded, scale):
        magnitude = scale * jnp.sqrt(jnp.abs(coded))
        return jnp.where(coded < 0.0, -magnitude, magnitude)

    def encode(x):
        scale = jnp.max(jnp.abs(x), axis=-1, keepdims=True) + 1e-06
        return (x * jnp.abs(x) / (scale * scale)).astype(BF16), scale

    fscales, sscales = [], []
    for g in range(DO // GROUP):
        at = slice(g * GROUP, (g + 1) * GROUP)
        clipped = grad_ref[:, at] * shrink
        first_old = decode(first_ref[:, at].astype(F32), fscale_ref[:, g : g + 1])
        second_old = decode(second_ref[:, at].astype(F32), sscale_ref[:, g : g + 1])
        first = beta_first * first_old + (1.0 - beta_first) * clipped
        second = beta_second * second_old + (1.0 - beta_second) * clipped * clipped
        weight = weight_ref[:, at]
        new_weight_ref[:, at] = weight - learn_rate * (
            first / (jnp.sqrt(second) + 1e-08) + decay_rate * weight
        )
        new_first_ref[:, at], scale = encode(first)
        fscales.append(scale)
        new_second_ref[:, at], scale = encode(second)
        sscales.append(scale)
    new_fscale_ref[...] = jnp.concatenate(fscales, axis=1)
    new_sscale_ref[...] = jnp.concatenate(sscales, axis=1)


def adam(grad, squares, weight, first, fscale, second, sscale):
    return pl.pallas_call(
        adam_kernel,
        out_shape=tuple(
            jax.ShapeDtypeStruct(a.shape, a.dtype) for a in (weight, first, fscale, second, sscale)
        ),
        compiler_params=params(),
        name="adam",
    )(grad, squares, weight, first, fscale, second, sscale)


def shift(x, axis, by):
    peers = lax.axis_size(axis)
    return lax.ppermute(x, axis, [(i, (i + by) % peers) for i in range(peers)])


def shift_y(x, by):
    pairs = []
    for y in range(4):
        to = (y + by) % 4
        pairs.append(((y % 2) * 2 + y // 2, (to % 2) * 2 + to // 2))
    return lax.ppermute(x, ("dp_1", "seq_1"), pairs)


def from_along(x, move):
    return [x] + [move(x, k) for k in (1, 2, 3)]


def local(
    queries, keys, values, segments, cotangent, weight,
    first_moment, first_scale, second_moment, second_scale,
):
    me = jnp.stack([lax.axis_index(a) for a in DP_SEQ]).astype(jnp.int32)
    across = lambda v, k: shift(v, "dp_0", k)

    packed = pack(queries[0], keys[0], values[0], segments)
    arrived = lax.all_to_all(packed, SEQ, 0, 0, tiled=True)

    cots = from_along(cotangent[0], across)
    cots = cots + [shift(v, "dp_2", 1) for v in cots]

    rows = weight.astype(BF16)
    rows = jnp.concatenate(from_along(rows, shift_y), axis=0)
    rows = jnp.concatenate(from_along(rows, lambda v, k: shift(v, "seq_0", k)), axis=0)
    rows = from_along(rows, across)
    rows = rows + [shift(v, "dp_2", 1) for v in rows]

    attended = attend(arrived)
    columns = lax.all_to_all(
        attended, ("dp_0", "dp_2", "seq_0", "seq_1"), 0, 0, tiled=True
    ).reshape(8, 256, TILE)
    partial = gradient_rows(me, columns, cots)
    parts = lax.all_to_all(partial, ("dp_1", "seq_0", "seq_1"), 0, 0, tiled=True)
    grad, squares = total_rows(parts)
    swap = [
        ((x * 4 + z) , (z * 4 + x)) for x in range(4) for z in range(4)
    ]
    grad = lax.ppermute(grad, ("dp_0", "seq_0"), swap)
    squares = lax.all_to_all(squares, DP_SEQ, 0, 0, tiled=True)
    new_weight, new_first, new_fscale, new_second, new_sscale = adam(
        grad, squares, weight, first_moment, first_scale, second_moment, second_scale
    )
    own = lax.all_to_all(columns, ("dp_0", "dp_2"), 0, 0, tiled=True).reshape(8, 16, 16, TILE)
    layer_out = project(me, own, rows)
    return (layer_out, new_weight, new_first, new_fscale, new_second, new_sscale)


def solution(mesh):
    finer = Mesh(mesh.devices.reshape(4, 2, 2, 4, 2), DP_SEQ)
    tokens = P(DP, SEQ, None)
    rows = P(DP_SEQ, None)
    return jax.shard_map(
        local,
        mesh=finer,
        in_specs=(tokens, tokens, tokens, P(DP, SEQ), tokens, rows, rows, rows, rows, rows),
        out_specs=(tokens, rows, rows, rows, rows, rows),
        check_vma=False,
    )
```

time: 414 us -> 198 us (0.48)
  waiting for transfers between devices: 257 us -> 75.5 us
  blocking collectives: 84.8 us -> 0 us
  starting transfers between devices: 0.12 us -> 75.2 us
  matrix products: 46.5 us -> 0 us
  Pallas kernels: 0 us -> 36.1 us
  between operations: 14.7 us -> 0.85 us
  other arithmetic: 6.43 us -> 0.75 us
  local copies, waits for them, and re-layouts: 4.02 us -> 8.76 us
    all_gather x2 -> x0, waiting for transfers between devices: 152 us -> none  [the longest x1 95.7 us: side_by_side(): result = lax.all_gather(both, axis, axis=dim, tiled=True)]
    reduce_scatter x1 -> x0, waiting for transfers between devices: 105 us -> none  [local(): lax.psum_scatter(lax.dot_general(columns, cot_rows, (((0,), (0,)), ((), (...]
    ppermute x0 -> x21, waiting for transfers between devices: none -> 63.4 us  [the longest x17 43.2 us: shift(): return lax.ppermute(x, axis, [(i, (i + by) % peers) for i in range(peers)])]
    dot_general x4 -> x0, matrix products: 46.5 us -> none  [the longest x1 17.4 us: local(): jnp.einsum('qgrk,kgd->qgrd', weights.astype(jnp.bfloat16), value_hat, pre...]
    ppermute x0 -> x21, starting transfers between devices: none -> 40.8 us  [the longest x17 34.1 us: shift(): return lax.ppermute(x, axis, [(i, (i + by) % peers) for i in range(peers)])]
    pallas_call x0 -> x6, Pallas kernels: none -> 36.1 us  [the longest x1 10.8 us: attend(): pl.pallas_call(attend_kernel, out_shape=jax.ShapeDtypeStruct((64, 32, TIL...]
    all_to_all x0 -> x5, starting transfers between devices: none -> 34.4 us  [the longest x1 8.63 us: local(): arrived = lax.all_to_all(packed, SEQ, 0, 0, tiled=True)]
    psum x5 -> x0, blocking collectives: 32.4 us -> none  [by_axis(): x = lax.psum(x, axis)]
  transfers between devices with their start and end apart: 3 -> 26, of which waited for: 3 -> 7; matrix products, arithmetic and copies ran while one was open for 0% -> 1% of each run, Pallas kernels for 0% -> 16%
where the time goes in v1:
time: 198 us; the launch traced here: 197 us
  waiting for transfers between devices  75.5 us (38%)
  starting transfers between devices  75.2 us (38%)
  Pallas kernels  36.1 us (18%)
  local copies, waits for them, and re-layouts  8.76 us (4%)
    ppermute x17, waiting for transfers between devices, shift(): return lax.ppermute(x, axis, [(i, (i + by) % peers) for i in range(peers)])  43.2 us
    ppermute x17, starting transfers between devices, shift(): return lax.ppermute(x, axis, [(i, (i + by) % peers) for i in range(peers)])  34.1 us
    ppermute x3, waiting for transfers between devices, shift_y(): return lax.ppermute(x, ('dp_1', 'seq_1'), pairs)  20.2 us
    all_to_all x1, waiting for transfers between devices, local(): lax.all_to_all(columns, ('dp_0', 'dp_2'), 0, 0, tiled=True)  12.1 us
    pallas_call x1, Pallas kernels, attend(): pl.pallas_call(attend_kernel, out_shape=jax.ShapeDtypeStruct((64, 32, TIL...  10.8 us
    pallas_call x1, Pallas kernels, gradient_rows(): pl.pallas_call(gradient_kernel, grid_spec=pltpu.PrefetchScalarGridSpec(nu...  10.5 us
    pallas_call x1, Pallas kernels, project(): pl.pallas_call(project_kernel, grid_spec=pltpu.PrefetchScalarGridSpec(num...  10.1 us
    unnamed x33, local copies, waits for them, and re-layouts  8.66 us
  transfers between devices with their start and end apart: 26, of which 7 were waited for; matrix products, arithmetic and copies ran while one was open for 1% of the time, Pallas kernels for 16%

profile of v1, /device:TPU:1, one launch (start us, length us, event | category | flops | bytes accessed | tf_op | source)
XLA Modules:
  0.0 197.2 jit_solution(1710837513405734626)
XLA Ops:
  0.6 1.2 copy-done.1
  1.9 1.0 copy-done.3
  2.9 1.0 copy-done.4
  3.9 0.7 copy-done.12
  4.6 1.9 pack.1
  6.5 1.4 copy-done
  7.9 8.6 %all-to-all-start = ((bf16[8,272,512]{2,1,0:T(8,128)(2,1)}), bf16[8,272,512]{2,1,0:T(8,128)(2,1)S(1)}, u32[]{:S(2)}, u32[]{:S(2)}) async-start(bf16[8,272,512]{2,1,0:T(8,128)(2,1)} %copy-done), calls=%async_computation | async-start | bytes 4456448 | tf_op jit(solution)/shard_map/all_to_all | solution.py:314
  16.5 1.2 collective-permute-start.13
  17.8 0.5 collective-permute-start
  18.2 3.6 %collective-permute-start.1 = (bf16[16,2304]{1,0:T(8,128)(2,1)S(1)}, bf16[16,2304]{1,0:T(8,128)(2,1)S(1)}, u32[]{:S(2)}, u32[]{:S(2)}) collective-permute-start(bf16[16,2304]{1,0:T(8,128)(2,1)S(1)} %get-tuple-element.21), channel_id=1, source_target_pairs={{0,1},{16,17},{1,0},{17,16},{2,3},{18,19},{3,2},{19,18},{4,5},{20,... | collective-permute-start | bytes 221192 | tf_op jit(solution)/shard_map/ppermute | solution.py:299
  21.8 1.1 collective-permute-start.2
  22.9 2.5 %collective-permute-start.14 = (bf16[256,2304]{1,0:T(8,128)(2,1)}, bf16[256,2304]{1,0:T(8,128)(2,1)}, u32[]{:S(2)}, u32[]{:S(2)}) collective-permute-start(bf16[256,2304]{1,0:T(8,128)(2,1)} %bitcast.10.refs_0_), channel_id=1, source_target_pairs={{0,64},{32,96},{64,0},{96,32},{1,65},{33,97},{65,1},{97,33},{2,66}... | collective-permute-start | bytes 3538952 | tf_op jit(solution)/shard_map/ppermute | solution.py:291
  25.3 20.2 %collective-permute-done = bf16[16,2304]{1,0:T(8,128)(2,1)S(1)} collective-permute-done((bf16[16,2304]{1,0:T(8,128)(2,1)S(1)}, bf16[16,2304]{1,0:T(8,128)(2,1)S(1)}, u32[]{:S(2)}, u32[]{:S(2)}) %collective-permute-start) | collective-permute-done | bytes 73760 | tf_op jit(solution)/shard_map/ppermute | solution.py:299
  45.5 2.1 %collective-permute-start.15 = (bf16[256,2304]{1,0:T(8,128)(2,1)}, bf16[256,2304]{1,0:T(8,128)(2,1)}, u32[]{:S(2)}, u32[]{:S(2)}) collective-permute-start(bf16[256,2304]{1,0:T(8,128)(2,1)} %bitcast.10.refs_0_), channel_id=1, source_target_pairs={{0,96},{32,0},{64,32},{96,64},{1,97},{33,1},{65,33},{97,65},{2,98}... | collective-permute-start | bytes 3538952 | tf_op jit(solution)/shard_map/ppermute | solution.py:291
  47.6 1.7 collective-permute-start.16
  49.3 0.0 collective-permute-done.2
  49.3 0.7 pad_maximum_fusion
  50.0 2.2 %collective-permute-start.3 = (bf16[64,2304]{1,0:T(8,128)(2,1)}, bf16[64,2304]{1,0:T(8,128)(2,1)}, u32[]{:S(2)}, u32[]{:S(2)}) collective-permute-start(bf16[64,2304]{1,0:T(8,128)(2,1)} %pad_maximum_fusion), channel_id=1, source_target_pairs={{0,2},{2,4},{4,6},{6,0},{1,3},{3,5},{5,7},{7,1},{8,10},{10,12},{12... | collective-permute-start | bytes 884744 | tf_op jit(solution)/shard_map/ppermute | solution.py:291
  52.3 0.4 collective-permute-start.17
  52.7 0.0 all-to-all-done.in_ref
  52.7 10.8 %attend.1 = bf16[64,32,256]{2,1,0:T(8,128)(2,1)} custom-call(bf16[8,272,512]{2,1,0:T(8,128)(2,1)S(1)} %all-to-all-done.in_ref), custom_call_target="tpu_custom_call" | custom-call | tf_op jit(solution)/shard_map/attend/pallas_call | solution.py:133
  63.5 8.4 %all-to-all-start.1 = ((bf16[64,32,256]{2,1,0:T(8,128)(2,1)}), bf16[64,32,256]{2,1,0:T(8,128)(2,1)}, u32[]{:S(2)}, u32[]{:S(2)}) async-start(bf16[64,32,256]{2,1,0:T(8,128)(2,1)} %attend.1), calls=%async_computation.1 | async-start | bytes 2097152 | tf_op jit(solution)/shard_map/all_to_all | solution.py:326
  71.9 3.0 %collective-permute-start.4 = (bf16[64,2304]{1,0:T(8,128)(2,1)}, bf16[64,2304]{1,0:T(8,128)(2,1)S(1)}, u32[]{:S(2)}, u32[]{:S(2)}) collective-permute-start(bf16[64,2304]{1,0:T(8,128)(2,1)} %pad_maximum_fusion), channel_id=1, source_target_pairs={{0,4},{2,6},{4,0},{6,2},{1,5},{3,7},{5,1},{7,3},{8,12},{10,14},{12... | collective-permute-start | bytes 884744 | tf_op jit(solution)/shard_map/ppermute | solution.py:291
  74.9 0.0 collective-permute-done.14.refs_2_
  74.9 0.6 collective-permute-start.18
  75.5 0.6 collective-permute-done.15.refs_3_
  76.1 3.9 %collective-permute-start.19 = (bf16[256,2304]{1,0:T(8,128)(2,1)}, bf16[256,2304]{1,0:T(8,128)(2,1)}, u32[]{:S(2)}, u32[]{:S(2)}) collective-permute-start(bf16[256,2304]{1,0:T(8,128)(2,1)} %collective-permute-done.15.refs_3_), channel_id=1, source_target_pairs={{0,8},{8,0},{1,9},{9,1},{2,10},{10,2},{3,11},{11,3},{4,12},{12,4},... | collective-permute-start | bytes 3538952 | tf_op jit(solution)/shard_map/ppermute | solution.py:291
  80.1 1.0 constant_dynamic-update-slice_fusion.2
  81.1 11.8 %collective-permute-done.4 = bf16[64,2304]{1,0:T(8,128)(2,1)S(1)} collective-permute-done((bf16[64,2304]{1,0:T(8,128)(2,1)}, bf16[64,2304]{1,0:T(8,128)(2,1)S(1)}, u32[]{:S(2)}, u32[]{:S(2)}) %collective-permute-start.4) | collective-permute-done | bytes 294944 | tf_op jit(solution)/shard_map/ppermute | solution.py:291
  92.9 2.2 %collective-permute-start.5 = (bf16[64,2304]{1,0:T(8,128)(2,1)}, bf16[64,2304]{1,0:T(8,128)(2,1)S(1)}, u32[]{:S(2)}, u32[]{:S(2)}) collective-permute-start(bf16[64,2304]{1,0:T(8,128)(2,1)} %pad_maximum_fusion), channel_id=1, source_target_pairs={{0,6},{2,0},{4,2},{6,4},{1,7},{3,1},{5,3},{7,5},{8,14},{10,8},{12,... | collective-permute-start | bytes 884744 | tf_op jit(solution)/shard_map/ppermute | solution.py:291
  95.1 6.2 %collective-permute-done.5 = bf16[64,2304]{1,0:T(8,128)(2,1)S(1)} collective-permute-done((bf16[64,2304]{1,0:T(8,128)(2,1)}, bf16[64,2304]{1,0:T(8,128)(2,1)S(1)}, u32[]{:S(2)}, u32[]{:S(2)}) %collective-permute-start.5) | collective-permute-done | bytes 294944 | tf_op jit(solution)/shard_map/ppermute | solution.py:291
  101.3 0.8 collective-permute-start.6
  102.1 0.0 collective-permute-done.16.refs_4_
  102.1 2.8 %collective-permute-start.7 = (bf16[256,2304]{1,0:T(8,128)(2,1)S(1)}, bf16[256,2304]{1,0:T(8,128)(2,1)}, u32[]{:S(2)}, u32[]{:S(2)}) collective-permute-start(bf16[256,2304]{1,0:T(8,128)(2,1)S(1)} %constant_dynamic-update-slice_fusion.refs_0_), channel_id=1, source_target_pairs={{0,64},{32,96},{64,0},{96,32},{1,65},{33,97},{65,1},{97,33},{2,66}... | collective-permute-start | bytes 3538952 | tf_op jit(solution)/shard_map/ppermute | solution.py:291
  104.9 0.0 collective-permute-done.17.refs_5_
  104.9 1.7 collective-permute-start.8
  106.6 0.1 stack.23.me_ref
  106.7 0.0 collective-permute-done.19.refs_7_
  106.7 0.0 all-to-all-done.1
  106.7 1.0 copy-done.13
  107.7 10.5 %gradient_rows.1 = bf16[16,16,2304]{2,1,0:T(8,128)(2,1)} custom-call(s32[5]{0:T(128)S(1)} %stack.23.me_ref, bf16[8,256,256]{2,1,0:T(8,128)(2,1)} %bitcast.8.att_ref, bf16[256,2304]{1,0:T(8,128)(2,1)} %bitcast.10.refs_0_, bf16[256,2304]{1,0:T(8,128)(2,1)} %collective-permute-done.13.refs_1_, bf16[256,2304]{1,0:T(8,128)(2,1)} %collective-permute-done.14.refs_2_, ...), custom_call_target="tpu_custom_call" | custom-call | tf_op jit(solution)/shard_map/gradient_rows/pallas_call | solution.py:163
  118.2 5.4 %all-to-all-start.3 = ((bf16[16,16,2304]{2,1,0:T(8,128)(2,1)}), bf16[16,16,2304]{2,1,0:T(8,128)(2,1)S(1)}, u32[]{:S(2)}, u32[]{:S(2)}) async-start(bf16[16,16,2304]{2,1,0:T(8,128)(2,1)} %gradient_rows.1), calls=%async_computation.3 | async-start | bytes 2359296 | tf_op jit(solution)/shard_map/all_to_all | solution.py:330
  123.7 2.7 %collective-permute-start.9 = (bf16[256,2304]{1,0:T(8,128)(2,1)S(1)}, bf16[256,2304]{1,0:T(8,128)(2,1)}, u32[]{:S(2)}, u32[]{:S(2)}) collective-permute-start(bf16[256,2304]{1,0:T(8,128)(2,1)S(1)} %constant_dynamic-update-slice_fusion.refs_0_), channel_id=1, source_target_pairs={{0,8},{8,0},{1,9},{9,1},{2,10},{10,2},{3,11},{11,3},{4,12},{12,4},... | collective-permute-start | bytes 3538952 | tf_op jit(solution)/shard_map/ppermute | solution.py:291
  126.4 2.5 %collective-permute-done.6.refs_1_ = bf16[256,2304]{1,0:T(8,128)(2,1)} collective-permute-done((bf16[256,2304]{1,0:T(8,128)(2,1)S(1)}, bf16[256,2304]{1,0:T(8,128)(2,1)}, u32[]{:S(2)}, u32[]{:S(2)}) %collective-permute-start.6) | collective-permute-done | bytes 1179680 | tf_op jit(solution)/shard_map/ppermute | solution.py:291
  128.8 3.7 %collective-permute-start.10 = (bf16[256,2304]{1,0:T(8,128)(2,1)}, bf16[256,2304]{1,0:T(8,128)(2,1)}, u32[]{:S(2)}, u32[]{:S(2)}) collective-permute-start(bf16[256,2304]{1,0:T(8,128)(2,1)} %collective-permute-done.6.refs_1_), channel_id=1, source_target_pairs={{0,8},{8,0},{1,9},{9,1},{2,10},{10,2},{3,11},{11,3},{4,12},{12,4},... | collective-permute-start | bytes 3538952 | tf_op jit(solution)/shard_map/ppermute | solution.py:291
  132.5 22.0 %collective-permute-done.7.refs_2_ = bf16[256,2304]{1,0:T(8,128)(2,1)} collective-permute-done((bf16[256,2304]{1,0:T(8,128)(2,1)S(1)}, bf16[256,2304]{1,0:T(8,128)(2,1)}, u32[]{:S(2)}, u32[]{:S(2)}) %collective-permute-start.7) | collective-permute-done | bytes 1179680 | tf_op jit(solution)/shard_map/ppermute | solution.py:291
  154.5 2.7 %collective-permute-start.11 = (bf16[256,2304]{1,0:T(8,128)(2,1)}, bf16[256,2304]{1,0:T(8,128)(2,1)}, u32[]{:S(2)}, u32[]{:S(2)}) collective-permute-start(bf16[256,2304]{1,0:T(8,128)(2,1)} %collective-permute-done.7.refs_2_), channel_id=1, source_target_pairs={{0,8},{8,0},{1,9},{9,1},{2,10},{10,2},{3,11},{11,3},{4,12},{12,4},... | collective-permute-start | bytes 3538952 | tf_op jit(solution)/shard_map/ppermute | solution.py:291
  157.2 0.0 collective-permute-done.8.refs_3_
  157.2 0.0 collective-permute-start.12
  157.2 0.0 all-to-all-done.3.parts_ref
  157.2 4.6 %all-to-all-start.2 = ((bf16[8,256,256]{2,1,0:T(8,128)(2,1)}), bf16[8,256,256]{2,1,0:T(8,128)(2,1)S(1)}, u32[]{:S(2)}, u32[]{:S(2)}) async-start(bf16[8,256,256]{2,1,0:T(8,128)(2,1)} %bitcast.8.att_ref), calls=%async_computation.2 | async-start | bytes 2097152 | tf_op jit(solution)/shard_map/all_to_all | solution.py:340
  161.8 0.8 total_rows.1
  162.7 0.6 copy-done.7
  163.3 1.6 collective-permute-start.20
  164.9 12.1 %all-to-all-done.2 = bf16[8,256,256]{2,1,0:T(8,128)(2,1)S(1)} async-done(((bf16[8,256,256]{2,1,0:T(8,128)(2,1)}), bf16[8,256,256]{2,1,0:T(8,128)(2,1)S(1)}, u32[]{:S(2)}, u32[]{:S(2)}) %all-to-all-start.2) | async-done | bytes 1048608 | tf_op jit(solution)/shard_map/all_to_all | solution.py:340
  177.0 7.3 %all-to-all-start.4 = ((f32[128,1,128]{2,1,0:T(1,128)}), f32[128,1,128]{2,1,0:T(1,128)S(1)}, u32[]{:S(2)}, u32[]{:S(2)}) async-start(f32[128,1,128]{2,1,0:T(1,128)} %copy-done.7), calls=%async_computation.4 | async-start | bytes 131072 | tf_op jit(solution)/shard_map/all_to_all | solution.py:336
  184.3 0.0 collective-permute-done.10.refs_5_
  184.3 0.0 collective-permute-done.11.refs_6_
  184.4 0.0 copy-start.11
  184.4 0.6 copy-done.11
  185.0 10.1 %project.1 = bf16[1,256,2304]{2,1,0:T(8,128)(2,1)} custom-call(s32[5]{0:T(128)S(1)} %copy-done.11, bf16[8,16,16,256]{3,2,1,0:T(8,128)(2,1)S(1)} %bitcast.11, bf16[256,2304]{1,0:T(8,128)(2,1)S(1)} %constant_dynamic-update-slice_fusion.refs_0_, bf16[256,2304]{1,0:T(8,128)(2,1)} %collective-permute-done.6.refs_1_, ...), custom_call_target="tpu_custom_call" | custom-call | tf_op jit(solution)/shard_map/project/pallas_call | solution.py:205
  195.2 0.0 all-to-all-done.4.squares_ref
  195.2 0.0 collective-permute-done.20.grad_ref
  195.2 2.0 adam.1
  (31 shorter events, 0.1 us)
Async XLA Ops:
  0.6 1.2 copy-start.1
  1.9 1.0 copy-start.3
  2.9 1.0 copy-start.4
  3.9 0.7 copy-start.12
  6.5 1.4 copy-start
  7.9 9.8 %copy-start.2 = (f32[16,2304]{1,0:T(8,128)S(1)}, f32[16,2304]{1,0:T(8,128)}, u32[]{:S(2)}) copy-start(f32[16,2304]{1,0:T(8,128)} %weight_ref.1) | copy-start | bytes 442372
  7.9 44.8 %all-to-all-start = ((bf16[8,272,512]{2,1,0:T(8,128)(2,1)}), bf16[8,272,512]{2,1,0:T(8,128)(2,1)S(1)}, u32[]{:S(2)}, u32[]{:S(2)}) async-start(bf16[8,272,512]{2,1,0:T(8,128)(2,1)} %copy-done), calls=%async_computation | async-start | bytes 4456448 | tf_op jit(solution)/shard_map/all_to_all | solution.py:314
  16.5 35.8 %collective-permute-start.13 = (bf16[256,2304]{1,0:T(8,128)(2,1)}, bf16[256,2304]{1,0:T(8,128)(2,1)}, u32[]{:S(2)}, u32[]{:S(2)}) collective-permute-start(bf16[256,2304]{1,0:T(8,128)(2,1)} %bitcast.10.refs_0_), channel_id=1, source_target_pairs={{0,32},{32,64},{64,96},{96,0},{1,33},{33,65},{65,97},{97,1},{2,34}... | collective-permute-start | bytes 3538952 | tf_op jit(solution)/shard_map/ppermute | solution.py:291
  17.8 27.7 %collective-permute-start = (bf16[16,2304]{1,0:T(8,128)(2,1)S(1)}, bf16[16,2304]{1,0:T(8,128)(2,1)S(1)}, u32[]{:S(2)}, u32[]{:S(2)}) collective-permute-start(bf16[16,2304]{1,0:T(8,128)(2,1)S(1)} %get-tuple-element.21), channel_id=1, source_target_pairs={{0,16},{16,1},{1,17},{17,0},{2,18},{18,3},{3,19},{19,2},{4,20},{20... | collective-permute-start | bytes 221192 | tf_op jit(solution)/shard_map/ppermute | solution.py:299
  18.2 29.4 %collective-permute-start.1 = (bf16[16,2304]{1,0:T(8,128)(2,1)S(1)}, bf16[16,2304]{1,0:T(8,128)(2,1)S(1)}, u32[]{:S(2)}, u32[]{:S(2)}) collective-permute-start(bf16[16,2304]{1,0:T(8,128)(2,1)S(1)} %get-tuple-element.21), channel_id=1, source_target_pairs={{0,1},{16,17},{1,0},{17,16},{2,3},{18,19},{3,2},{19,18},{4,5},{20,... | collective-permute-start | bytes 221192 | tf_op jit(solution)/shard_map/ppermute | solution.py:299
  21.8 27.5 %collective-permute-start.2 = (bf16[16,2304]{1,0:T(8,128)(2,1)S(1)}, bf16[16,2304]{1,0:T(8,128)(2,1)S(1)}, u32[]{:S(2)}, u32[]{:S(2)}) collective-permute-start(bf16[16,2304]{1,0:T(8,128)(2,1)S(1)} %get-tuple-element.21), channel_id=1, source_target_pairs={{0,17},{16,0},{1,16},{17,1},{2,19},{18,2},{3,18},{19,3},{4,21},{20... | collective-permute-start | bytes 221192 | tf_op jit(solution)/shard_map/ppermute | solution.py:299
  22.9 52.0 %collective-permute-start.14 = (bf16[256,2304]{1,0:T(8,128)(2,1)}, bf16[256,2304]{1,0:T(8,128)(2,1)}, u32[]{:S(2)}, u32[]{:S(2)}) collective-permute-start(bf16[256,2304]{1,0:T(8,128)(2,1)} %bitcast.10.refs_0_), channel_id=1, source_target_pairs={{0,64},{32,96},{64,0},{96,32},{1,65},{33,97},{65,1},{97,33},{2,66}... | collective-permute-start | bytes 3538952 | tf_op jit(solution)/shard_map/ppermute | solution.py:291
  45.5 30.7 %collective-permute-start.15 = (bf16[256,2304]{1,0:T(8,128)(2,1)}, bf16[256,2304]{1,0:T(8,128)(2,1)}, u32[]{:S(2)}, u32[]{:S(2)}) collective-permute-start(bf16[256,2304]{1,0:T(8,128)(2,1)} %bitcast.10.refs_0_), channel_id=1, source_target_pairs={{0,96},{32,0},{64,32},{96,64},{1,97},{33,1},{65,33},{97,65},{2,98}... | collective-permute-start | bytes 3538952 | tf_op jit(solution)/shard_map/ppermute | solution.py:291
  47.6 54.6 %collective-permute-start.16 = (bf16[256,2304]{1,0:T(8,128)(2,1)}, bf16[256,2304]{1,0:T(8,128)(2,1)}, u32[]{:S(2)}, u32[]{:S(2)}) collective-permute-start(bf16[256,2304]{1,0:T(8,128)(2,1)} %bitcast.10.refs_0_), channel_id=1, source_target_pairs={{0,8},{8,0},{1,9},{9,1},{2,10},{10,2},{3,11},{11,3},{4,12},{12,4},... | collective-permute-start | bytes 3538952 | tf_op jit(solution)/shard_map/ppermute | solution.py:291
  50.0 21.8 %collective-permute-start.3 = (bf16[64,2304]{1,0:T(8,128)(2,1)}, bf16[64,2304]{1,0:T(8,128)(2,1)}, u32[]{:S(2)}, u32[]{:S(2)}) collective-permute-start(bf16[64,2304]{1,0:T(8,128)(2,1)} %pad_maximum_fusion), channel_id=1, source_target_pairs={{0,2},{2,4},{4,6},{6,0},{1,3},{3,5},{5,7},{7,1},{8,10},{10,12},{12... | collective-permute-start | bytes 884744 | tf_op jit(solution)/shard_map/ppermute | solution.py:291
  52.3 52.6 %collective-permute-start.17 = (bf16[256,2304]{1,0:T(8,128)(2,1)}, bf16[256,2304]{1,0:T(8,128)(2,1)}, u32[]{:S(2)}, u32[]{:S(2)}) collective-permute-start(bf16[256,2304]{1,0:T(8,128)(2,1)} %collective-permute-done.13.refs_1_), channel_id=1, source_target_pairs={{0,8},{8,0},{1,9},{9,1},{2,10},{10,2},{3,11},{11,3},{4,12},{12,4},... | collective-permute-start | bytes 3538952 | tf_op jit(solution)/shard_map/ppermute | solution.py:291
  63.5 43.3 %all-to-all-start.1 = ((bf16[64,32,256]{2,1,0:T(8,128)(2,1)}), bf16[64,32,256]{2,1,0:T(8,128)(2,1)}, u32[]{:S(2)}, u32[]{:S(2)}) async-start(bf16[64,32,256]{2,1,0:T(8,128)(2,1)} %attend.1), calls=%async_computation.1 | async-start | bytes 2097152 | tf_op jit(solution)/shard_map/all_to_all | solution.py:326
  71.9 21.0 %collective-permute-start.4 = (bf16[64,2304]{1,0:T(8,128)(2,1)}, bf16[64,2304]{1,0:T(8,128)(2,1)S(1)}, u32[]{:S(2)}, u32[]{:S(2)}) collective-permute-start(bf16[64,2304]{1,0:T(8,128)(2,1)} %pad_maximum_fusion), channel_id=1, source_target_pairs={{0,4},{2,6},{4,0},{6,2},{1,5},{3,7},{5,1},{7,3},{8,12},{10,14},{12... | collective-permute-start | bytes 884744 | tf_op jit(solution)/shard_map/ppermute | solution.py:291
  74.9 31.9 %collective-permute-start.18 = (bf16[256,2304]{1,0:T(8,128)(2,1)}, bf16[256,2304]{1,0:T(8,128)(2,1)S(1)}, u32[]{:S(2)}, u32[]{:S(2)}) collective-permute-start(bf16[256,2304]{1,0:T(8,128)(2,1)} %collective-permute-done.14.refs_2_), channel_id=1, source_target_pairs={{0,8},{8,0},{1,9},{9,1},{2,10},{10,2},{3,11},{11,3},{4,12},{12,4},... | collective-permute-start | bytes 3538952 | tf_op jit(solution)/shard_map/ppermute | solution.py:291
  76.1 30.6 %collective-permute-start.19 = (bf16[256,2304]{1,0:T(8,128)(2,1)}, bf16[256,2304]{1,0:T(8,128)(2,1)}, u32[]{:S(2)}, u32[]{:S(2)}) collective-permute-start(bf16[256,2304]{1,0:T(8,128)(2,1)} %collective-permute-done.15.refs_3_), channel_id=1, source_target_pairs={{0,8},{8,0},{1,9},{9,1},{2,10},{10,2},{3,11},{11,3},{4,12},{12,4},... | collective-permute-start | bytes 3538952 | tf_op jit(solution)/shard_map/ppermute | solution.py:291
  92.9 8.4 %collective-permute-start.5 = (bf16[64,2304]{1,0:T(8,128)(2,1)}, bf16[64,2304]{1,0:T(8,128)(2,1)S(1)}, u32[]{:S(2)}, u32[]{:S(2)}) collective-permute-start(bf16[64,2304]{1,0:T(8,128)(2,1)} %pad_maximum_fusion), channel_id=1, source_target_pairs={{0,6},{2,0},{4,2},{6,4},{1,7},{3,1},{5,3},{7,5},{8,14},{10,8},{12,... | collective-permute-start | bytes 884744 | tf_op jit(solution)/shard_map/ppermute | solution.py:291
  101.3 27.5 %collective-permute-start.6 = (bf16[256,2304]{1,0:T(8,128)(2,1)S(1)}, bf16[256,2304]{1,0:T(8,128)(2,1)}, u32[]{:S(2)}, u32[]{:S(2)}) collective-permute-start(bf16[256,2304]{1,0:T(8,128)(2,1)S(1)} %constant_dynamic-update-slice_fusion.refs_0_), channel_id=1, source_target_pairs={{0,32},{32,64},{64,96},{96,0},{1,33},{33,65},{65,97},{97,1},{2,34}... | collective-permute-start | bytes 3538952 | tf_op jit(solution)/shard_map/ppermute | solution.py:291
  102.1 52.4 %collective-permute-start.7 = (bf16[256,2304]{1,0:T(8,128)(2,1)S(1)}, bf16[256,2304]{1,0:T(8,128)(2,1)}, u32[]{:S(2)}, u32[]{:S(2)}) collective-permute-start(bf16[256,2304]{1,0:T(8,128)(2,1)S(1)} %constant_dynamic-update-slice_fusion.refs_0_), channel_id=1, source_target_pairs={{0,64},{32,96},{64,0},{96,32},{1,65},{33,97},{65,1},{97,33},{2,66}... | collective-permute-start | bytes 3538952 | tf_op jit(solution)/shard_map/ppermute | solution.py:291
  104.9 52.3 %collective-permute-start.8 = (bf16[256,2304]{1,0:T(8,128)(2,1)S(1)}, bf16[256,2304]{1,0:T(8,128)(2,1)}, u32[]{:S(2)}, u32[]{:S(2)}) collective-permute-start(bf16[256,2304]{1,0:T(8,128)(2,1)S(1)} %constant_dynamic-update-slice_fusion.refs_0_), channel_id=1, source_target_pairs={{0,96},{32,0},{64,32},{96,64},{1,97},{33,1},{65,33},{97,65},{2,98}... | collective-permute-start | bytes 3538952 | tf_op jit(solution)/shard_map/ppermute | solution.py:291
  106.7 11.5 %copy-start.10 = (s32[5]{0:T(128)}, s32[5]{0:T(128)S(1)}, u32[]{:S(2)}) copy-start(s32[5]{0:T(128)S(1)} %stack.23.me_ref) | copy-start | bytes 64
  106.7 1.0 copy-start.13
  118.2 39.0 %all-to-all-start.3 = ((bf16[16,16,2304]{2,1,0:T(8,128)(2,1)}), bf16[16,16,2304]{2,1,0:T(8,128)(2,1)S(1)}, u32[]{:S(2)}, u32[]{:S(2)}) async-start(bf16[16,16,2304]{2,1,0:T(8,128)(2,1)} %gradient_rows.1), calls=%async_computation.3 | async-start | bytes 2359296 | tf_op jit(solution)/shard_map/all_to_all | solution.py:330
  123.7 60.6 %collective-permute-start.9 = (bf16[256,2304]{1,0:T(8,128)(2,1)S(1)}, bf16[256,2304]{1,0:T(8,128)(2,1)}, u32[]{:S(2)}, u32[]{:S(2)}) collective-permute-start(bf16[256,2304]{1,0:T(8,128)(2,1)S(1)} %constant_dynamic-update-slice_fusion.refs_0_), channel_id=1, source_target_pairs={{0,8},{8,0},{1,9},{9,1},{2,10},{10,2},{3,11},{11,3},{4,12},{12,4},... | collective-permute-start | bytes 3538952 | tf_op jit(solution)/shard_map/ppermute | solution.py:291
  128.8 55.5 %collective-permute-start.10 = (bf16[256,2304]{1,0:T(8,128)(2,1)}, bf16[256,2304]{1,0:T(8,128)(2,1)}, u32[]{:S(2)}, u32[]{:S(2)}) collective-permute-start(bf16[256,2304]{1,0:T(8,128)(2,1)} %collective-permute-done.6.refs_1_), channel_id=1, source_target_pairs={{0,8},{8,0},{1,9},{9,1},{2,10},{10,2},{3,11},{11,3},{4,12},{12,4},... | collective-permute-start | bytes 3538952 | tf_op jit(solution)/shard_map/ppermute | solution.py:291
  154.5 29.8 %collective-permute-start.11 = (bf16[256,2304]{1,0:T(8,128)(2,1)}, bf16[256,2304]{1,0:T(8,128)(2,1)}, u32[]{:S(2)}, u32[]{:S(2)}) collective-permute-start(bf16[256,2304]{1,0:T(8,128)(2,1)} %collective-permute-done.7.refs_2_), channel_id=1, source_target_pairs={{0,8},{8,0},{1,9},{9,1},{2,10},{10,2},{3,11},{11,3},{4,12},{12,4},... | collective-permute-start | bytes 3538952 | tf_op jit(solution)/shard_map/ppermute | solution.py:291
  157.2 27.1 %collective-permute-start.12 = (bf16[256,2304]{1,0:T(8,128)(2,1)}, bf16[256,2304]{1,0:T(8,128)(2,1)}, u32[]{:S(2)}, u32[]{:S(2)}) collective-permute-start(bf16[256,2304]{1,0:T(8,128)(2,1)} %collective-permute-done.8.refs_3_), channel_id=1, source_target_pairs={{0,8},{8,0},{1,9},{9,1},{2,10},{10,2},{3,11},{11,3},{4,12},{12,4},... | collective-permute-start | bytes 3538952 | tf_op jit(solution)/shard_map/ppermute | solution.py:291
  157.2 19.7 %all-to-all-start.2 = ((bf16[8,256,256]{2,1,0:T(8,128)(2,1)}), bf16[8,256,256]{2,1,0:T(8,128)(2,1)S(1)}, u32[]{:S(2)}, u32[]{:S(2)}) async-start(bf16[8,256,256]{2,1,0:T(8,128)(2,1)} %bitcast.8.att_ref), calls=%async_computation.2 | async-start | bytes 2097152 | tf_op jit(solution)/shard_map/all_to_all | solution.py:340
  162.7 0.6 copy-start.7
  163.3 31.9 %collective-permute-start.20 = (f32[16,2304]{1,0:T(8,128)}, f32[16,2304]{1,0:T(8,128)S(1)}, u32[]{:S(2)}, u32[]{:S(2)}) collective-permute-start(f32[16,2304]{1,0:T(8,128)} %get-tuple-element.13), channel_id=1, source_target_pairs={{0,0},{2,32},{4,64},{6,96},{32,2},{34,34},{36,66},{38,98},{64,4},{... | collective-permute-start | bytes 442376 | tf_op jit(solution)/shard_map/ppermute | solution.py:335
  177.0 18.2 %all-to-all-start.4 = ((f32[128,1,128]{2,1,0:T(1,128)}), f32[128,1,128]{2,1,0:T(1,128)S(1)}, u32[]{:S(2)}, u32[]{:S(2)}) async-start(f32[128,1,128]{2,1,0:T(1,128)} %copy-done.7), calls=%async_computation.4 | async-start | bytes 131072 | tf_op jit(solution)/shard_map/all_to_all | solution.py:336
  184.4 0.7 copy-start.11
  185.0 10.2 %copy-start.5 = (bf16[16,2304]{1,0:T(8,128)(2,1)S(1)}, bf16[16,2304]{1,0:T(8,128)(2,1)}, u32[]{:S(2)}) copy-start(bf16[16,2304]{1,0:T(8,128)(2,1)} %first_ref.1) | copy-start | bytes 221188
  185.0 10.2 %copy-start.6 = (bf16[16,2304]{1,0:T(8,128)(2,1)S(1)}, bf16[16,2304]{1,0:T(8,128)(2,1)}, u32[]{:S(2)}) copy-start(bf16[16,2304]{1,0:T(8,128)(2,1)} %second_ref.1) | copy-start | bytes 221188
  185.0 10.2 %copy-start.8 = (f32[16,18]{1,0:T(8,128)S(1)}, f32[16,18]{1,0:T(8,128)}, u32[]{:S(2)}) copy-start(f32[16,18]{1,0:T(8,128)} %fscale_ref.1) | copy-start | bytes 3460
  185.0 10.2 %copy-start.9 = (f32[16,18]{1,0:T(8,128)S(1)}, f32[16,18]{1,0:T(8,128)}, u32[]{:S(2)}) copy-start(f32[16,18]{1,0:T(8,128)} %sscale_ref.1) | copy-start | bytes 3460

commit v2 on v1

--- a/solution.py
+++ b/solution.py
@@ -12,11 +12,12 @@
 TILE = 256
 BLOCKS = 8
 NOTE = 16
+WIDE = 768
 SEQ = ("seq_0", "seq_1")
 DP = ("dp_0", "dp_1", "dp_2")
 DP_SEQ = ("dp_0", "dp_1", "dp_2", "seq_0", "seq_1")
 LOG2E = 1.4426950408889634
-VMEM_LIMIT = 48 * 1024 * 1024
+VMEM_LIMIT = 60 * 1024 * 1024
 
 score_scale = 144.0 ** (-0.5)
 soft_cap = 50.0
@@ -141,17 +142,18 @@
     )(packed)
 
 
-def gradient_kernel(me_ref, att_ref, *refs):
-    cots, out_ref = refs[:8], refs[8]
-    x, c = me_ref[0], me_ref[2]
-    total = jnp.zeros((256, TILE), F32)
-    for core in range(2):
-        for k in range(4):
-            member = lax.rem(x - k + 4, 4) * 2 + (c if core == 0 else 1 - c)
-            total += jnp.dot(
-                att_ref[member], cots[core * 4 + k][...], preferred_element_type=F32
-            )
-    low = total.astype(BF16)
+def gradient_kernel(c_ref, att_ref, own_ref, other_ref, out_ref, left):
+    @pl.when(pl.program_id(0) == 0)
+    def _():
+        for core in range(2):
+            mine = c_ref[0] if core == 0 else 1 - c_ref[0]
+            for x in range(4):
+                left[core, :, x * TILE : (x + 1) * TILE] = att_ref[x * 2 + mine]
+
+    low = (
+        jnp.dot(left[0], own_ref[...], preferred_element_type=F32)
+        + jnp.dot(left[1], other_ref[...], preferred_element_type=F32)
+    ).astype(BF16)
     for fx in range(4):
         for fy in range(2):
             for fh in range(2):
@@ -159,63 +161,64 @@
                 out_ref[(fy * 4 + fx) * 2 + fh] = low[row : row + 16]
 
 
-def gradient_rows(me, att, cots):
+def gradient_rows(core, att, own, other):
     return pl.pallas_call(
         gradient_kernel,
         grid_spec=pltpu.PrefetchScalarGridSpec(
             num_scalar_prefetch=1,
-            grid=(DO // TILE,),
-            in_specs=[pl.BlockSpec((8, 256, TILE), lambda n, me: (0, 0, 0))]
-            + [pl.BlockSpec((TILE, TILE), lambda n, me: (0, n))] * 8,
-            out_specs=pl.BlockSpec((16, 16, TILE), lambda n, me: (0, 0, n)),
+            grid=(DO // WIDE,),
+            in_specs=[
+                pl.BlockSpec((8, 256, TILE), lambda n, c: (0, 0, 0)),
+                pl.BlockSpec((1024, WIDE), lambda n, c: (0, n)),
+                pl.BlockSpec((1024, WIDE), lambda n, c: (0, n)),
+            ],
+            out_specs=pl.BlockSpec((16, 16, WIDE), lambda n, c: (0, 0, n)),
+            scratch_shapes=[pltpu.VMEM((2, 256, 1024), BF16)],
         ),
         out_shape=jax.ShapeDtypeStruct((16, 16, DO), BF16),
         compiler_params=params("arbitrary"),
+        cost_estimate=pl.CostEstimate(
+            flops=2 * 256 * 2048 * DO, bytes_accessed=12_000_000, transcendentals=0
+        ),
         name="gradient_rows",
-    )(me, att, *cots)
-
-
-def project_kernel(me_ref, att_ref, *refs):
-    rows, out_ref, left = refs[:8], refs[8], refs[9]
-    x, c, z = me_ref[0], me_ref[2], me_ref[3]
-    y = me_ref[4] * 2 + me_ref[1]
-
+    )(core, att, own, other)
+
+
+def project_kernel(c_ref, att_ref, own_ref, other_ref, out_ref, left):
     @pl.when(pl.program_id(0) == 0)
     def _():
         for core in range(2):
-            fc = c if core == 0 else 1 - c
-            for kx in range(4):
-                fx = lax.rem(x - kx + 4, 4)
-                blocks = []
-                for kz in range(4):
-                    fz = lax.rem(z - kz + 4, 4)
-                    for ky in range(4):
-                        fy = lax.rem(y - ky + 4, 4)
-                        low, high = lax.rem(fy, 2), fy // 2
-                        blocks.append(att_ref[fz * 2 + fc, fx * 4 + low * 2 + high])
-                left[core * 4 + kx] = jnp.concatenate(blocks, axis=0).T
-
-    total = jnp.zeros((TILE, TILE), F32)
-    for k in range(8):
-        total += jnp.dot(left[k], rows[k][...], preferred_element_type=F32)
-    out_ref[0] = total.astype(BF16)
-
-
-def project(me, att, rows):
+            mine = c_ref[0] if core == 0 else 1 - c_ref[0]
+            for z in range(4):
+                left[core, :, z * TILE : (z + 1) * TILE] = att_ref[z * 2 + mine].T
+
+    out_ref[0] = (
+        jnp.dot(left[0], own_ref[...], preferred_element_type=F32)
+        + jnp.dot(left[1], other_ref[...], preferred_element_type=F32)
+    ).astype(BF16)
+
+
+def project(core, att, own, other):
     return pl.pallas_call(
         project_kernel,
         grid_spec=pltpu.PrefetchScalarGridSpec(
             num_scalar_prefetch=1,
-            grid=(DO // TILE,),
-            in_specs=[pl.BlockSpec((8, 16, 16, TILE), lambda n, me: (0, 0, 0, 0))]
-            + [pl.BlockSpec((TILE, TILE), lambda n, me: (0, n))] * 8,
-            out_specs=pl.BlockSpec((1, TILE, TILE), lambda n, me: (0, 0, n)),
-            scratch_shapes=[pltpu.VMEM((8, TILE, TILE), BF16)],
+            grid=(DO // WIDE,),
+            in_specs=[
+                pl.BlockSpec((8, 256, TILE), lambda n, c: (0, 0, 0)),
+                pl.BlockSpec((1024, WIDE), lambda n, c: (0, n)),
+                pl.BlockSpec((1024, WIDE), lambda n, c: (0, n)),
+            ],
+            out_specs=pl.BlockSpec((1, TILE, WIDE), lambda n, c: (0, 0, n)),
+            scratch_shapes=[pltpu.VMEM((2, TILE, 1024), BF16)],
         ),
         out_shape=jax.ShapeDtypeStruct((1, TILE, DO), BF16),
         compiler_params=params("arbitrary"),
+        cost_estimate=pl.CostEstimate(
+            flops=2 * 256 * 2048 * DO, bytes_accessed=12_000_000, transcendentals=0
+        ),
         name="project",
-    )(me, att, *rows)
+    )(core, att, own, other)
 
 
 def total_kernel(parts_ref, grad_ref, squares_ref):
@@ -291,54 +294,43 @@
     return lax.ppermute(x, axis, [(i, (i + by) % peers) for i in range(peers)])
 
 
-def shift_y(x, by):
-    pairs = []
-    for y in range(4):
-        to = (y + by) % 4
-        pairs.append(((y % 2) * 2 + y // 2, (to % 2) * 2 + to // 2))
-    return lax.ppermute(x, ("dp_1", "seq_1"), pairs)
-
-
-def from_along(x, move):
-    return [x] + [move(x, k) for k in (1, 2, 3)]
+def sent_to_all(x, axes):
+    peers = lax.axis_size(axes)
+    return lax.all_to_all(jnp.broadcast_to(x[None], (peers, *x.shape)), axes, 0, 0, tiled=True)
 
 
 def local(
     queries, keys, values, segments, cotangent, weight,
     first_moment, first_scale, second_moment, second_scale,
 ):
-    me = jnp.stack([lax.axis_index(a) for a in DP_SEQ]).astype(jnp.int32)
-    across = lambda v, k: shift(v, "dp_0", k)
+    core = lax.axis_index("dp_2").astype(jnp.int32)[None]
 
     packed = pack(queries[0], keys[0], values[0], segments)
     arrived = lax.all_to_all(packed, SEQ, 0, 0, tiled=True)
 
-    cots = from_along(cotangent[0], across)
-    cots = cots + [shift(v, "dp_2", 1) for v in cots]
-
-    rows = weight.astype(BF16)
-    rows = jnp.concatenate(from_along(rows, shift_y), axis=0)
-    rows = jnp.concatenate(from_along(rows, lambda v, k: shift(v, "seq_0", k)), axis=0)
-    rows = from_along(rows, across)
-    rows = rows + [shift(v, "dp_2", 1) for v in rows]
+    cots = sent_to_all(cotangent[0], "dp_0").reshape(1024, DO)
+    other_cots = shift(cots, "dp_2", 1)
+
+    rows = sent_to_all(weight.astype(BF16), ("dp_0", "dp_1", "seq_1")).reshape(256, DO)
+    rows = sent_to_all(rows, "seq_0").reshape(1024, DO)
+    other_rows = shift(rows, "dp_2", 1)
 
     attended = attend(arrived)
     columns = lax.all_to_all(
         attended, ("dp_0", "dp_2", "seq_0", "seq_1"), 0, 0, tiled=True
     ).reshape(8, 256, TILE)
-    partial = gradient_rows(me, columns, cots)
+    partial = gradient_rows(core, columns, cots, other_cots)
     parts = lax.all_to_all(partial, ("dp_1", "seq_0", "seq_1"), 0, 0, tiled=True)
     grad, squares = total_rows(parts)
-    swap = [
-        ((x * 4 + z) , (z * 4 + x)) for x in range(4) for z in range(4)
-    ]
-    grad = lax.ppermute(grad, ("dp_0", "seq_0"), swap)
+    grad = lax.ppermute(
+        grad, ("dp_0", "seq_0"), [(x * 4 + z, z * 4 + x) for x in range(4) for z in range(4)]
+    )
     squares = lax.all_to_all(squares, DP_SEQ, 0, 0, tiled=True)
     new_weight, new_first, new_fscale, new_second, new_sscale = adam(
         grad, squares, weight, first_moment, first_scale, second_moment, second_scale
     )
-    own = lax.all_to_all(columns, ("dp_0", "dp_2"), 0, 0, tiled=True).reshape(8, 16, 16, TILE)
-    layer_out = project(me, own, rows)
+    own = lax.all_to_all(columns, ("dp_0", "dp_2"), 0, 0, tiled=True)
+    layer_out = project(core, own, rows, other_rows)
     return (layer_out, new_weight, new_first, new_fscale, new_second, new_sscale)
 
 

time: 198 us -> 287 us (1.45)
  blocking collectives: 0 us -> 103 us
  starting transfers between devices: 75.2 us -> 39.7 us
  waiting for transfers between devices: 75.5 us -> 96.8 us
    all_to_all x0 -> x3, blocking collectives: none -> 103 us  [the longest x2 80.7 us: sent_to_all(): lax.all_to_all(jnp.broadcast_to(x[None], (peers, *x.shape)), axes, 0, 0,...]
    ppermute x17 -> x2, waiting for transfers between devices: 43.2 us -> 0.01 us  [shift(): return lax.ppermute(x, axis, [(i, (i + by) % peers) for i in range(peers)])]
    all_to_all x2, waiting for transfers between devices: 12.1 us -> 53.7 us  [the longest x1 42.3 us: sent_to_all(): lax.all_to_all(jnp.broadcast_to(x[None], (peers, *x.shape)), axes, 0, 0,...]
    ppermute x17 -> x2, starting transfers between devices: 34.1 us -> 7.64 us  [shift(): return lax.ppermute(x, axis, [(i, (i + by) % peers) for i in range(peers)])]
    all_to_all x1, waiting for transfers between devices: 0.01 us -> 21.4 us  [local(): arrived = lax.all_to_all(packed, SEQ, 0, 0, tiled=True)]
    ppermute x4 -> x1, waiting for transfers between devices: 20.2 us -> 0.01 us  [local(): lax.ppermute(grad, ('dp_0', 'seq_0'), [(x * 4 + z, z * 4 + x) for x in ra...]
    all_to_all x1, waiting for transfers between devices: 0.01 us -> 19.4 us  [local(): lax.all_to_all(attended, ('dp_0', 'dp_2', 'seq_0', 'seq_1'), 0, 0, tiled=...]
    ppermute x4 -> x1, starting transfers between devices: 6.66 us -> 1.56 us  [local(): lax.ppermute(grad, ('dp_0', 'seq_0'), [(x * 4 + z, z * 4 + x) for x in ra...]
  transfers between devices with their start and end apart: 26 -> 8, of which waited for: 7 -> 5; matrix products, arithmetic and copies ran while one was open for 1% -> 0% of each run, Pallas kernels for 16% -> 12%
where the time goes in v2:
time: 287 us; the launch traced here: 286 us
  blocking collectives  103 us (36%)
  waiting for transfers between devices  96.8 us (34%)
  starting transfers between devices  39.7 us (14%)
  Pallas kernels  38.6 us (13%)
  local copies, waits for them, and re-layouts  6.47 us (2%)
    all_to_all x2, blocking collectives, sent_to_all(): lax.all_to_all(jnp.broadcast_to(x[None], (peers, *x.shape)), axes, 0, 0,...  80.7 us
    all_to_all x1, waiting for transfers between devices, sent_to_all(): lax.all_to_all(jnp.broadcast_to(x[None], (peers, *x.shape)), axes, 0, 0,...  42.3 us
    all_to_all x1, blocking collectives, local(): lax.all_to_all(partial, ('dp_1', 'seq_0', 'seq_1'), 0, 0, tiled=True)  22.3 us
    all_to_all x1, waiting for transfers between devices, local(): arrived = lax.all_to_all(packed, SEQ, 0, 0, tiled=True)  21.4 us
    all_to_all x1, waiting for transfers between devices, local(): lax.all_to_all(attended, ('dp_0', 'dp_2', 'seq_0', 'seq_1'), 0, 0, tiled=...  19.4 us
    pallas_call x1, Pallas kernels, attend(): pl.pallas_call(attend_kernel, out_shape=jax.ShapeDtypeStruct((64, 32, TIL...  12.4 us
    all_to_all x1, starting transfers between devices, local(): lax.all_to_all(attended, ('dp_0', 'dp_2', 'seq_0', 'seq_1'), 0, 0, tiled=...  11.4 us
    all_to_all x1, waiting for transfers between devices, local(): own = lax.all_to_all(columns, ('dp_0', 'dp_2'), 0, 0, tiled=True)  11.4 us
  transfers between devices with their start and end apart: 8, of which 5 were waited for; matrix products, arithmetic and copies ran while one was open for 0% of the time, Pallas kernels for 12%

profile of v2, /device:TPU:1, one launch (start us, length us, event | category | flops | bytes accessed | tf_op | source)
XLA Modules:
  0.0 286.4 jit_solution(13832873991533633197)
XLA Ops:
  0.6 0.0 copy-start.3
  0.6 1.0 convert_element_type.3
  1.7 0.1 broadcast_in_dim.24
  1.7 25.1 %all_to_all.40 = bf16[16,16,2304]{2,1,0:T(8,128)(2,1)S(1)} all-to-all(bf16[16,16,2304]{2,1,0:T(8,128)(2,1)S(1)} %broadcast_in_dim.24), channel_id=1, replica_groups=mesh['dp_0'=4,'dp_1'=2,'dp_2'=2,'seq_0'=4,'seq_1'=2] {'dp_0','dp_1','seq..., dimensions={0} | all-to-all | bytes 2359296 | tf_op jit(solution)/shard_map/all_to_all | solution.py:299
  26.9 0.0 copy-done.3
  26.9 0.3 broadcast_in_dim.28
  27.2 55.6 %all_to_all.41 = bf16[4,256,2304]{2,1,0:T(8,128)(2,1)} all-to-all(bf16[4,256,2304]{2,1,0:T(8,128)(2,1)S(1)} %broadcast_in_dim.28), channel_id=1, replica_groups=mesh['dp_0'=4,'dp_1'=2,'dp_2'=2,'seq_0'=4,'seq_1'=2] {'dp_0'}, dimensions={0} | all-to-all | bytes 9437184 | tf_op jit(solution)/shard_map/all_to_all | solution.py:299
  82.8 2.5 broadcast_in_dim.26
  85.3 5.0 %all-to-all-start.4 = ((bf16[4,256,2304]{2,1,0:T(8,128)(2,1)}), bf16[4,256,2304]{2,1,0:T(8,128)(2,1)}, u32[]{:S(2)}, u32[]{:S(2)}) async-start(bf16[4,256,2304]{2,1,0:T(8,128)(2,1)} %broadcast_in_dim.26), calls=%async_computation.4 | async-start | bytes 9437184 | tf_op jit(solution)/shard_map/all_to_all | solution.py:299
  90.3 3.5 %collective-permute-start.1 = (bf16[1024,2304]{1,0:T(8,128)(2,1)}, bf16[1024,2304]{1,0:T(8,128)(2,1)}, u32[]{:S(2)}, u32[]{:S(2)}) collective-permute-start(bf16[1024,2304]{1,0:T(8,128)(2,1)} %bitcast.9), channel_id=1, source_target_pairs={{0,8},{8,0},{1,9},{9,1},{2,10},{10,2},{3,11},{11,3},{4,12},{12,4},... | collective-permute-start | bytes 14155784 | tf_op jit(solution)/shard_map/ppermute | solution.py:294
  93.9 6.2 %pack.1 = bf16[8,272,512]{2,1,0:T(8,128)(2,1)} custom-call(bf16[256,2048]{1,0:T(8,128)(2,1)} %bitcast.15, bf16[256,1024]{1,0:T(8,128)(2,1)} %bitcast.16, bf16[256,1024]{1,0:T(8,128)(2,1)} %bitcast.17, s32[1,256]{1,0:T(1,128)} %seg_ref.1), custom_call_target="tpu_custom_call" | custom-call | tf_op jit(solution)/shard_map/pack/pallas_call | solution.py:59
  100.1 42.3 %all-to-all-done.4 = bf16[4,256,2304]{2,1,0:T(8,128)(2,1)} async-done(((bf16[4,256,2304]{2,1,0:T(8,128)(2,1)}), bf16[4,256,2304]{2,1,0:T(8,128)(2,1)}, u32[]{:S(2)}, u32[]{:S(2)}) %all-to-all-start.4) | async-done | bytes 4718624 | tf_op jit(solution)/shard_map/all_to_all | solution.py:299
  142.5 3.6 %all-to-all-start = ((bf16[8,272,512]{2,1,0:T(8,128)(2,1)}), bf16[8,272,512]{2,1,0:T(8,128)(2,1)S(1)}, u32[]{:S(2)}, u32[]{:S(2)}) async-start(bf16[8,272,512]{2,1,0:T(8,128)(2,1)} %pack.1), calls=%async_computation | async-start | bytes 4456448 | tf_op jit(solution)/shard_map/all_to_all | solution.py:309
  146.1 4.1 %collective-permute-start = (bf16[1024,2304]{1,0:T(8,128)(2,1)}, bf16[1024,2304]{1,0:T(8,128)(2,1)}, u32[]{:S(2)}, u32[]{:S(2)}) collective-permute-start(bf16[1024,2304]{1,0:T(8,128)(2,1)} %bitcast.6.own_ref), channel_id=1, source_target_pairs={{0,8},{8,0},{1,9},{9,1},{2,10},{10,2},{3,11},{11,3},{4,12},{12,4},... | collective-permute-start | bytes 14155784 | tf_op jit(solution)/shard_map/ppermute | solution.py:294
  150.2 21.4 %all-to-all-done.in_ref = bf16[8,272,512]{2,1,0:T(8,128)(2,1)S(1)} async-done(((bf16[8,272,512]{2,1,0:T(8,128)(2,1)}), bf16[8,272,512]{2,1,0:T(8,128)(2,1)S(1)}, u32[]{:S(2)}, u32[]{:S(2)}) %all-to-all-start) | async-done | bytes 2228256 | tf_op jit(solution)/shard_map/all_to_all | solution.py:309
  171.6 0.0 copy-start.1
  171.6 1.3 copy-done.1
  172.9 12.4 %attend.1 = bf16[64,32,256]{2,1,0:T(8,128)(2,1)} custom-call(bf16[8,272,512]{2,1,0:T(8,128)(2,1)} %copy-done.1), custom_call_target="tpu_custom_call" | custom-call | tf_op jit(solution)/shard_map/attend/pallas_call | solution.py:134
  185.4 11.4 %all-to-all-start.1 = ((bf16[64,32,256]{2,1,0:T(8,128)(2,1)}), bf16[64,32,256]{2,1,0:T(8,128)(2,1)S(1)}, u32[]{:S(2)}, u32[]{:S(2)}) async-start(bf16[64,32,256]{2,1,0:T(8,128)(2,1)} %attend.1), calls=%async_computation.1 | async-start | bytes 2097152 | tf_op jit(solution)/shard_map/all_to_all | solution.py:319
  196.8 19.4 %all-to-all-done.1 = bf16[64,32,256]{2,1,0:T(8,128)(2,1)S(1)} async-done(((bf16[64,32,256]{2,1,0:T(8,128)(2,1)}), bf16[64,32,256]{2,1,0:T(8,128)(2,1)S(1)}, u32[]{:S(2)}, u32[]{:S(2)}) %all-to-all-start.1) | async-done | bytes 1048608 | tf_op jit(solution)/shard_map/all_to_all | solution.py:319
  216.2 0.0 copy-start
  216.2 0.0 collective-permute-done.1.other_ref
  216.2 1.0 copy-done
  217.2 7.2 %gradient_rows.1 = bf16[16,16,2304]{2,1,0:T(8,128)(2,1)} custom-call(s32[1]{0:T(128)} %bitcast.c_ref, bf16[8,256,256]{2,1,0:T(8,128)(2,1)} %bitcast.11, bf16[1024,2304]{1,0:T(8,128)(2,1)} %bitcast.10, bf16[1024,2304]{1,0:T(8,128)(2,1)} %collective-permute-done.1.other_ref), custom_call_target="tpu_custom_call" | custom-call | flops 2415919104 | bytes 12000000 | tf_op jit(solution)/shard_map/gradient_rows/pallas_call | solution.py:165
  224.4 22.3 %all_to_all.42.parts_ref = bf16[16,16,2304]{2,1,0:T(8,128)(2,1)} all-to-all(bf16[16,16,2304]{2,1,0:T(8,128)(2,1)} %gradient_rows.1), channel_id=1, replica_groups=mesh['dp_0'=4,'dp_1'=2,'dp_2'=2,'seq_0'=4,'seq_1'=2] {'dp_1','seq_0','se..., dimensions={0} | all-to-all | bytes 2359296 | tf_op jit(solution)/shard_map/all_to_all | solution.py:323
  246.7 5.1 %all-to-all-start.2 = ((bf16[8,256,256]{2,1,0:T(8,128)(2,1)}), bf16[8,256,256]{2,1,0:T(8,128)(2,1)S(1)}, u32[]{:S(2)}, u32[]{:S(2)}) async-start(bf16[8,256,256]{2,1,0:T(8,128)(2,1)} %bitcast.12), calls=%async_computation.2 | async-start | bytes 2097152 | tf_op jit(solution)/shard_map/all_to_all | solution.py:332
  251.8 2.2 total_rows.1
  254.1 1.6 collective-permute-start.2
  255.6 11.4 %all-to-all-done.2.att_ref = bf16[8,256,256]{2,1,0:T(8,128)(2,1)S(1)} async-done(((bf16[8,256,256]{2,1,0:T(8,128)(2,1)}), bf16[8,256,256]{2,1,0:T(8,128)(2,1)S(1)}, u32[]{:S(2)}, u32[]{:S(2)}) %all-to-all-start.2) | async-done | bytes 1048608 | tf_op jit(solution)/shard_map/all_to_all | solution.py:332
  267.0 0.0 copy-start.2
  267.0 5.3 %all-to-all-start.7 = ((f32[128,1,128]{2,1,0:T(1,128)}), f32[128,1,128]{2,1,0:T(1,128)S(1)}, u32[]{:S(2)}, u32[]{:S(2)}) async-start(f32[128,1,128]{2,1,0:T(1,128)} %get-tuple-element.14), calls=%async_computation.7 | async-start | bytes 131072 | tf_op jit(solution)/shard_map/all_to_all | solution.py:328
  272.3 0.0 collective-permute-done.other_ref
  272.3 0.0 copy-done.2
  272.3 7.4 %project.1 = bf16[1,256,2304]{2,1,0:T(8,128)(2,1)} custom-call(s32[1]{0:T(128)} %bitcast.c_ref, bf16[8,256,256]{2,1,0:T(8,128)(2,1)} %copy-done.2, bf16[1024,2304]{1,0:T(8,128)(2,1)} %bitcast.6.own_ref, bf16[1024,2304]{1,0:T(8,128)(2,1)} %collective-permute-done.other_ref), custom_call_target="tpu_custom_call" | custom-call | flops 2415919104 | bytes 12000000 | tf_op jit(solution)/shard_map/project/pallas_call | solution.py:202
  279.8 2.3 all-to-all-done.7.squares_ref
  282.1 0.0 copy-start.4
  282.1 0.0 collective-permute-done.2.grad_ref
  282.1 0.6 copy-done.4
  282.7 0.0 copy-start.5
  282.7 0.6 copy-done.5
  283.4 3.0 %adam.1 = (f32[16,2304]{1,0:T(8,128)}, bf16[16,2304]{1,0:T(8,128)(2,1)}, f32[16,18]{1,0:T(8,128)}, bf16[16,2304]{1,0:T(8,128)(2,1)}, f32[16,18]{1,0:T(8,128)}) custom-call(f32[16,2304]{1,0:T(8,128)} %copy-done.5, f32[128,1,128]{2,1,0:T(1,128)} %copy-done.4, f32[16,2304]{1,0:T(8,128)} %weight_ref.1, bf16[16,2304]{1,0:T(8,128)(2,1)} %first_ref.1, ...), custom_call_target="tpu_custom_call" | custom-call | tf_op jit(solution)/shard_map/adam/pallas_call | solution.py:282
Async XLA Ops:
  0.6 26.3 %copy-start.3 = (bf16[1,256,2304]{2,1,0:T(8,128)(2,1)S(1)}, bf16[1,256,2304]{2,1,0:T(8,128)(2,1)}, u32[]{:S(2)}) copy-start(bf16[1,256,2304]{2,1,0:T(8,128)(2,1)} %param.14) | copy-start | bytes 3538948
  85.3 57.2 %all-to-all-start.4 = ((bf16[4,256,2304]{2,1,0:T(8,128)(2,1)}), bf16[4,256,2304]{2,1,0:T(8,128)(2,1)}, u32[]{:S(2)}, u32[]{:S(2)}) async-start(bf16[4,256,2304]{2,1,0:T(8,128)(2,1)} %broadcast_in_dim.26), calls=%async_computation.4 | async-start | bytes 9437184 | tf_op jit(solution)/shard_map/all_to_all | solution.py:299
  90.3 125.9 %collective-permute-start.1 = (bf16[1024,2304]{1,0:T(8,128)(2,1)}, bf16[1024,2304]{1,0:T(8,128)(2,1)}, u32[]{:S(2)}, u32[]{:S(2)}) collective-permute-start(bf16[1024,2304]{1,0:T(8,128)(2,1)} %bitcast.9), channel_id=1, source_target_pairs={{0,8},{8,0},{1,9},{9,1},{2,10},{10,2},{3,11},{11,3},{4,12},{12,4},... | collective-permute-start | bytes 14155784 | tf_op jit(solution)/shard_map/ppermute | solution.py:294
  142.5 29.1 %all-to-all-start = ((bf16[8,272,512]{2,1,0:T(8,128)(2,1)}), bf16[8,272,512]{2,1,0:T(8,128)(2,1)S(1)}, u32[]{:S(2)}, u32[]{:S(2)}) async-start(bf16[8,272,512]{2,1,0:T(8,128)(2,1)} %pack.1), calls=%async_computation | async-start | bytes 4456448 | tf_op jit(solution)/shard_map/all_to_all | solution.py:309
  146.1 126.2 %collective-permute-start = (bf16[1024,2304]{1,0:T(8,128)(2,1)}, bf16[1024,2304]{1,0:T(8,128)(2,1)}, u32[]{:S(2)}, u32[]{:S(2)}) collective-permute-start(bf16[1024,2304]{1,0:T(8,128)(2,1)} %bitcast.6.own_ref), channel_id=1, source_target_pairs={{0,8},{8,0},{1,9},{9,1},{2,10},{10,2},{3,11},{11,3},{4,12},{12,4},... | collective-permute-start | bytes 14155784 | tf_op jit(solution)/shard_map/ppermute | solution.py:294
  171.6 1.3 copy-start.1
  185.4 30.8 %all-to-all-start.1 = ((bf16[64,32,256]{2,1,0:T(8,128)(2,1)}), bf16[64,32,256]{2,1,0:T(8,128)(2,1)S(1)}, u32[]{:S(2)}, u32[]{:S(2)}) async-start(bf16[64,32,256]{2,1,0:T(8,128)(2,1)} %attend.1), calls=%async_computation.1 | async-start | bytes 2097152 | tf_op jit(solution)/shard_map/all_to_all | solution.py:319
  216.2 1.0 copy-start
  246.7 20.3 %all-to-all-start.2 = ((bf16[8,256,256]{2,1,0:T(8,128)(2,1)}), bf16[8,256,256]{2,1,0:T(8,128)(2,1)S(1)}, u32[]{:S(2)}, u32[]{:S(2)}) async-start(bf16[8,256,256]{2,1,0:T(8,128)(2,1)} %bitcast.12), calls=%async_computation.2 | async-start | bytes 2097152 | tf_op jit(solution)/shard_map/all_to_all | solution.py:332
  254.1 28.0 %collective-permute-start.2 = (f32[16,2304]{1,0:T(8,128)}, f32[16,2304]{1,0:T(8,128)S(1)}, u32[]{:S(2)}, u32[]{:S(2)}) collective-permute-start(f32[16,2304]{1,0:T(8,128)} %get-tuple-element.13), channel_id=1, source_target_pairs={{0,0},{2,32},{4,64},{6,96},{32,2},{34,34},{36,66},{38,98},{64,4},{... | collective-permute-start | bytes 442376 | tf_op jit(solution)/shard_map/ppermute | solution.py:325
  267.0 5.3 %copy-start.2 = (bf16[8,256,256]{2,1,0:T(8,128)(2,1)}, bf16[8,256,256]{2,1,0:T(8,128)(2,1)S(1)}, u32[]{:S(2)}) copy-start(bf16[8,256,256]{2,1,0:T(8,128)(2,1)S(1)} %all-to-all-done.2.att_ref) | copy-start | bytes 3145732
  267.0 15.1 %all-to-all-start.7 = ((f32[128,1,128]{2,1,0:T(1,128)}), f32[128,1,128]{2,1,0:T(1,128)S(1)}, u32[]{:S(2)}, u32[]{:S(2)}) async-start(f32[128,1,128]{2,1,0:T(1,128)} %get-tuple-element.14), calls=%async_computation.7 | async-start | bytes 131072 | tf_op jit(solution)/shard_map/all_to_all | solution.py:328
  282.1 0.6 copy-start.4
  282.7 0.6 copy-start.5

commit v3 on v1

--- a/solution.py
+++ b/solution.py
@@ -12,11 +12,13 @@
 TILE = 256
 BLOCKS = 8
 NOTE = 16
+WIDE = 768
+ORDER = (0, 1, 3, 2)
 SEQ = ("seq_0", "seq_1")
 DP = ("dp_0", "dp_1", "dp_2")
 DP_SEQ = ("dp_0", "dp_1", "dp_2", "seq_0", "seq_1")
 LOG2E = 1.4426950408889634
-VMEM_LIMIT = 48 * 1024 * 1024
+VMEM_LIMIT = 60 * 1024 * 1024
 
 score_scale = 144.0 ** (-0.5)
 soft_cap = 50.0
@@ -44,29 +46,25 @@
 
 
 def pack_kernel(q_ref, k_ref, v_ref, seg_ref, out_ref):
-    out_ref[0, :TILE, 0:256] = q_ref[...]
-    out_ref[0, :TILE, 256:384] = restored(k_ref[...])
-    out_ref[0, :TILE, 384:512] = restored(v_ref[...])
     seg = seg_ref[...]
     below_1 = jnp.sum((seg < 1).astype(F32), axis=-1, keepdims=True)
     below_2 = jnp.sum((seg < 2).astype(F32), axis=-1, keepdims=True)
-    out_ref[0, TILE:, 0:256] = jnp.broadcast_to(below_1, (NOTE, 256)).astype(BF16)
-    out_ref[0, TILE:, 256:512] = jnp.broadcast_to(below_2, (NOTE, 256)).astype(BF16)
+    notes = jnp.concatenate(
+        [jnp.broadcast_to(b, (NOTE, 256)) for b in (below_1, below_2)], axis=1
+    ).astype(BF16)
+    for h in range(BLOCKS):
+        out_ref[h, :TILE, 0:256] = q_ref[:, h * 256 : (h + 1) * 256]
+        out_ref[h, :TILE, 256:384] = restored(k_ref[:, h * 128 : (h + 1) * 128])
+        out_ref[h, :TILE, 384:512] = restored(v_ref[:, h * 128 : (h + 1) * 128])
+        out_ref[h, TILE:, :] = notes
 
 
 def pack(q, k, v, seg):
     return pl.pallas_call(
         pack_kernel,
-        grid=(BLOCKS,),
-        in_specs=[
-            pl.BlockSpec((TILE, 256), lambda h: (0, h)),
-            pl.BlockSpec((TILE, 128), lambda h: (0, h)),
-            pl.BlockSpec((TILE, 128), lambda h: (0, h)),
-            pl.BlockSpec((1, TILE), lambda h: (0, 0)),
-        ],
-        out_specs=pl.BlockSpec((1, TILE + NOTE, 512), lambda h: (h, 0, 0)),
         out_shape=jax.ShapeDtypeStruct((BLOCKS, TILE + NOTE, 512), BF16),
-        compiler_params=params("arbitrary"),
+        compiler_params=params(),
+        cost_estimate=pl.CostEstimate(flops=0, bytes_accessed=6_000_000, transcendentals=0),
         name="pack",
     )(q, k, v, seg)
 
@@ -122,100 +120,83 @@
         step(i, (key_row <= query_col) & (key_row + i * TILE >= start_row))
 
         attended = (acc[...] / jnp.sum(total[...], axis=0, keepdims=True)).astype(BF16)
-        for x in range(4):
-            for c in range(2):
-                out_ref[(x * 2 + c) * BLOCKS + i] = attended[
-                    x * 32 : (x + 1) * 32, c * TILE : (c + 1) * TILE
-                ]
+        for c in range(2):
+            out_ref[i, c * 128 : (c + 1) * 128] = attended[:, c * TILE : (c + 1) * TILE]
 
 
 def attend(packed):
     return pl.pallas_call(
         attend_kernel,
-        out_shape=jax.ShapeDtypeStruct((64, 32, TILE), BF16),
+        out_shape=jax.ShapeDtypeStruct((BLOCKS, 256, TILE), BF16),
         in_specs=[pl.BlockSpec(memory_space=pltpu.VMEM)],
         out_specs=pl.BlockSpec(memory_space=pltpu.VMEM),
         scratch_shapes=[pltpu.VMEM((128, 2 * TILE), F32), pltpu.VMEM((8, 2 * TILE), F32)],
         compiler_params=params(),
+        cost_estimate=pl.CostEstimate(
+            flops=10_000_000_000, bytes_accessed=4_000_000, transcendentals=0
+        ),
         name="attend",
     )(packed)
 
 
 def gradient_kernel(me_ref, att_ref, *refs):
-    cots, out_ref = refs[:8], refs[8]
-    x, c = me_ref[0], me_ref[2]
-    total = jnp.zeros((256, TILE), F32)
-    for core in range(2):
-        for k in range(4):
-            member = lax.rem(x - k + 4, 4) * 2 + (c if core == 0 else 1 - c)
-            total += jnp.dot(
-                att_ref[member], cots[core * 4 + k][...], preferred_element_type=F32
-            )
-    low = total.astype(BF16)
-    for fx in range(4):
-        for fy in range(2):
-            for fh in range(2):
-                row = ((fx * 2 + fy) * 2 + fh) * 16
-                out_ref[(fy * 4 + fx) * 2 + fh] = low[row : row + 16]
-
-
-def gradient_rows(me, att, cots):
-    return pl.pallas_call(
-        gradient_kernel,
-        grid_spec=pltpu.PrefetchScalarGridSpec(
-            num_scalar_prefetch=1,
-            grid=(DO // TILE,),
-            in_specs=[pl.BlockSpec((8, 256, TILE), lambda n, me: (0, 0, 0))]
-            + [pl.BlockSpec((TILE, TILE), lambda n, me: (0, n))] * 8,
-            out_specs=pl.BlockSpec((16, 16, TILE), lambda n, me: (0, 0, n)),
-        ),
-        out_shape=jax.ShapeDtypeStruct((16, 16, DO), BF16),
-        compiler_params=params("arbitrary"),
-        name="gradient_rows",
-    )(me, att, *cots)
-
-
-def project_kernel(me_ref, att_ref, *refs):
-    rows, out_ref, left = refs[:8], refs[8], refs[9]
-    x, c, z = me_ref[0], me_ref[2], me_ref[3]
-    y = me_ref[4] * 2 + me_ref[1]
+    cots, out_ref, left = refs[:10], refs[10], refs[11]
 
     @pl.when(pl.program_id(0) == 0)
     def _():
         for core in range(2):
-            fc = c if core == 0 else 1 - c
-            for kx in range(4):
-                fx = lax.rem(x - kx + 4, 4)
+            mine = me_ref[2] if core == 0 else 1 - me_ref[2]
+            for k, back in enumerate(ORDER):
+                x = lax.rem(me_ref[0] + 4 - back, 4)
+                low = core * 1024 + k * TILE
+                left[:, low : low + TILE] = att_ref[x * 2 + mine]
+
+    right = jnp.concatenate([r[...] for r in cots], axis=0)
+    low = jnp.dot(left[...], right, preferred_element_type=F32).astype(BF16)
+    out_ref[...] = low.reshape(16, 16, WIDE)
+
+
+def project_kernel(me_ref, att_ref, *refs):
+    rows, out_ref, left = refs[:10], refs[10], refs[11]
+    x, c, z = me_ref[0], me_ref[2], me_ref[3]
+    y = me_ref[4] * 2 + me_ref[1]
+
+    @pl.when(pl.program_id(0) == 0)
+    def _():
+        for core in range(2):
+            row_c = c if core == 0 else 1 - c
+            for k, back in enumerate(ORDER):
+                row_x = lax.rem(x + 4 - back, 4)
                 blocks = []
-                for kz in range(4):
-                    fz = lax.rem(z - kz + 4, 4)
-                    for ky in range(4):
-                        fy = lax.rem(y - ky + 4, 4)
-                        low, high = lax.rem(fy, 2), fy // 2
-                        blocks.append(att_ref[fz * 2 + fc, fx * 4 + low * 2 + high])
-                left[core * 4 + kx] = jnp.concatenate(blocks, axis=0).T
-
-    total = jnp.zeros((TILE, TILE), F32)
-    for k in range(8):
-        total += jnp.dot(left[k], rows[k][...], preferred_element_type=F32)
-    out_ref[0] = total.astype(BF16)
-
-
-def project(me, att, rows):
-    return pl.pallas_call(
-        project_kernel,
+                for back_z in range(4):
+                    row_z = lax.rem(z + 4 - back_z, 4)
+                    for back_y in range(4):
+                        row_y = lax.rem(y + 4 - back_y, 4)
+                        low, high = lax.rem(row_y, 2), row_y // 2
+                        blocks.append(att_ref[row_x * 2 + low, row_c * 8 + row_z * 2 + high])
+                at = core * 1024 + k * TILE
+                left[:, at : at + TILE] = jnp.concatenate(blocks, axis=0).T
+
+    right = jnp.concatenate([r[...] for r in rows], axis=0)
+    out_ref[0] = jnp.dot(left[...], right, preferred_element_type=F32).astype(BF16)
+
+
+def over_columns(kernel, me, fixed, moving, out_block, out_shape, name, flops):
+    return pl.pallas_call(
+        kernel,
         grid_spec=pltpu.PrefetchScalarGridSpec(
             num_scalar_prefetch=1,
-            grid=(DO // TILE,),
-            in_specs=[pl.BlockSpec((8, 16, 16, TILE), lambda n, me: (0, 0, 0, 0))]
-            + [pl.BlockSpec((TILE, TILE), lambda n, me: (0, n))] * 8,
-            out_specs=pl.BlockSpec((1, TILE, TILE), lambda n, me: (0, 0, n)),
-            scratch_shapes=[pltpu.VMEM((8, TILE, TILE), BF16)],
+            grid=(DO // WIDE,),
+            in_specs=[pl.BlockSpec(a.shape, lambda n, me, d=a.ndim: (0,) * d) for a in fixed]
+            + [pl.BlockSpec((a.shape[0], WIDE), lambda n, me: (0, n)) for a in moving],
+            out_specs=pl.BlockSpec(out_block, lambda n, me: (0, 0, n)),
+            scratch_shapes=[pltpu.VMEM((TILE, 2048), BF16)],
         ),
-        out_shape=jax.ShapeDtypeStruct((1, TILE, DO), BF16),
+        out_shape=jax.ShapeDtypeStruct(out_shape, BF16),
         compiler_params=params("arbitrary"),
-        name="project",
-    )(me, att, *rows)
+        cost_estimate=pl.CostEstimate(flops=flops, bytes_accessed=flops // 200, transcendentals=0),
+        name=name,
+    )(me, *fixed, *moving)
 
 
 def total_kernel(parts_ref, grad_ref, squares_ref):
@@ -291,6 +272,21 @@
     return lax.ppermute(x, axis, [(i, (i + by) % peers) for i in range(peers)])
 
 
+def after(x, earlier):
+    return lax.optimization_barrier((x, earlier))[0]
+
+
+def from_ring(mine):
+    half = mine.shape[0] // 2
+    left, right = shift(mine, "dp_0", 1), shift(mine, "dp_0", -1)
+    top, bottom = shift(left[:half], "dp_0", 1), shift(right[half:], "dp_0", -1)
+    return [mine, left, right, top, bottom]
+
+
+def from_partner(arrays):
+    return [shift(a, "dp_2", 1) for a in arrays]
+
+
 def shift_y(x, by):
     pairs = []
     for y in range(4):
@@ -299,46 +295,47 @@
     return lax.ppermute(x, ("dp_1", "seq_1"), pairs)
 
 
-def from_along(x, move):
-    return [x] + [move(x, k) for k in (1, 2, 3)]
-
-
 def local(
     queries, keys, values, segments, cotangent, weight,
     first_moment, first_scale, second_moment, second_scale,
 ):
     me = jnp.stack([lax.axis_index(a) for a in DP_SEQ]).astype(jnp.int32)
-    across = lambda v, k: shift(v, "dp_0", k)
 
     packed = pack(queries[0], keys[0], values[0], segments)
     arrived = lax.all_to_all(packed, SEQ, 0, 0, tiled=True)
-
-    cots = from_along(cotangent[0], across)
-    cots = cots + [shift(v, "dp_2", 1) for v in cots]
-
-    rows = weight.astype(BF16)
-    rows = jnp.concatenate(from_along(rows, shift_y), axis=0)
-    rows = jnp.concatenate(from_along(rows, lambda v, k: shift(v, "seq_0", k)), axis=0)
-    rows = from_along(rows, across)
-    rows = rows + [shift(v, "dp_2", 1) for v in rows]
+    cots = from_ring(cotangent[0])
 
     attended = attend(arrived)
-    columns = lax.all_to_all(
-        attended, ("dp_0", "dp_2", "seq_0", "seq_1"), 0, 0, tiled=True
-    ).reshape(8, 256, TILE)
-    partial = gradient_rows(me, columns, cots)
+    own = lax.all_to_all(attended, SEQ, 0, 0, tiled=True)
+    cots = cots + from_partner([after(a, attended) for a in cots])
+    rows = after(weight.astype(BF16), attended)
+    rows = jnp.concatenate([rows] + [shift_y(rows, k) for k in (1, 2, 3)], axis=0)
+
+    columns = lax.all_to_all(own, ("dp_0", "dp_2"), 0, 0, tiled=True)
+    rows = after(rows, own)
+    rows = jnp.concatenate([rows] + [shift(rows, "seq_0", k) for k in (1, 2, 3)], axis=0)
+
+    partial = over_columns(
+        gradient_kernel, me, [columns], cots, (16, 16, WIDE), (16, 16, DO), "gradient_rows",
+        2 * 256 * 2048 * DO,
+    )
+    rows = from_ring(after(rows, columns))
     parts = lax.all_to_all(partial, ("dp_1", "seq_0", "seq_1"), 0, 0, tiled=True)
-    grad, squares = total_rows(parts)
-    swap = [
-        ((x * 4 + z) , (z * 4 + x)) for x in range(4) for z in range(4)
-    ]
-    grad = lax.ppermute(grad, ("dp_0", "seq_0"), swap)
+
+    sums, squares = total_rows(parts)
+    grad = lax.ppermute(sums, ("dp_1", "dp_2"), [(0, 0), (1, 2), (2, 1), (3, 3)])
     squares = lax.all_to_all(squares, DP_SEQ, 0, 0, tiled=True)
+    rows = rows + from_partner(
+        [after(a, partial) for a in rows[:3]] + [after(a, sums) for a in rows[3:]]
+    )
+    layer_out = over_columns(
+        project_kernel, me, [own.reshape(8, 16, 16, TILE)], rows,
+        (1, TILE, WIDE), (1, TILE, DO), "project", 1000,
+    )
     new_weight, new_first, new_fscale, new_second, new_sscale = adam(
-        grad, squares, weight, first_moment, first_scale, second_moment, second_scale
-    )
-    own = lax.all_to_all(columns, ("dp_0", "dp_2"), 0, 0, tiled=True).reshape(8, 16, 16, TILE)
-    layer_out = project(me, own, rows)
+        after(grad, layer_out), squares, weight,
+        first_moment, first_scale, second_moment, second_scale,
+    )
     return (layer_out, new_weight, new_first, new_fscale, new_second, new_sscale)
 
 

time: 198 us -> 180 us (0.909)
  waiting for transfers between devices: 75.5 us -> 63 us
  starting transfers between devices: 75.2 us -> 63.4 us
  Pallas kernels: 36.1 us -> 38.8 us
  local copies, waits for them, and re-layouts: 8.76 us -> 11.1 us
    all_to_all x1, waiting for transfers between devices: 0.01 us -> 26.3 us  [local(): arrived = lax.all_to_all(packed, SEQ, 0, 0, tiled=True)]
    ppermute x3, waiting for transfers between devices: 20.2 us -> 5.93 us  [shift_y(): return lax.ppermute(x, ('dp_1', 'seq_1'), pairs)]
    ppermute x17 -> x21, waiting for transfers between devices: 43.2 us -> 30.8 us  [shift(): return lax.ppermute(x, axis, [(i, (i + by) % peers) for i in range(peers)])]
    all_to_all x2, waiting for transfers between devices: 12.1 us -> 0.01 us  [the longest x1 0.01 us: local(): columns = lax.all_to_all(own, ('dp_0', 'dp_2'), 0, 0, tiled=True)]
    ppermute x17 -> x21, starting transfers between devices: 34.1 us -> 27.1 us  [shift(): return lax.ppermute(x, axis, [(i, (i + by) % peers) for i in range(peers)])]
    slice x0 -> x4, local copies, waits for them, and re-layouts: none -> 5.8 us  [the longest x2 3.84 us: from_ring(): right[half:]]
    unnamed x33 -> x26, local copies, waits for them, and re-layouts: 8.66 us -> 4.7 us
  transfers between devices with their start and end apart: 26 -> 30, of which waited for: 7 -> 8; matrix products, arithmetic and copies ran while one was open for 1% -> 4% of each run, Pallas kernels for 16% -> 18%
where the time goes in v3:
time: 180 us; the launch traced here: 178 us
  starting transfers between devices  63.4 us (35%)
  waiting for transfers between devices  63 us (35%)
  Pallas kernels  38.8 us (22%)
  local copies, waits for them, and re-layouts  11.1 us (6%)
    ppermute x21, waiting for transfers between devices, shift(): return lax.ppermute(x, axis, [(i, (i + by) % peers) for i in range(peers)])  30.8 us
    ppermute x21, starting transfers between devices, shift(): return lax.ppermute(x, axis, [(i, (i + by) % peers) for i in range(peers)])  27.1 us
    all_to_all x1, waiting for transfers between devices, local(): arrived = lax.all_to_all(packed, SEQ, 0, 0, tiled=True)  26.3 us
    pallas_call x2, Pallas kernels, over_columns(): pl.pallas_call(kernel, grid_spec=pltpu.PrefetchScalarGridSpec(num_scalar_...  17.3 us
    pallas_call x1, Pallas kernels, attend(): pl.pallas_call(attend_kernel, out_shape=jax.ShapeDtypeStruct((BLOCKS, 256...  12.4 us
    all_to_all x1, starting transfers between devices, local(): arrived = lax.all_to_all(packed, SEQ, 0, 0, tiled=True)  8.49 us
    all_to_all x1, starting transfers between devices, local(): columns = lax.all_to_all(own, ('dp_0', 'dp_2'), 0, 0, tiled=True)  6.95 us
    ppermute x3, waiting for transfers between devices, shift_y(): return lax.ppermute(x, ('dp_1', 'seq_1'), pairs)  5.93 us
  transfers between devices with their start and end apart: 30, of which 8 were waited for; matrix products, arithmetic and copies ran while one was open for 4% of the time, Pallas kernels for 18%

profile of v3, /device:TPU:1, one launch (start us, length us, event | category | flops | bytes accessed | tf_op | source)
XLA Modules:
  0.0 178.4 jit_solution(3253662418673381863)
XLA Ops:
  0.6 3.8 %pack.1 = bf16[8,272,512]{2,1,0:T(8,128)(2,1)} custom-call(bf16[256,2048]{1,0:T(8,128)(2,1)} %bitcast.10, bf16[256,1024]{1,0:T(8,128)(2,1)} %bitcast.11, bf16[256,1024]{1,0:T(8,128)(2,1)} %bitcast.12, s32[1,256]{1,0:T(1,128)} %seg_ref.1), custom_call_target="tpu_custom_call" | custom-call | bytes 6000000 | tf_op jit(solution)/shard_map/pack/pallas_call | solution.py:63
  4.5 8.5 %all-to-all-start = ((bf16[8,272,512]{2,1,0:T(8,128)(2,1)}), bf16[8,272,512]{2,1,0:T(8,128)(2,1)S(1)}, u32[]{:S(2)}, u32[]{:S(2)}) async-start(bf16[8,272,512]{2,1,0:T(8,128)(2,1)} %pack.1), calls=%async_computation | async-start | bytes 4456448 | tf_op jit(solution)/shard_map/all_to_all | solution.py:305
  13.0 1.2 collective-permute-start.10
  14.2 1.5 collective-permute-start.11
  15.6 26.3 %all-to-all-done.in_ref = bf16[8,272,512]{2,1,0:T(8,128)(2,1)S(1)} async-done(((bf16[8,272,512]{2,1,0:T(8,128)(2,1)}), bf16[8,272,512]{2,1,0:T(8,128)(2,1)S(1)}, u32[]{:S(2)}, u32[]{:S(2)}) %all-to-all-start) | async-done | bytes 2228256 | tf_op jit(solution)/shard_map/all_to_all | solution.py:305
  41.9 1.4 copy-done.4
  43.3 12.4 %attend.1 = bf16[8,256,256]{2,1,0:T(8,128)(2,1)} custom-call(bf16[8,272,512]{2,1,0:T(8,128)(2,1)} %copy-done.4), custom_call_target="tpu_custom_call" | custom-call | flops 10000000000 | bytes 4000000 | tf_op jit(solution)/shard_map/attend/pallas_call | solution.py:128
  55.7 4.4 %all-to-all-start.1 = ((bf16[8,256,256]{2,1,0:T(8,128)(2,1)}), bf16[8,256,256]{2,1,0:T(8,128)(2,1)}, u32[]{:S(2)}, u32[]{:S(2)}) async-start(bf16[8,256,256]{2,1,0:T(8,128)(2,1)} %attend.1), calls=%async_computation.1 | async-start | bytes 2097152 | tf_op jit(solution)/shard_map/all_to_all | solution.py:309
  60.1 0.5 collective-permute-start
  60.6 3.4 %collective-permute-start.1 = (bf16[16,2304]{1,0:T(8,128)(2,1)S(1)}, bf16[16,2304]{1,0:T(8,128)(2,1)S(1)}, u32[]{:S(2)}, u32[]{:S(2)}) collective-permute-start(bf16[16,2304]{1,0:T(8,128)(2,1)S(1)} %convert_element_type.3), channel_id=1, source_target_pairs={{0,1},{16,17},{1,0},{17,16},{2,3},{18,19},{3,2},{19,18},{4,5},{20,... | collective-permute-start | bytes 221192 | tf_op jit(solution)/shard_map/ppermute | solution.py:295
  64.1 1.1 collective-permute-start.2
  65.1 0.0 collective-permute-done.10.refs_1_
  65.2 3.7 %collective-permute-start.12 = (bf16[128,2304]{1,0:T(8,128)(2,1)S(1)}, bf16[128,2304]{1,0:T(8,128)(2,1)}, u32[]{:S(2)}, u32[]{:S(2)}) collective-permute-start(bf16[128,2304]{1,0:T(8,128)(2,1)S(1)} %slice.18), channel_id=1, source_target_pairs={{0,32},{32,64},{64,96},{96,0},{1,33},{33,65},{65,97},{97,1},{2,34}... | collective-permute-start | bytes 1769480 | tf_op jit(solution)/shard_map/ppermute | solution.py:272
  68.8 1.9 %slice.19 = bf16[128,2304]{1,0:T(8,128)(2,1)} slice(bf16[256,2304]{1,0:T(8,128)(2,1)} %collective-permute-done.11.refs_2_), slice={[128:256], [0:2304]} | slice | bytes 1179648 | tf_op jit(solution)/shard_map/slice | solution.py:282
  70.7 5.0 %collective-permute-done = bf16[16,2304]{1,0:T(8,128)(2,1)S(1)} collective-permute-done((bf16[16,2304]{1,0:T(8,128)(2,1)S(1)}, bf16[16,2304]{1,0:T(8,128)(2,1)S(1)}, u32[]{:S(2)}, u32[]{:S(2)}) %collective-permute-start) | collective-permute-done | bytes 73760 | tf_op jit(solution)/shard_map/ppermute | solution.py:295
  75.8 0.9 collective-permute-done.1
  76.7 2.3 %collective-permute-start.3 = (bf16[64,2304]{1,0:T(8,128)(2,1)S(1)}, bf16[64,2304]{1,0:T(8,128)(2,1)S(1)}, u32[]{:S(2)}, u32[]{:S(2)}) collective-permute-start(bf16[64,2304]{1,0:T(8,128)(2,1)S(1)} %pad_maximum_fusion.1), channel_id=1, source_target_pairs={{0,2},{2,4},{4,6},{6,0},{1,3},{3,5},{5,7},{7,1},{8,10},{10,12},{12... | collective-permute-start | bytes 884744 | tf_op jit(solution)/shard_map/ppermute | solution.py:272
  79.1 7.0 %all-to-all-start.2 = ((bf16[8,256,256]{2,1,0:T(8,128)(2,1)}), bf16[8,256,256]{2,1,0:T(8,128)(2,1)S(1)}, u32[]{:S(2)}, u32[]{:S(2)}) async-start(bf16[8,256,256]{2,1,0:T(8,128)(2,1)} %all-to-all-done.1), calls=%async_computation.2 | async-start | bytes 2097152 | tf_op jit(solution)/shard_map/all_to_all | solution.py:314
  86.0 2.4 %collective-permute-start.4 = (bf16[64,2304]{1,0:T(8,128)(2,1)S(1)}, bf16[64,2304]{1,0:T(8,128)(2,1)S(1)}, u32[]{:S(2)}, u32[]{:S(2)}) collective-permute-start(bf16[64,2304]{1,0:T(8,128)(2,1)S(1)} %pad_maximum_fusion.1), channel_id=1, source_target_pairs={{0,4},{2,6},{4,0},{6,2},{1,5},{3,7},{5,1},{7,3},{8,12},{10,14},{12... | collective-permute-start | bytes 884744 | tf_op jit(solution)/shard_map/ppermute | solution.py:272
  88.4 1.8 %collective-permute-start.5 = (bf16[64,2304]{1,0:T(8,128)(2,1)S(1)}, bf16[64,2304]{1,0:T(8,128)(2,1)S(1)}, u32[]{:S(2)}, u32[]{:S(2)}) collective-permute-start(bf16[64,2304]{1,0:T(8,128)(2,1)S(1)} %pad_maximum_fusion.1), channel_id=1, source_target_pairs={{0,6},{2,0},{4,2},{6,4},{1,7},{3,1},{5,3},{7,5},{8,14},{10,8},{12,... | collective-permute-start | bytes 884744 | tf_op jit(solution)/shard_map/ppermute | solution.py:272
  90.2 0.0 collective-permute-done.12.refs_3_
  90.2 0.6 collective-permute-start.15
  90.8 0.0 collective-permute-done.13.refs_4_
  90.8 0.3 collective-permute-start.16
  91.1 0.0 collective-permute-done.3
  91.1 0.2 collective-permute-start.14
  91.3 4.8 %collective-permute-done.4 = bf16[64,2304]{1,0:T(8,128)(2,1)S(1)} collective-permute-done((bf16[64,2304]{1,0:T(8,128)(2,1)S(1)}, bf16[64,2304]{1,0:T(8,128)(2,1)S(1)}, u32[]{:S(2)}, u32[]{:S(2)}) %collective-permute-start.4) | collective-permute-done | bytes 294944 | tf_op jit(solution)/shard_map/ppermute | solution.py:272
  96.1 0.8 collective-permute-start.17
  96.9 5.2 %collective-permute-done.5 = bf16[64,2304]{1,0:T(8,128)(2,1)S(1)} collective-permute-done((bf16[64,2304]{1,0:T(8,128)(2,1)S(1)}, bf16[64,2304]{1,0:T(8,128)(2,1)S(1)}, u32[]{:S(2)}, u32[]{:S(2)}) %collective-permute-start.5) | collective-permute-done | bytes 294944 | tf_op jit(solution)/shard_map/ppermute | solution.py:272
  102.2 0.8 collective-permute-start.18
  103.0 1.1 pad_maximum_fusion.refs_0_
  104.1 0.0 all-to-all-done.2.att_ref
  104.1 0.0 collective-permute-done.17.refs_8_
  104.1 2.7 %collective-permute-start.7 = (bf16[256,2304]{1,0:T(8,128)(2,1)S(1)}, bf16[256,2304]{1,0:T(8,128)(2,1)}, u32[]{:S(2)}, u32[]{:S(2)}) collective-permute-start(bf16[256,2304]{1,0:T(8,128)(2,1)S(1)} %pad_maximum_fusion.refs_0_), channel_id=1, source_target_pairs={{0,96},{32,0},{64,32},{96,64},{1,97},{33,1},{65,33},{97,65},{2,98}... | collective-permute-start | bytes 3538952 | tf_op jit(solution)/shard_map/ppermute | solution.py:272
  106.8 0.0 collective-permute-done.18.refs_9_
  106.8 0.0 collective-permute-start.6
  106.8 0.6 stack.23.me_ref
  107.5 8.5 %gradient_rows.1 = bf16[16,16,2304]{2,1,0:T(8,128)(2,1)} custom-call(s32[5]{0:T(128)} %stack.23.me_ref, bf16[8,256,256]{2,1,0:T(8,128)(2,1)} %copy-done.2, bf16[256,2304]{1,0:T(8,128)(2,1)} %bitcast.9.refs_0_, bf16[256,2304]{1,0:T(8,128)(2,1)} %copy-done.3, bf16[256,2304]{1,0:T(8,128)(2,1)} %collective-permute-done.11.refs_2_, ...), custom_call_target="tpu_custom_call" | custom-call | flops 2415919104 | bytes 12079595 | tf_op jit(solution)/shard_map/gradient_rows/pallas_call | solution.py:185
  116.0 4.1 %all-to-all-start.3 = ((bf16[16,16,2304]{2,1,0:T(8,128)(2,1)}), bf16[16,16,2304]{2,1,0:T(8,128)(2,1)S(1)}, u32[]{:S(2)}, u32[]{:S(2)}) async-start(bf16[16,16,2304]{2,1,0:T(8,128)(2,1)} %gradient_rows.1), calls=%async_computation.3 | async-start | bytes 2359296 | tf_op jit(solution)/shard_map/all_to_all | solution.py:323
  120.1 0.6 collective-permute-start.19
  120.8 11.4 %collective-permute-done.7.refs_2_ = bf16[256,2304]{1,0:T(8,128)(2,1)} collective-permute-done((bf16[256,2304]{1,0:T(8,128)(2,1)S(1)}, bf16[256,2304]{1,0:T(8,128)(2,1)}, u32[]{:S(2)}, u32[]{:S(2)}) %collective-permute-start.7) | collective-permute-done | bytes 1179680 | tf_op jit(solution)/shard_map/ppermute | solution.py:272
  132.2 1.9 %slice.17 = bf16[128,2304]{1,0:T(8,128)(2,1)} slice(bf16[256,2304]{1,0:T(8,128)(2,1)} %collective-permute-done.7.refs_2_), slice={[128:256], [0:2304]} | slice | bytes 1179648 | tf_op jit(solution)/shard_map/slice | solution.py:282
  134.1 3.5 %collective-permute-start.9 = (bf16[128,2304]{1,0:T(8,128)(2,1)}, bf16[128,2304]{1,0:T(8,128)(2,1)}, u32[]{:S(2)}, u32[]{:S(2)}) collective-permute-start(bf16[128,2304]{1,0:T(8,128)(2,1)} %slice.17), channel_id=1, source_target_pairs={{0,96},{32,0},{64,32},{96,64},{1,97},{33,1},{65,33},{97,65},{2,98}... | collective-permute-start | bytes 1769480 | tf_op jit(solution)/shard_map/ppermute | solution.py:272
  137.7 0.0 collective-permute-done.6.refs_1_
  137.7 1.9 %slice.16 = bf16[128,2304]{1,0:T(8,128)(2,1)} slice(bf16[256,2304]{1,0:T(8,128)(2,1)} %collective-permute-done.6.refs_1_), slice={[0:128], [0:2304]} | slice | bytes 1179648 | tf_op jit(solution)/shard_map/slice | solution.py:282
  139.6 1.1 collective-permute-start.21
  140.7 0.0 collective-permute-start.20
  140.7 0.0 all-to-all-done.3.parts_ref
  140.7 1.0 copy-done.1
  141.7 2.2 %total_rows.1 = (f32[16,2304]{1,0:T(8,128)}, f32[128,1,128]{2,1,0:T(1,128)}) custom-call(bf16[16,16,2304]{2,1,0:T(8,128)(2,1)} %copy-done.1), custom_call_target="tpu_custom_call" | custom-call | tf_op jit(solution)/shard_map/total_rows/pallas_call | solution.py:212
  143.9 5.9 %collective-permute-done.9.refs_4_ = bf16[128,2304]{1,0:T(8,128)(2,1)} collective-permute-done((bf16[128,2304]{1,0:T(8,128)(2,1)}, bf16[128,2304]{1,0:T(8,128)(2,1)}, u32[]{:S(2)}, u32[]{:S(2)}) %collective-permute-start.9) | collective-permute-done | bytes 589856 | tf_op jit(solution)/shard_map/ppermute | solution.py:272
  149.8 1.7 collective-permute-start.23
  151.5 3.3 %collective-permute-done.8.refs_3_ = bf16[128,2304]{1,0:T(8,128)(2,1)} collective-permute-done((bf16[128,2304]{1,0:T(8,128)(2,1)}, bf16[128,2304]{1,0:T(8,128)(2,1)}, u32[]{:S(2)}, u32[]{:S(2)}) %collective-permute-start.8) | collective-permute-done | bytes 589856 | tf_op jit(solution)/shard_map/ppermute | solution.py:272
  154.9 2.0 %collective-permute-start.22 = (bf16[128,2304]{1,0:T(8,128)(2,1)}, bf16[128,2304]{1,0:T(8,128)(2,1)S(1)}, u32[]{:S(2)}, u32[]{:S(2)}) collective-permute-start(bf16[128,2304]{1,0:T(8,128)(2,1)} %collective-permute-done.8.refs_3_), channel_id=1, source_target_pairs={{0,8},{8,0},{1,9},{9,1},{2,10},{10,2},{3,11},{11,3},{4,12},{12,4},... | collective-permute-start | bytes 1769480 | tf_op jit(solution)/shard_map/ppermute | solution.py:272
  156.8 0.0 collective-permute-done.19.refs_5_
  156.9 1.9 %collective-permute-start.24 = (f32[16,2304]{1,0:T(8,128)}, f32[16,2304]{1,0:T(8,128)S(1)}, u32[]{:S(2)}, u32[]{:S(2)}) collective-permute-start(f32[16,2304]{1,0:T(8,128)} %get-tuple-element.38), channel_id=1, source_target_pairs={{0,0},{8,16},{16,8},{24,24},{1,1},{9,17},{17,9},{25,25},{2,2},{10,... | collective-permute-start | bytes 442376 | tf_op jit(solution)/shard_map/ppermute | solution.py:326
  158.8 5.5 %all-to-all-start.4 = ((f32[128,1,128]{2,1,0:T(1,128)}), f32[128,1,128]{2,1,0:T(1,128)S(1)}, u32[]{:S(2)}, u32[]{:S(2)}) async-start(f32[128,1,128]{2,1,0:T(1,128)} %get-tuple-element.42), calls=%async_computation.4 | async-start | bytes 131072 | tf_op jit(solution)/shard_map/all_to_all | solution.py:327
  164.3 0.0 collective-permute-done.22.refs_8_
  164.3 0.8 copy-done.7
  165.1 0.2 copy-done.8
  165.3 8.7 %project.1 = bf16[1,256,2304]{2,1,0:T(8,128)(2,1)} custom-call(s32[5]{0:T(128)} %stack.23.me_ref, bf16[8,16,16,256]{3,2,1,0:T(8,128)(2,1)} %bitcast.8.att_ref, bf16[256,2304]{1,0:T(8,128)(2,1)} %copy-done, bf16[256,2304]{1,0:T(8,128)(2,1)} %collective-permute-done.6.refs_1_, bf16[256,2304]{1,0:T(8,128)(2,1)} %collective-permute-done.7.refs_2_, ...), custom_call_target="tpu_custom_call" | custom-call | flops 1000 | bytes 5 | tf_op jit(solution)/shard_map/project/pallas_call | solution.py:185
  174.1 0.6 copy-done.12
  174.7 0.6 copy-done.11
  175.4 3.0 %adam.1 = (f32[16,2304]{1,0:T(8,128)}, bf16[16,2304]{1,0:T(8,128)(2,1)}, f32[16,18]{1,0:T(8,128)}, bf16[16,2304]{1,0:T(8,128)(2,1)}, f32[16,18]{1,0:T(8,128)}) custom-call(f32[16,2304]{1,0:T(8,128)} %copy-done.12, f32[128,1,128]{2,1,0:T(1,128)} %copy-done.11, f32[16,2304]{1,0:T(8,128)} %weight_ref.1, bf16[16,2304]{1,0:T(8,128)(2,1)} %first_ref.1, ...), custom_call_target="tpu_custom_call" | custom-call | tf_op jit(solution)/shard_map/adam/pallas_call | solution.py:260
  (36 shorter events, 0.1 us)
Async XLA Ops:
  4.5 37.4 %all-to-all-start = ((bf16[8,272,512]{2,1,0:T(8,128)(2,1)}), bf16[8,272,512]{2,1,0:T(8,128)(2,1)S(1)}, u32[]{:S(2)}, u32[]{:S(2)}) async-start(bf16[8,272,512]{2,1,0:T(8,128)(2,1)} %pack.1), calls=%async_computation | async-start | bytes 4456448 | tf_op jit(solution)/shard_map/all_to_all | solution.py:305
  13.0 52.2 %collective-permute-start.10 = (bf16[256,2304]{1,0:T(8,128)(2,1)}, bf16[256,2304]{1,0:T(8,128)(2,1)S(1)}, u32[]{:S(2)}, u32[]{:S(2)}) collective-permute-start(bf16[256,2304]{1,0:T(8,128)(2,1)} %bitcast.9.refs_0_), channel_id=1, source_target_pairs={{0,32},{32,64},{64,96},{96,0},{1,33},{33,65},{65,97},{97,1},{2,34}... | collective-permute-start | bytes 3538952 | tf_op jit(solution)/shard_map/ppermute | solution.py:272
  14.2 54.7 %collective-permute-start.11 = (bf16[256,2304]{1,0:T(8,128)(2,1)}, bf16[256,2304]{1,0:T(8,128)(2,1)}, u32[]{:S(2)}, u32[]{:S(2)}) collective-permute-start(bf16[256,2304]{1,0:T(8,128)(2,1)} %bitcast.9.refs_0_), channel_id=1, source_target_pairs={{0,96},{32,0},{64,32},{96,64},{1,97},{33,1},{65,33},{97,65},{2,98}... | collective-permute-start | bytes 3538952 | tf_op jit(solution)/shard_map/ppermute | solution.py:272
  41.9 1.4 copy-start.4
  55.7 4.4 %copy-start.9 = (f32[16,2304]{1,0:T(8,128)S(1)}, f32[16,2304]{1,0:T(8,128)}, u32[]{:S(2)}) copy-start(f32[16,2304]{1,0:T(8,128)} %weight_ref.1) | copy-start | bytes 442372
  55.7 21.0 %all-to-all-start.1 = ((bf16[8,256,256]{2,1,0:T(8,128)(2,1)}), bf16[8,256,256]{2,1,0:T(8,128)(2,1)}, u32[]{:S(2)}, u32[]{:S(2)}) async-start(bf16[8,256,256]{2,1,0:T(8,128)(2,1)} %attend.1), calls=%async_computation.1 | async-start | bytes 2097152 | tf_op jit(solution)/shard_map/all_to_all | solution.py:309
  60.1 15.6 %collective-permute-start = (bf16[16,2304]{1,0:T(8,128)(2,1)S(1)}, bf16[16,2304]{1,0:T(8,128)(2,1)S(1)}, u32[]{:S(2)}, u32[]{:S(2)}) collective-permute-start(bf16[16,2304]{1,0:T(8,128)(2,1)S(1)} %convert_element_type.3), channel_id=1, source_target_pairs={{0,16},{16,1},{1,17},{17,0},{2,18},{18,3},{3,19},{19,2},{4,20},{20... | collective-permute-start | bytes 221192 | tf_op jit(solution)/shard_map/ppermute | solution.py:295
  60.6 16.0 %collective-permute-start.1 = (bf16[16,2304]{1,0:T(8,128)(2,1)S(1)}, bf16[16,2304]{1,0:T(8,128)(2,1)S(1)}, u32[]{:S(2)}, u32[]{:S(2)}) collective-permute-start(bf16[16,2304]{1,0:T(8,128)(2,1)S(1)} %convert_element_type.3), channel_id=1, source_target_pairs={{0,1},{16,17},{1,0},{17,16},{2,3},{18,19},{3,2},{19,18},{4,5},{20,... | collective-permute-start | bytes 221192 | tf_op jit(solution)/shard_map/ppermute | solution.py:295
  64.1 12.6 %collective-permute-start.2 = (bf16[16,2304]{1,0:T(8,128)(2,1)S(1)}, bf16[16,2304]{1,0:T(8,128)(2,1)S(1)}, u32[]{:S(2)}, u32[]{:S(2)}) collective-permute-start(bf16[16,2304]{1,0:T(8,128)(2,1)S(1)} %convert_element_type.3), channel_id=1, source_target_pairs={{0,17},{16,0},{1,16},{17,1},{2,19},{18,2},{3,18},{19,3},{4,21},{20... | collective-permute-start | bytes 221192 | tf_op jit(solution)/shard_map/ppermute | solution.py:295
  65.1 25.1 %copy-start.3 = (bf16[256,2304]{1,0:T(8,128)(2,1)}, bf16[256,2304]{1,0:T(8,128)(2,1)S(1)}, u32[]{:S(2)}) copy-start(bf16[256,2304]{1,0:T(8,128)(2,1)S(1)} %collective-permute-done.10.refs_1_) | copy-start | bytes 3538948
  65.2 25.1 %collective-permute-start.12 = (bf16[128,2304]{1,0:T(8,128)(2,1)S(1)}, bf16[128,2304]{1,0:T(8,128)(2,1)}, u32[]{:S(2)}, u32[]{:S(2)}) collective-permute-start(bf16[128,2304]{1,0:T(8,128)(2,1)S(1)} %slice.18), channel_id=1, source_target_pairs={{0,32},{32,64},{64,96},{96,0},{1,33},{33,65},{65,97},{97,1},{2,34}... | collective-permute-start | bytes 1769480 | tf_op jit(solution)/shard_map/ppermute | solution.py:272
  70.7 20.0 %collective-permute-start.13 = (bf16[128,2304]{1,0:T(8,128)(2,1)}, bf16[128,2304]{1,0:T(8,128)(2,1)}, u32[]{:S(2)}, u32[]{:S(2)}) collective-permute-start(bf16[128,2304]{1,0:T(8,128)(2,1)} %slice.19), channel_id=1, source_target_pairs={{0,96},{32,0},{64,32},{96,64},{1,97},{33,1},{65,33},{97,65},{2,98}... | collective-permute-start | bytes 1769480 | tf_op jit(solution)/shard_map/ppermute | solution.py:272
  76.7 25.5 %copy-start.6 = (bf16[64,2304]{1,0:T(8,128)(2,1)}, bf16[64,2304]{1,0:T(8,128)(2,1)S(1)}, u32[]{:S(2)}) copy-start(bf16[64,2304]{1,0:T(8,128)(2,1)S(1)} %pad_maximum_fusion.1) | copy-start | bytes 884740
  76.7 14.3 %collective-permute-start.3 = (bf16[64,2304]{1,0:T(8,128)(2,1)S(1)}, bf16[64,2304]{1,0:T(8,128)(2,1)S(1)}, u32[]{:S(2)}, u32[]{:S(2)}) collective-permute-start(bf16[64,2304]{1,0:T(8,128)(2,1)S(1)} %pad_maximum_fusion.1), channel_id=1, source_target_pairs={{0,2},{2,4},{4,6},{6,0},{1,3},{3,5},{5,7},{7,1},{8,10},{10,12},{12... | collective-permute-start | bytes 884744 | tf_op jit(solution)/shard_map/ppermute | solution.py:272
  79.1 25.1 %all-to-all-start.2 = ((bf16[8,256,256]{2,1,0:T(8,128)(2,1)}), bf16[8,256,256]{2,1,0:T(8,128)(2,1)S(1)}, u32[]{:S(2)}, u32[]{:S(2)}) async-start(bf16[8,256,256]{2,1,0:T(8,128)(2,1)} %all-to-all-done.1), calls=%async_computation.2 | async-start | bytes 2097152 | tf_op jit(solution)/shard_map/all_to_all | solution.py:314
  86.0 10.1 %collective-permute-start.4 = (bf16[64,2304]{1,0:T(8,128)(2,1)S(1)}, bf16[64,2304]{1,0:T(8,128)(2,1)S(1)}, u32[]{:S(2)}, u32[]{:S(2)}) collective-permute-start(bf16[64,2304]{1,0:T(8,128)(2,1)S(1)} %pad_maximum_fusion.1), channel_id=1, source_target_pairs={{0,4},{2,6},{4,0},{6,2},{1,5},{3,7},{5,1},{7,3},{8,12},{10,14},{12... | collective-permute-start | bytes 884744 | tf_op jit(solution)/shard_map/ppermute | solution.py:272
  88.4 13.8 %collective-permute-start.5 = (bf16[64,2304]{1,0:T(8,128)(2,1)S(1)}, bf16[64,2304]{1,0:T(8,128)(2,1)S(1)}, u32[]{:S(2)}, u32[]{:S(2)}) collective-permute-start(bf16[64,2304]{1,0:T(8,128)(2,1)S(1)} %pad_maximum_fusion.1), channel_id=1, source_target_pairs={{0,6},{2,0},{4,2},{6,4},{1,7},{3,1},{5,3},{7,5},{8,14},{10,8},{12,... | collective-permute-start | bytes 884744 | tf_op jit(solution)/shard_map/ppermute | solution.py:272
  90.2 17.2 %collective-permute-start.15 = (bf16[256,2304]{1,0:T(8,128)(2,1)S(1)}, bf16[256,2304]{1,0:T(8,128)(2,1)}, u32[]{:S(2)}, u32[]{:S(2)}) collective-permute-start(bf16[256,2304]{1,0:T(8,128)(2,1)S(1)} %collective-permute-done.10.refs_1_), channel_id=1, source_target_pairs={{0,8},{8,0},{1,9},{9,1},{2,10},{10,2},{3,11},{11,3},{4,12},{12,4},... | collective-permute-start | bytes 3538952 | tf_op jit(solution)/shard_map/ppermute | solution.py:272
  90.8 16.6 %collective-permute-start.16 = (bf16[256,2304]{1,0:T(8,128)(2,1)}, bf16[256,2304]{1,0:T(8,128)(2,1)}, u32[]{:S(2)}, u32[]{:S(2)}) collective-permute-start(bf16[256,2304]{1,0:T(8,128)(2,1)} %collective-permute-done.11.refs_2_), channel_id=1, source_target_pairs={{0,8},{8,0},{1,9},{9,1},{2,10},{10,2},{3,11},{11,3},{4,12},{12,4},... | collective-permute-start | bytes 3538952 | tf_op jit(solution)/shard_map/ppermute | solution.py:272
  91.1 11.1 %copy-start.10 = (bf16[64,2304]{1,0:T(8,128)(2,1)}, bf16[64,2304]{1,0:T(8,128)(2,1)S(1)}, u32[]{:S(2)}) copy-start(bf16[64,2304]{1,0:T(8,128)(2,1)S(1)} %collective-permute-done.3) | copy-start | bytes 884740
  91.1 16.4 %collective-permute-start.14 = (bf16[256,2304]{1,0:T(8,128)(2,1)}, bf16[256,2304]{1,0:T(8,128)(2,1)}, u32[]{:S(2)}, u32[]{:S(2)}) collective-permute-start(bf16[256,2304]{1,0:T(8,128)(2,1)} %bitcast.9.refs_0_), channel_id=1, source_target_pairs={{0,8},{8,0},{1,9},{9,1},{2,10},{10,2},{3,11},{11,3},{4,12},{12,4},... | collective-permute-start | bytes 3538952 | tf_op jit(solution)/shard_map/ppermute | solution.py:272
  96.1 8.0 %collective-permute-start.17 = (bf16[128,2304]{1,0:T(8,128)(2,1)}, bf16[128,2304]{1,0:T(8,128)(2,1)}, u32[]{:S(2)}, u32[]{:S(2)}) collective-permute-start(bf16[128,2304]{1,0:T(8,128)(2,1)} %collective-permute-done.12.refs_3_), channel_id=1, source_target_pairs={{0,8},{8,0},{1,9},{9,1},{2,10},{10,2},{3,11},{11,3},{4,12},{12,4},... | collective-permute-start | bytes 1769480 | tf_op jit(solution)/shard_map/ppermute | solution.py:272
  102.2 4.6 %collective-permute-start.18 = (bf16[128,2304]{1,0:T(8,128)(2,1)}, bf16[128,2304]{1,0:T(8,128)(2,1)}, u32[]{:S(2)}, u32[]{:S(2)}) collective-permute-start(bf16[128,2304]{1,0:T(8,128)(2,1)} %collective-permute-done.13.refs_4_), channel_id=1, source_target_pairs={{0,8},{8,0},{1,9},{9,1},{2,10},{10,2},{3,11},{11,3},{4,12},{12,4},... | collective-permute-start | bytes 1769480 | tf_op jit(solution)/shard_map/ppermute | solution.py:272
  104.1 16.0 %copy-start = (bf16[256,2304]{1,0:T(8,128)(2,1)}, bf16[256,2304]{1,0:T(8,128)(2,1)S(1)}, u32[]{:S(2)}) copy-start(bf16[256,2304]{1,0:T(8,128)(2,1)S(1)} %pad_maximum_fusion.refs_0_) | copy-start | bytes 3538948
  104.1 3.3 %copy-start.2 = (bf16[8,256,256]{2,1,0:T(8,128)(2,1)}, bf16[8,256,256]{2,1,0:T(8,128)(2,1)S(1)}, u32[]{:S(2)}) copy-start(bf16[8,256,256]{2,1,0:T(8,128)(2,1)S(1)} %all-to-all-done.2.att_ref) | copy-start | bytes 3145732
  104.1 28.1 %collective-permute-start.7 = (bf16[256,2304]{1,0:T(8,128)(2,1)S(1)}, bf16[256,2304]{1,0:T(8,128)(2,1)}, u32[]{:S(2)}, u32[]{:S(2)}) collective-permute-start(bf16[256,2304]{1,0:T(8,128)(2,1)S(1)} %pad_maximum_fusion.refs_0_), channel_id=1, source_target_pairs={{0,96},{32,0},{64,32},{96,64},{1,97},{33,1},{65,33},{97,65},{2,98}... | collective-permute-start | bytes 3538952 | tf_op jit(solution)/shard_map/ppermute | solution.py:272
  106.8 30.8 %collective-permute-start.6 = (bf16[256,2304]{1,0:T(8,128)(2,1)S(1)}, bf16[256,2304]{1,0:T(8,128)(2,1)}, u32[]{:S(2)}, u32[]{:S(2)}) collective-permute-start(bf16[256,2304]{1,0:T(8,128)(2,1)S(1)} %pad_maximum_fusion.refs_0_), channel_id=1, source_target_pairs={{0,32},{32,64},{64,96},{96,0},{1,33},{33,65},{65,97},{97,1},{2,34}... | collective-permute-start | bytes 3538952 | tf_op jit(solution)/shard_map/ppermute | solution.py:272
  116.0 24.7 %all-to-all-start.3 = ((bf16[16,16,2304]{2,1,0:T(8,128)(2,1)}), bf16[16,16,2304]{2,1,0:T(8,128)(2,1)S(1)}, u32[]{:S(2)}, u32[]{:S(2)}) async-start(bf16[16,16,2304]{2,1,0:T(8,128)(2,1)} %gradient_rows.1), calls=%async_computation.3 | async-start | bytes 2359296 | tf_op jit(solution)/shard_map/all_to_all | solution.py:323
  120.1 36.7 %collective-permute-start.19 = (bf16[256,2304]{1,0:T(8,128)(2,1)S(1)}, bf16[256,2304]{1,0:T(8,128)(2,1)S(1)}, u32[]{:S(2)}, u32[]{:S(2)}) collective-permute-start(bf16[256,2304]{1,0:T(8,128)(2,1)S(1)} %pad_maximum_fusion.refs_0_), channel_id=1, source_target_pairs={{0,8},{8,0},{1,9},{9,1},{2,10},{10,2},{3,11},{11,3},{4,12},{12,4},... | collective-permute-start | bytes 3538952 | tf_op jit(solution)/shard_map/ppermute | solution.py:272
  134.1 15.7 %collective-permute-start.9 = (bf16[128,2304]{1,0:T(8,128)(2,1)}, bf16[128,2304]{1,0:T(8,128)(2,1)}, u32[]{:S(2)}, u32[]{:S(2)}) collective-permute-start(bf16[128,2304]{1,0:T(8,128)(2,1)} %slice.17), channel_id=1, source_target_pairs={{0,96},{32,0},{64,32},{96,64},{1,97},{33,1},{65,33},{97,65},{2,98}... | collective-permute-start | bytes 1769480 | tf_op jit(solution)/shard_map/ppermute | solution.py:272
  139.6 15.3 %collective-permute-start.8 = (bf16[128,2304]{1,0:T(8,128)(2,1)}, bf16[128,2304]{1,0:T(8,128)(2,1)}, u32[]{:S(2)}, u32[]{:S(2)}) collective-permute-start(bf16[128,2304]{1,0:T(8,128)(2,1)} %slice.16), channel_id=1, source_target_pairs={{0,32},{32,64},{64,96},{96,0},{1,33},{33,65},{65,97},{97,1},{2,34}... | collective-permute-start | bytes 1769480 | tf_op jit(solution)/shard_map/ppermute | solution.py:272
  139.6 24.7 %collective-permute-start.21 = (bf16[256,2304]{1,0:T(8,128)(2,1)}, bf16[256,2304]{1,0:T(8,128)(2,1)}, u32[]{:S(2)}, u32[]{:S(2)}) collective-permute-start(bf16[256,2304]{1,0:T(8,128)(2,1)} %collective-permute-done.7.refs_2_), channel_id=1, source_target_pairs={{0,8},{8,0},{1,9},{9,1},{2,10},{10,2},{3,11},{11,3},{4,12},{12,4},... | collective-permute-start | bytes 3538952 | tf_op jit(solution)/shard_map/ppermute | solution.py:272
  140.7 23.6 %collective-permute-start.20 = (bf16[256,2304]{1,0:T(8,128)(2,1)}, bf16[256,2304]{1,0:T(8,128)(2,1)}, u32[]{:S(2)}, u32[]{:S(2)}) collective-permute-start(bf16[256,2304]{1,0:T(8,128)(2,1)} %collective-permute-done.6.refs_1_), channel_id=1, source_target_pairs={{0,8},{8,0},{1,9},{9,1},{2,10},{10,2},{3,11},{11,3},{4,12},{12,4},... | collective-permute-start | bytes 3538952 | tf_op jit(solution)/shard_map/ppermute | solution.py:272
  140.7 1.0 copy-start.1
  149.8 14.4 %collective-permute-start.23 = (bf16[128,2304]{1,0:T(8,128)(2,1)}, bf16[128,2304]{1,0:T(8,128)(2,1)S(1)}, u32[]{:S(2)}, u32[]{:S(2)}) collective-permute-start(bf16[128,2304]{1,0:T(8,128)(2,1)} %collective-permute-done.9.refs_4_), channel_id=1, source_target_pairs={{0,8},{8,0},{1,9},{9,1},{2,10},{10,2},{3,11},{11,3},{4,12},{12,4},... | collective-permute-start | bytes 1769480 | tf_op jit(solution)/shard_map/ppermute | solution.py:272
  154.9 9.4 %collective-permute-start.22 = (bf16[128,2304]{1,0:T(8,128)(2,1)}, bf16[128,2304]{1,0:T(8,128)(2,1)S(1)}, u32[]{:S(2)}, u32[]{:S(2)}) collective-permute-start(bf16[128,2304]{1,0:T(8,128)(2,1)} %collective-permute-done.8.refs_3_), channel_id=1, source_target_pairs={{0,8},{8,0},{1,9},{9,1},{2,10},{10,2},{3,11},{11,3},{4,12},{12,4},... | collective-permute-start | bytes 1769480 | tf_op jit(solution)/shard_map/ppermute | solution.py:272
  156.9 7.5 %copy-start.5 = (bf16[256,2304]{1,0:T(8,128)(2,1)}, bf16[256,2304]{1,0:T(8,128)(2,1)S(1)}, u32[]{:S(2)}) copy-start(bf16[256,2304]{1,0:T(8,128)(2,1)S(1)} %collective-permute-done.19.refs_5_) | copy-start | bytes 3538948
  156.9 17.2 %collective-permute-start.24 = (f32[16,2304]{1,0:T(8,128)}, f32[16,2304]{1,0:T(8,128)S(1)}, u32[]{:S(2)}, u32[]{:S(2)}) collective-permute-start(f32[16,2304]{1,0:T(8,128)} %get-tuple-element.38), channel_id=1, source_target_pairs={{0,0},{8,16},{16,8},{24,24},{1,1},{9,17},{17,9},{25,25},{2,2},{10,... | collective-permute-start | bytes 442376 | tf_op jit(solution)/shard_map/ppermute | solution.py:326
  158.8 15.3 %all-to-all-start.4 = ((f32[128,1,128]{2,1,0:T(1,128)}), f32[128,1,128]{2,1,0:T(1,128)S(1)}, u32[]{:S(2)}, u32[]{:S(2)}) async-start(f32[128,1,128]{2,1,0:T(1,128)} %get-tuple-element.42), calls=%async_computation.4 | async-start | bytes 131072 | tf_op jit(solution)/shard_map/all_to_all | solution.py:327
  164.3 0.8 copy-start.7
  164.3 1.1 copy-start.8
  174.1 0.7 copy-start.12
  174.7 0.6 copy-start.11

commit v4 on v3

--- a/solution.py
+++ b/solution.py
@@ -12,7 +12,7 @@
 TILE = 256
 BLOCKS = 8
 NOTE = 16
-WIDE = 768
+WIDE = 1152
 ORDER = (0, 1, 3, 2)
 SEQ = ("seq_0", "seq_1")
 DP = ("dp_0", "dp_1", "dp_2")
@@ -69,7 +69,7 @@
     )(q, k, v, seg)
 
 
-def attend_kernel(in_ref, out_ref, acc, total):
+def attend_kernel(in_ref, out_ref):
     notes = in_ref[:, TILE : TILE + 8, :].astype(F32).sum(axis=0)
     first_of_1 = jnp.max(notes[:, 0:128]).astype(jnp.int32)
     first_of_2 = jnp.max(notes[:, 256:384]).astype(jnp.int32)
@@ -79,49 +79,30 @@
             place < first_of_1, 0, jnp.where(place < first_of_2, first_of_1, first_of_2)
         )
 
-    key_row = lax.broadcasted_iota(jnp.int32, (TILE, 2 * TILE), 0)
-    lane = lax.broadcasted_iota(jnp.int32, (1, 2 * TILE), 1)
-    query_col = jnp.where(lane < TILE, lane, lane - TILE)
-
-    for i in range(BLOCKS):
+    def tile(i, low):
+        lane = lax.broadcasted_iota(jnp.int32, (1, 2 * TILE), 1)
+        place = jnp.where(lane < TILE, lane, lane - TILE) + i * TILE
+        seen = range(low, i + 1)
         query = jnp.concatenate([in_ref[i, :TILE, 0:128], in_ref[i, :TILE, 128:256]], axis=0)
-        start_row = first_seen(i * TILE + query_col)
-        start_low = first_seen(jnp.int32(i * TILE))
-        start_high = first_seen(jnp.int32(i * TILE + TILE - 1))
-        acc[...] = jnp.zeros_like(acc)
-        total[...] = jnp.zeros_like(total)
-
-        def step(j, mask, query=query):
-            key = in_ref[j, :TILE, 256:384]
-            value = in_ref[j, :TILE, 384:512]
-            scores = lax.dot_general(
-                key, query, (((1,), (1,)), ((), ())), preferred_element_type=F32
-            )
-            capped = jnp.tanh(scores * (score_scale / soft_cap))
-            weights = jnp.exp2(capped * (soft_cap * LOG2E))
-            if mask is not None:
-                weights = jnp.where(mask, weights, 0.0)
-            total[...] += weights.reshape(TILE // 8, 8, 2 * TILE).sum(axis=0)
-            acc[...] += lax.dot_general(
-                value, weights.astype(BF16), (((0,), (0,)), ((), ())), preferred_element_type=F32
-            )
-
-        low = start_low // TILE
-        clear = jnp.minimum((start_high + TILE - 1) // TILE, i)
-
-        @pl.loop(low, clear)
-        def _(j):
-            step(j, key_row + j * TILE >= start_row)
-
-        @pl.loop(clear, i)
-        def _(j):
-            step(j, None)
-
-        step(i, (key_row <= query_col) & (key_row + i * TILE >= start_row))
-
-        attended = (acc[...] / jnp.sum(total[...], axis=0, keepdims=True)).astype(BF16)
+        key = jnp.concatenate([in_ref[j, :TILE, 256:384] for j in seen], axis=0)
+        value = jnp.concatenate([in_ref[j, :TILE, 384:512] for j in seen], axis=0)
+        key_place = lax.broadcasted_iota(jnp.int32, (len(seen) * TILE, 2 * TILE), 0) + low * TILE
+        scores = lax.dot_general(key, query, (((1,), (1,)), ((), ())), preferred_element_type=F32)
+        capped = jnp.tanh(scores * (score_scale / soft_cap))
+        weights = jnp.exp2(capped * (soft_cap * LOG2E))
+        weights = jnp.where((key_place >= first_seen(place)) & (key_place <= place), weights, 0.0)
+        total = jnp.sum(weights, axis=0, keepdims=True)
+        mixed = lax.dot_general(
+            value, weights.astype(BF16), (((0,), (0,)), ((), ())), preferred_element_type=F32
+        )
+        attended = (mixed / total).astype(BF16)
         for c in range(2):
             out_ref[i, c * 128 : (c + 1) * 128] = attended[:, c * TILE : (c + 1) * TILE]
+
+    for i in range(BLOCKS):
+        first = first_seen(jnp.int32(i * TILE)) // TILE
+        for low in range(max(0, i - 5), i + 1):
+            pl.when(first == low)(lambda i=i, low=low: tile(i, low))
 
 
 def attend(packed):
@@ -130,7 +111,6 @@
         out_shape=jax.ShapeDtypeStruct((BLOCKS, 256, TILE), BF16),
         in_specs=[pl.BlockSpec(memory_space=pltpu.VMEM)],
         out_specs=pl.BlockSpec(memory_space=pltpu.VMEM),
-        scratch_shapes=[pltpu.VMEM((128, 2 * TILE), F32), pltpu.VMEM((8, 2 * TILE), F32)],
         compiler_params=params(),
         cost_estimate=pl.CostEstimate(
             flops=10_000_000_000, bytes_accessed=4_000_000, transcendentals=0
@@ -157,7 +137,7 @@
 
 
 def project_kernel(me_ref, att_ref, *refs):
-    rows, out_ref, left = refs[:10], refs[10], refs[11]
+    rows, out_ref, left = refs[:16], refs[16], refs[17]
     x, c, z = me_ref[0], me_ref[2], me_ref[3]
     y = me_ref[4] * 2 + me_ref[1]
 
@@ -263,6 +243,9 @@
             jax.ShapeDtypeStruct(a.shape, a.dtype) for a in (weight, first, fscale, second, sscale)
         ),
         compiler_params=params(),
+        cost_estimate=pl.CostEstimate(
+            flops=30_000_000_000, bytes_accessed=1_000_000, transcendentals=0
+        ),
         name="adam",
     )(grad, squares, weight, first, fscale, second, sscale)
 
@@ -313,27 +296,33 @@
 
     columns = lax.all_to_all(own, ("dp_0", "dp_2"), 0, 0, tiled=True)
     rows = after(rows, own)
-    rows = jnp.concatenate([rows] + [shift(rows, "seq_0", k) for k in (1, 2, 3)], axis=0)
+    rows = [rows] + [shift(rows, "seq_0", k) for k in (1, 2, 3)]
+    top, bottom = jnp.concatenate(rows[:2], axis=0), jnp.concatenate(rows[2:], axis=0)
 
     partial = over_columns(
         gradient_kernel, me, [columns], cots, (16, 16, WIDE), (16, 16, DO), "gradient_rows",
         2 * 256 * 2048 * DO,
     )
-    rows = from_ring(after(rows, columns))
+    top, bottom = after(top, columns), after(bottom, columns)
+    left_top, right_bottom = shift(top, "dp_0", 1), shift(bottom, "dp_0", -1)
+    far_top, far_bottom = shift(left_top, "dp_0", 1), shift(right_bottom, "dp_0", -1)
+    left_bottom = shift(after(bottom, partial), "dp_0", 1)
+    right_top = shift(after(top, partial), "dp_0", -1)
+    rows = [top, bottom, left_top, left_bottom, right_top, right_bottom, far_top, far_bottom]
     parts = lax.all_to_all(partial, ("dp_1", "seq_0", "seq_1"), 0, 0, tiled=True)
 
     sums, squares = total_rows(parts)
     grad = lax.ppermute(sums, ("dp_1", "dp_2"), [(0, 0), (1, 2), (2, 1), (3, 3)])
     squares = lax.all_to_all(squares, DP_SEQ, 0, 0, tiled=True)
     rows = rows + from_partner(
-        [after(a, partial) for a in rows[:3]] + [after(a, sums) for a in rows[3:]]
+        [after(a, partial if k in (0, 1, 2, 5) else squares) for k, a in enumerate(rows)]
     )
     layer_out = over_columns(
         project_kernel, me, [own.reshape(8, 16, 16, TILE)], rows,
         (1, TILE, WIDE), (1, TILE, DO), "project", 1000,
     )
     new_weight, new_first, new_fscale, new_second, new_sscale = adam(
-        after(grad, layer_out), squares, weight,
+        grad, squares, weight,
         first_moment, first_scale, second_moment, second_scale,
     )
     return (layer_out, new_weight, new_first, new_fscale, new_second, new_sscale)

time: 180 us -> 195 us (1.083)
  starting transfers between devices: 63.4 us -> 79.6 us
  local copies, waits for them, and re-layouts: 11.1 us -> 5.78 us
  waiting for transfers between devices: 63 us -> 68.2 us
  Pallas kernels: 38.8 us -> 34.7 us
  other arithmetic: 1.16 us -> 4.72 us
    all_to_all x1, waiting for transfers between devices: 0.01 us -> 9.81 us  [local(): squares = lax.all_to_all(squares, DP_SEQ, 0, 0, tiled=True)]
    ppermute x21 -> x26, starting transfers between devices: 27.1 us -> 35.3 us  [shift(): return lax.ppermute(x, axis, [(i, (i + by) % peers) for i in range(peers)])]
    ppermute x3, waiting for transfers between devices: 5.93 us -> 0.01 us  [shift_y(): return lax.ppermute(x, ('dp_1', 'seq_1'), pairs)]
    all_to_all x1, starting transfers between devices: 5.47 us -> 9.33 us  [local(): squares = lax.all_to_all(squares, DP_SEQ, 0, 0, tiled=True)]
    ppermute x1, starting transfers between devices: 1.91 us -> 5.11 us  [local(): lax.ppermute(sums, ('dp_1', 'dp_2'), [(0, 0), (1, 2), (2, 1), (3, 3)])]
    slice x2 -> x1, local copies, waits for them, and re-layouts: 3.84 us -> 0.91 us  [from_ring(): right[half:]]
    pallas_call x1, Pallas kernels: 12.4 us -> 9.68 us  [attend(): pl.pallas_call(attend_kernel, out_shape=jax.ShapeDtypeStruct((BLOCKS, 256...]
    ppermute x21 -> x26, waiting for transfers between devices: 30.8 us -> 32 us  [shift(): return lax.ppermute(x, axis, [(i, (i + by) % peers) for i in range(peers)])]
  transfers between devices with their start and end apart: 30 -> 35, of which waited for: 8 -> 12; matrix products, arithmetic and copies ran while one was open for 4% -> 3% of each run, Pallas kernels for 18% -> 12%
where the time goes in v4:
time: 195 us; the launch traced here: 194 us
  starting transfers between devices  79.6 us (41%)
  waiting for transfers between devices  68.2 us (35%)
  Pallas kernels  34.7 us (18%)
  local copies, waits for them, and re-layouts  5.78 us (3%)
  other arithmetic  4.72 us (2%)
    ppermute x26, starting transfers between devices, shift(): return lax.ppermute(x, axis, [(i, (i + by) % peers) for i in range(peers)])  35.3 us
    ppermute x26, waiting for transfers between devices, shift(): return lax.ppermute(x, axis, [(i, (i + by) % peers) for i in range(peers)])  32 us
    all_to_all x1, waiting for transfers between devices, local(): arrived = lax.all_to_all(packed, SEQ, 0, 0, tiled=True)  26.4 us
    pallas_call x2, Pallas kernels, over_columns(): pl.pallas_call(kernel, grid_spec=pltpu.PrefetchScalarGridSpec(num_scalar_...  15.9 us
    all_to_all x1, waiting for transfers between devices, local(): squares = lax.all_to_all(squares, DP_SEQ, 0, 0, tiled=True)  9.81 us
    pallas_call x1, Pallas kernels, attend(): pl.pallas_call(attend_kernel, out_shape=jax.ShapeDtypeStruct((BLOCKS, 256...  9.68 us
    all_to_all x1, starting transfers between devices, local(): squares = lax.all_to_all(squares, DP_SEQ, 0, 0, tiled=True)  9.33 us
    all_to_all x1, starting transfers between devices, local(): arrived = lax.all_to_all(packed, SEQ, 0, 0, tiled=True)  8.49 us
  transfers between devices with their start and end apart: 35, of which 12 were waited for; matrix products, arithmetic and copies ran while one was open for 3% of the time, Pallas kernels for 12%

profile of v4, /device:TPU:1, one launch (start us, length us, event | category | flops | bytes accessed | tf_op | source)
XLA Modules:
  0.0 194.1 jit_solution(4187363057972845468)
XLA Ops:
  0.6 3.8 %pack.1 = bf16[8,272,512]{2,1,0:T(8,128)(2,1)} custom-call(bf16[256,2048]{1,0:T(8,128)(2,1)} %bitcast.10, bf16[256,1024]{1,0:T(8,128)(2,1)} %bitcast.11, bf16[256,1024]{1,0:T(8,128)(2,1)} %bitcast.12, s32[1,256]{1,0:T(1,128)} %seg_ref.1), custom_call_target="tpu_custom_call" | custom-call | bytes 6000000 | tf_op jit(solution)/shard_map/pack/pallas_call | solution.py:63
  4.5 8.5 %all-to-all-start = ((bf16[8,272,512]{2,1,0:T(8,128)(2,1)}), bf16[8,272,512]{2,1,0:T(8,128)(2,1)}, u32[]{:S(2)}, u32[]{:S(2)}) async-start(bf16[8,272,512]{2,1,0:T(8,128)(2,1)} %pack.1), calls=%async_computation | async-start | bytes 4456448 | tf_op jit(solution)/shard_map/all_to_all | solution.py:288
  13.0 1.2 collective-permute-start.7
  14.2 1.5 collective-permute-start.8
  15.6 26.4 %all-to-all-done.in_ref = bf16[8,272,512]{2,1,0:T(8,128)(2,1)} async-done(((bf16[8,272,512]{2,1,0:T(8,128)(2,1)}), bf16[8,272,512]{2,1,0:T(8,128)(2,1)}, u32[]{:S(2)}, u32[]{:S(2)}) %all-to-all-start) | async-done | bytes 2228256 | tf_op jit(solution)/shard_map/all_to_all | solution.py:288
  42.0 9.7 %attend.1 = bf16[8,256,256]{2,1,0:T(8,128)(2,1)} custom-call(bf16[8,272,512]{2,1,0:T(8,128)(2,1)} %all-to-all-done.in_ref), custom_call_target="tpu_custom_call" | custom-call | flops 10000000000 | bytes 4000000 | tf_op jit(solution)/shard_map/attend/pallas_call | solution.py:109
  51.7 4.3 %all-to-all-start.1 = ((bf16[8,256,256]{2,1,0:T(8,128)(2,1)}), bf16[8,256,256]{2,1,0:T(8,128)(2,1)}, u32[]{:S(2)}, u32[]{:S(2)}) async-start(bf16[8,256,256]{2,1,0:T(8,128)(2,1)} %attend.1), calls=%async_computation.1 | async-start | bytes 2097152 | tf_op jit(solution)/shard_map/all_to_all | solution.py:292
  55.9 0.0 copy-start.13
  55.9 0.0 collective-permute-done.7.refs_1_
  56.0 0.0 copy-start.2
  56.0 1.6 collective-permute-start.9
  57.7 0.9 slice.9
  58.6 1.2 collective-permute-start.10
  59.8 0.1 collective-permute-start
  59.8 3.1 %collective-permute-start.1 = (bf16[16,2304]{1,0:T(8,128)(2,1)S(1)}, bf16[16,2304]{1,0:T(8,128)(2,1)}, u32[]{:S(2)}, u32[]{:S(2)}) collective-permute-start(bf16[16,2304]{1,0:T(8,128)(2,1)S(1)} %convert_element_type.3), channel_id=1, source_target_pairs={{0,1},{16,17},{1,0},{17,16},{2,3},{18,19},{3,2},{19,18},{4,5},{20,... | collective-permute-start | bytes 221192 | tf_op jit(solution)/shard_map/ppermute | solution.py:278
  62.9 1.8 collective-permute-start.2
  64.7 5.7 %collective-permute-done.9.refs_3_ = bf16[128,2304]{1,0:T(8,128)(2,1)} collective-permute-done((bf16[128,2304]{1,0:T(8,128)(2,1)S(1)}, bf16[128,2304]{1,0:T(8,128)(2,1)}, u32[]{:S(2)}, u32[]{:S(2)}) %collective-permute-start.9) | collective-permute-done | bytes 589856 | tf_op jit(solution)/shard_map/ppermute | solution.py:255
  70.4 2.7 %collective-permute-start.14 = (bf16[128,2304]{1,0:T(8,128)(2,1)}, bf16[128,2304]{1,0:T(8,128)(2,1)}, u32[]{:S(2)}, u32[]{:S(2)}) collective-permute-start(bf16[128,2304]{1,0:T(8,128)(2,1)} %collective-permute-done.9.refs_3_), channel_id=1, source_target_pairs={{0,8},{8,0},{1,9},{9,1},{2,10},{10,2},{3,11},{11,3},{4,12},{12,4},... | collective-permute-start | bytes 1769480 | tf_op jit(solution)/shard_map/ppermute | solution.py:255
  73.2 6.7 %all-to-all-start.2 = ((bf16[8,256,256]{2,1,0:T(8,128)(2,1)}), bf16[8,256,256]{2,1,0:T(8,128)(2,1)S(1)}, u32[]{:S(2)}, u32[]{:S(2)}) async-start(bf16[8,256,256]{2,1,0:T(8,128)(2,1)} %all-to-all-done.1), calls=%async_computation.2 | async-start | bytes 2097152 | tf_op jit(solution)/shard_map/all_to_all | solution.py:297
  79.8 0.1 collective-permute-start.12
  79.9 0.5 collective-permute-start.13
  80.4 0.1 collective-permute-start.11
  80.5 1.6 pad_maximum_fusion.2
  82.2 0.6 collective-permute-start.4
  82.7 0.9 collective-permute-start.5
  83.6 8.6 %collective-permute-done.4 = bf16[64,2304]{1,0:T(8,128)(2,1)} collective-permute-done((bf16[64,2304]{1,0:T(8,128)(2,1)}, bf16[64,2304]{1,0:T(8,128)(2,1)}, u32[]{:S(2)}, u32[]{:S(2)}) %collective-permute-start.4) | collective-permute-done | bytes 294944 | tf_op jit(solution)/shard_map/ppermute | solution.py:255
  92.2 1.2 collective-permute-start.15
  93.4 0.6 stack.23.me_ref
  94.0 2.7 %collective-permute-done.5 = bf16[64,2304]{1,0:T(8,128)(2,1)} collective-permute-done((bf16[64,2304]{1,0:T(8,128)(2,1)}, bf16[64,2304]{1,0:T(8,128)(2,1)}, u32[]{:S(2)}, u32[]{:S(2)}) %collective-permute-start.5) | collective-permute-done | bytes 294944 | tf_op jit(solution)/shard_map/ppermute | solution.py:255
  96.7 1.6 collective-permute-start.3
  98.3 2.0 %pad_maximum_fusion.1.refs_1_ = bf16[128,2304]{1,0:T(8,128)(2,1)} fusion(bf16[64,2304]{1,0:T(8,128)(2,1)} %collective-permute-done.5, bf16[64,2304]{1,0:T(8,128)(2,1)} %collective-permute-done.4), kind=kLoop, calls=%fused_computation.1 | loop fusion | flops 1179648 | bytes 1179648 | tf_op jit(solution)/shard_map/concatenate | solution.py:300
  100.3 1.1 copy-done.1
  101.4 8.2 %gradient_rows.1 = bf16[16,16,2304]{2,1,0:T(8,128)(2,1)} custom-call(s32[5]{0:T(128)} %stack.23.me_ref, bf16[8,256,256]{2,1,0:T(8,128)(2,1)} %copy-done.1, bf16[256,2304]{1,0:T(8,128)(2,1)} %bitcast.9.refs_0_, bf16[256,2304]{1,0:T(8,128)(2,1)} %copy-done.2, bf16[256,2304]{1,0:T(8,128)(2,1)} %copy-done.3, bf16[128,2304]{1,0:T(8,128)(2,1)} %collective-permute-done.9.refs_3_, ...), custom_call_target="tpu_custom_call" | custom-call | flops 2415919104 | bytes 12079595 | tf_op jit(solution)/shard_map/gradient_rows/pallas_call | solution.py:165
  109.6 5.5 %all-to-all-start.3 = ((bf16[16,16,2304]{2,1,0:T(8,128)(2,1)}), bf16[16,16,2304]{2,1,0:T(8,128)(2,1)S(1)}, u32[]{:S(2)}, u32[]{:S(2)}) async-start(bf16[16,16,2304]{2,1,0:T(8,128)(2,1)} %gradient_rows.1), calls=%async_computation.3 | async-start | bytes 2359296 | tf_op jit(solution)/shard_map/all_to_all | solution.py:312
  115.1 2.9 %collective-permute-start.18 = (bf16[128,2304]{1,0:T(8,128)(2,1)S(1)}, bf16[128,2304]{1,0:T(8,128)(2,1)S(1)}, u32[]{:S(2)}, u32[]{:S(2)}) collective-permute-start(bf16[128,2304]{1,0:T(8,128)(2,1)S(1)} %copy-done.4), channel_id=1, source_target_pairs={{0,96},{32,0},{64,32},{96,64},{1,97},{33,1},{65,33},{97,65},{2,98}... | collective-permute-start | bytes 1769480 | tf_op jit(solution)/shard_map/ppermute | solution.py:255
  118.0 1.1 pad_maximum_fusion.refs_0_
  119.1 0.1 collective-permute-start.6
  119.2 2.7 %collective-permute-start.17 = (bf16[128,2304]{1,0:T(8,128)(2,1)S(1)}, bf16[128,2304]{1,0:T(8,128)(2,1)S(1)}, u32[]{:S(2)}, u32[]{:S(2)}) collective-permute-start(bf16[128,2304]{1,0:T(8,128)(2,1)S(1)} %pad_maximum_fusion.refs_0_), channel_id=1, source_target_pairs={{0,96},{32,0},{64,32},{96,64},{1,97},{33,1},{65,33},{97,65},{2,98}... | collective-permute-start | bytes 1769480 | tf_op jit(solution)/shard_map/ppermute | solution.py:255
  121.9 7.7 %collective-permute-done.18.refs_5_ = bf16[128,2304]{1,0:T(8,128)(2,1)S(1)} collective-permute-done((bf16[128,2304]{1,0:T(8,128)(2,1)S(1)}, bf16[128,2304]{1,0:T(8,128)(2,1)S(1)}, u32[]{:S(2)}, u32[]{:S(2)}) %collective-permute-start.18) | collective-permute-done | bytes 589856 | tf_op jit(solution)/shard_map/ppermute | solution.py:255
  129.6 3.4 %collective-permute-start.20 = (bf16[128,2304]{1,0:T(8,128)(2,1)S(1)}, bf16[128,2304]{1,0:T(8,128)(2,1)}, u32[]{:S(2)}, u32[]{:S(2)}) collective-permute-start(bf16[128,2304]{1,0:T(8,128)(2,1)S(1)} %collective-permute-done.18.refs_5_), channel_id=1, source_target_pairs={{0,96},{32,0},{64,32},{96,64},{1,97},{33,1},{65,33},{97,65},{2,98}... | collective-permute-start | bytes 1769480 | tf_op jit(solution)/shard_map/ppermute | solution.py:255
  133.0 0.9 collective-permute-done.6.refs_2_
  133.9 4.1 %collective-permute-start.21 = (bf16[128,2304]{1,0:T(8,128)(2,1)S(1)}, bf16[128,2304]{1,0:T(8,128)(2,1)}, u32[]{:S(2)}, u32[]{:S(2)}) collective-permute-start(bf16[128,2304]{1,0:T(8,128)(2,1)S(1)} %pad_maximum_fusion.refs_0_), channel_id=1, source_target_pairs={{0,8},{8,0},{1,9},{9,1},{2,10},{10,2},{3,11},{11,3},{4,12},{12,4},... | collective-permute-start | bytes 1769480 | tf_op jit(solution)/shard_map/ppermute | solution.py:255
  138.0 4.2 %collective-permute-done.17.refs_4_ = bf16[128,2304]{1,0:T(8,128)(2,1)S(1)} collective-permute-done((bf16[128,2304]{1,0:T(8,128)(2,1)S(1)}, bf16[128,2304]{1,0:T(8,128)(2,1)S(1)}, u32[]{:S(2)}, u32[]{:S(2)}) %collective-permute-start.17) | collective-permute-done | bytes 589856 | tf_op jit(solution)/shard_map/ppermute | solution.py:255
  142.2 3.5 %collective-permute-start.22 = (bf16[128,2304]{1,0:T(8,128)(2,1)S(1)}, bf16[128,2304]{1,0:T(8,128)(2,1)}, u32[]{:S(2)}, u32[]{:S(2)}) collective-permute-start(bf16[128,2304]{1,0:T(8,128)(2,1)S(1)} %copy-done.4), channel_id=1, source_target_pairs={{0,8},{8,0},{1,9},{9,1},{2,10},{10,2},{3,11},{11,3},{4,12},{12,4},... | collective-permute-start | bytes 1769480 | tf_op jit(solution)/shard_map/ppermute | solution.py:255
  145.8 0.8 collective-permute-done.16.refs_3_
  146.5 0.8 copy-done.9
  147.4 4.1 %collective-permute-start.26 = (bf16[128,2304]{1,0:T(8,128)(2,1)S(1)}, bf16[128,2304]{1,0:T(8,128)(2,1)}, u32[]{:S(2)}, u32[]{:S(2)}) collective-permute-start(bf16[128,2304]{1,0:T(8,128)(2,1)S(1)} %collective-permute-done.18.refs_5_), channel_id=1, source_target_pairs={{0,8},{8,0},{1,9},{9,1},{2,10},{10,2},{3,11},{11,3},{4,12},{12,4},... | collective-permute-start | bytes 1769480 | tf_op jit(solution)/shard_map/ppermute | solution.py:255
  151.5 1.0 copy-done
  152.5 2.2 %total_rows.1 = (f32[16,2304]{1,0:T(8,128)}, f32[128,1,128]{2,1,0:T(1,128)}) custom-call(bf16[16,16,2304]{2,1,0:T(8,128)(2,1)} %copy-done), custom_call_target="tpu_custom_call" | custom-call | tf_op jit(solution)/shard_map/total_rows/pallas_call | solution.py:192
  154.7 0.1 collective-permute-done.20.refs_7_
  154.9 5.1 %collective-permute-start.29 = (f32[16,2304]{1,0:T(8,128)}, f32[16,2304]{1,0:T(8,128)}, u32[]{:S(2)}, u32[]{:S(2)}) collective-permute-start(f32[16,2304]{1,0:T(8,128)} %get-tuple-element.48), channel_id=1, source_target_pairs={{0,0},{8,16},{16,8},{24,24},{1,1},{9,17},{17,9},{25,25},{2,2},{10,... | collective-permute-start | bytes 442376 | tf_op jit(solution)/shard_map/ppermute | solution.py:315
  160.0 9.3 %all-to-all-start.4 = ((f32[128,1,128]{2,1,0:T(1,128)}), f32[128,1,128]{2,1,0:T(1,128)S(1)}, u32[]{:S(2)}, u32[]{:S(2)}) async-start(f32[128,1,128]{2,1,0:T(1,128)} %get-tuple-element.42), calls=%async_computation.4 | async-start | bytes 131072 | tf_op jit(solution)/shard_map/all_to_all | solution.py:316
  169.3 9.8 %all-to-all-done.4.squares_ref = f32[128,1,128]{2,1,0:T(1,128)S(1)} async-done(((f32[128,1,128]{2,1,0:T(1,128)}), f32[128,1,128]{2,1,0:T(1,128)S(1)}, u32[]{:S(2)}, u32[]{:S(2)}) %all-to-all-start.4) | async-done | bytes 65568 | tf_op jit(solution)/shard_map/all_to_all | solution.py:316
  179.2 0.6 copy-done.14
  179.8 0.4 collective-permute-start.23
  180.2 0.1 collective-permute-start.25
  180.3 0.4 collective-permute-start.24
  180.7 0.1 collective-permute-start.28
  180.8 0.4 collective-permute-start.27
  181.2 3.0 %adam.1 = (f32[16,2304]{1,0:T(8,128)}, bf16[16,2304]{1,0:T(8,128)(2,1)}, f32[16,18]{1,0:T(8,128)}, bf16[16,2304]{1,0:T(8,128)(2,1)}, f32[16,18]{1,0:T(8,128)}) custom-call(f32[16,2304]{1,0:T(8,128)} %collective-permute-done.29.grad_ref, f32[128,1,128]{2,1,0:T(1,128)} %copy-done.14, f32[16,2304]{1,0:T(8,128)} %weight_ref.1, bf16[16,2304]{1,0:T(8,128)(2,1)} %first_ref.1, ...), custom_call_target="tpu_custom_call" | custom-call | flops 30000001024 | bytes 1000000 | tf_op jit(solution)/shard_map/adam/pallas_call | solution.py:240
  184.3 1.1 collective-permute-done.24.refs_11_
  185.4 0.1 collective-permute-done.27.refs_14_
  185.5 0.7 copy-done.12
  186.2 7.7 %project.1 = bf16[1,256,2304]{2,1,0:T(8,128)(2,1)} custom-call(s32[5]{0:T(128)} %stack.23.me_ref, bf16[8,16,16,256]{3,2,1,0:T(8,128)(2,1)} %bitcast.8.att_ref, bf16[128,2304]{1,0:T(8,128)(2,1)} %copy-done.5, bf16[128,2304]{1,0:T(8,128)(2,1)} %pad_maximum_fusion.1.refs_1_, bf16[128,2304]{1,0:T(8,128)(2,1)} %copy-done.7, bf16[128,2304]{1,0:T(8,128)(2,1)} %copy-done.9, ...), custom_call_target="tpu_custom_call" | custom-call | flops 1000 | bytes 5 | tf_op jit(solution)/shard_map/project/pallas_call | solution.py:165
  (49 shorter events, 0.2 us)
Async XLA Ops:
  4.5 37.5 %all-to-all-start = ((bf16[8,272,512]{2,1,0:T(8,128)(2,1)}), bf16[8,272,512]{2,1,0:T(8,128)(2,1)}, u32[]{:S(2)}, u32[]{:S(2)}) async-start(bf16[8,272,512]{2,1,0:T(8,128)(2,1)} %pack.1), calls=%async_computation | async-start | bytes 4456448 | tf_op jit(solution)/shard_map/all_to_all | solution.py:288
  13.0 43.0 %collective-permute-start.7 = (bf16[256,2304]{1,0:T(8,128)(2,1)}, bf16[256,2304]{1,0:T(8,128)(2,1)S(1)}, u32[]{:S(2)}, u32[]{:S(2)}) collective-permute-start(bf16[256,2304]{1,0:T(8,128)(2,1)} %bitcast.9.refs_0_), channel_id=1, source_target_pairs={{0,32},{32,64},{64,96},{96,0},{1,33},{33,65},{65,97},{97,1},{2,34}... | collective-permute-start | bytes 3538952 | tf_op jit(solution)/shard_map/ppermute | solution.py:255
  14.2 43.5 %collective-permute-start.8 = (bf16[256,2304]{1,0:T(8,128)(2,1)}, bf16[256,2304]{1,0:T(8,128)(2,1)S(1)}, u32[]{:S(2)}, u32[]{:S(2)}) collective-permute-start(bf16[256,2304]{1,0:T(8,128)(2,1)} %bitcast.9.refs_0_), channel_id=1, source_target_pairs={{0,96},{32,0},{64,32},{96,64},{1,97},{33,1},{65,33},{97,65},{2,98}... | collective-permute-start | bytes 3538952 | tf_op jit(solution)/shard_map/ppermute | solution.py:255
  51.7 21.5 %all-to-all-start.1 = ((bf16[8,256,256]{2,1,0:T(8,128)(2,1)}), bf16[8,256,256]{2,1,0:T(8,128)(2,1)}, u32[]{:S(2)}, u32[]{:S(2)}) async-start(bf16[8,256,256]{2,1,0:T(8,128)(2,1)} %attend.1), calls=%async_computation.1 | async-start | bytes 2097152 | tf_op jit(solution)/shard_map/all_to_all | solution.py:292
  55.9 3.8 %copy-start.13 = (f32[16,2304]{1,0:T(8,128)S(1)}, f32[16,2304]{1,0:T(8,128)}, u32[]{:S(2)}) copy-start(f32[16,2304]{1,0:T(8,128)} %weight_ref.1) | copy-start | bytes 442372
  56.0 23.9 %copy-start.2 = (bf16[256,2304]{1,0:T(8,128)(2,1)}, bf16[256,2304]{1,0:T(8,128)(2,1)S(1)}, u32[]{:S(2)}) copy-start(bf16[256,2304]{1,0:T(8,128)(2,1)S(1)} %collective-permute-done.7.refs_1_) | copy-start | bytes 3538948
  56.0 14.4 %collective-permute-start.9 = (bf16[128,2304]{1,0:T(8,128)(2,1)S(1)}, bf16[128,2304]{1,0:T(8,128)(2,1)}, u32[]{:S(2)}, u32[]{:S(2)}) collective-permute-start(bf16[128,2304]{1,0:T(8,128)(2,1)S(1)} %slice.8), channel_id=1, source_target_pairs={{0,32},{32,64},{64,96},{96,0},{1,33},{33,65},{65,97},{97,1},{2,34}... | collective-permute-start | bytes 1769480 | tf_op jit(solution)/shard_map/ppermute | solution.py:255
  57.7 22.3 %copy-start.3 = (bf16[256,2304]{1,0:T(8,128)(2,1)}, bf16[256,2304]{1,0:T(8,128)(2,1)S(1)}, u32[]{:S(2)}) copy-start(bf16[256,2304]{1,0:T(8,128)(2,1)S(1)} %collective-permute-done.8.refs_2_) | copy-start | bytes 3538948
  58.6 23.6 %collective-permute-start.10 = (bf16[128,2304]{1,0:T(8,128)(2,1)}, bf16[128,2304]{1,0:T(8,128)(2,1)}, u32[]{:S(2)}, u32[]{:S(2)}) collective-permute-start(bf16[128,2304]{1,0:T(8,128)(2,1)} %slice.9), channel_id=1, source_target_pairs={{0,96},{32,0},{64,32},{96,64},{1,97},{33,1},{65,33},{97,65},{2,98}... | collective-permute-start | bytes 1769480 | tf_op jit(solution)/shard_map/ppermute | solution.py:255
  59.8 20.1 %collective-permute-start = (bf16[16,2304]{1,0:T(8,128)(2,1)S(1)}, bf16[16,2304]{1,0:T(8,128)(2,1)S(1)}, u32[]{:S(2)}, u32[]{:S(2)}) collective-permute-start(bf16[16,2304]{1,0:T(8,128)(2,1)S(1)} %convert_element_type.3), channel_id=1, source_target_pairs={{0,16},{16,1},{1,17},{17,0},{2,18},{18,3},{3,19},{19,2},{4,20},{20... | collective-permute-start | bytes 221192 | tf_op jit(solution)/shard_map/ppermute | solution.py:278
  59.8 20.1 %collective-permute-start.1 = (bf16[16,2304]{1,0:T(8,128)(2,1)S(1)}, bf16[16,2304]{1,0:T(8,128)(2,1)}, u32[]{:S(2)}, u32[]{:S(2)}) collective-permute-start(bf16[16,2304]{1,0:T(8,128)(2,1)S(1)} %convert_element_type.3), channel_id=1, source_target_pairs={{0,1},{16,17},{1,0},{17,16},{2,3},{18,19},{3,2},{19,18},{4,5},{20,... | collective-permute-start | bytes 221192 | tf_op jit(solution)/shard_map/ppermute | solution.py:278
  62.9 17.5 %collective-permute-start.2 = (bf16[16,2304]{1,0:T(8,128)(2,1)S(1)}, bf16[16,2304]{1,0:T(8,128)(2,1)}, u32[]{:S(2)}, u32[]{:S(2)}) collective-permute-start(bf16[16,2304]{1,0:T(8,128)(2,1)S(1)} %convert_element_type.3), channel_id=1, source_target_pairs={{0,17},{16,0},{1,16},{17,1},{2,19},{18,2},{3,18},{19,3},{4,21},{20... | collective-permute-start | bytes 221192 | tf_op jit(solution)/shard_map/ppermute | solution.py:278
  70.4 12.3 %collective-permute-start.14 = (bf16[128,2304]{1,0:T(8,128)(2,1)}, bf16[128,2304]{1,0:T(8,128)(2,1)}, u32[]{:S(2)}, u32[]{:S(2)}) collective-permute-start(bf16[128,2304]{1,0:T(8,128)(2,1)} %collective-permute-done.9.refs_3_), channel_id=1, source_target_pairs={{0,8},{8,0},{1,9},{9,1},{2,10},{10,2},{3,11},{11,3},{4,12},{12,4},... | collective-permute-start | bytes 1769480 | tf_op jit(solution)/shard_map/ppermute | solution.py:255
  73.2 27.1 %all-to-all-start.2 = ((bf16[8,256,256]{2,1,0:T(8,128)(2,1)}), bf16[8,256,256]{2,1,0:T(8,128)(2,1)S(1)}, u32[]{:S(2)}, u32[]{:S(2)}) async-start(bf16[8,256,256]{2,1,0:T(8,128)(2,1)} %all-to-all-done.1), calls=%async_computation.2 | async-start | bytes 2097152 | tf_op jit(solution)/shard_map/all_to_all | solution.py:297
  79.8 20.4 %collective-permute-start.12 = (bf16[256,2304]{1,0:T(8,128)(2,1)S(1)}, bf16[256,2304]{1,0:T(8,128)(2,1)}, u32[]{:S(2)}, u32[]{:S(2)}) collective-permute-start(bf16[256,2304]{1,0:T(8,128)(2,1)S(1)} %collective-permute-done.7.refs_1_), channel_id=1, source_target_pairs={{0,8},{8,0},{1,9},{9,1},{2,10},{10,2},{3,11},{11,3},{4,12},{12,4},... | collective-permute-start | bytes 3538952 | tf_op jit(solution)/shard_map/ppermute | solution.py:255
  79.9 20.3 %collective-permute-start.13 = (bf16[256,2304]{1,0:T(8,128)(2,1)S(1)}, bf16[256,2304]{1,0:T(8,128)(2,1)}, u32[]{:S(2)}, u32[]{:S(2)}) collective-permute-start(bf16[256,2304]{1,0:T(8,128)(2,1)S(1)} %collective-permute-done.8.refs_2_), channel_id=1, source_target_pairs={{0,8},{8,0},{1,9},{9,1},{2,10},{10,2},{3,11},{11,3},{4,12},{12,4},... | collective-permute-start | bytes 3538952 | tf_op jit(solution)/shard_map/ppermute | solution.py:255
  80.4 19.9 %collective-permute-start.11 = (bf16[256,2304]{1,0:T(8,128)(2,1)}, bf16[256,2304]{1,0:T(8,128)(2,1)}, u32[]{:S(2)}, u32[]{:S(2)}) collective-permute-start(bf16[256,2304]{1,0:T(8,128)(2,1)} %bitcast.9.refs_0_), channel_id=1, source_target_pairs={{0,8},{8,0},{1,9},{9,1},{2,10},{10,2},{3,11},{11,3},{4,12},{12,4},... | collective-permute-start | bytes 3538952 | tf_op jit(solution)/shard_map/ppermute | solution.py:255
  82.2 10.0 %collective-permute-start.4 = (bf16[64,2304]{1,0:T(8,128)(2,1)}, bf16[64,2304]{1,0:T(8,128)(2,1)}, u32[]{:S(2)}, u32[]{:S(2)}) collective-permute-start(bf16[64,2304]{1,0:T(8,128)(2,1)} %pad_maximum_fusion.2), channel_id=1, source_target_pairs={{0,4},{2,6},{4,0},{6,2},{1,5},{3,7},{5,1},{7,3},{8,12},{10,14},{12... | collective-permute-start | bytes 884744 | tf_op jit(solution)/shard_map/ppermute | solution.py:255
  82.7 14.0 %collective-permute-start.5 = (bf16[64,2304]{1,0:T(8,128)(2,1)}, bf16[64,2304]{1,0:T(8,128)(2,1)}, u32[]{:S(2)}, u32[]{:S(2)}) collective-permute-start(bf16[64,2304]{1,0:T(8,128)(2,1)} %pad_maximum_fusion.2), channel_id=1, source_target_pairs={{0,6},{2,0},{4,2},{6,4},{1,7},{3,1},{5,3},{7,5},{8,14},{10,8},{12,... | collective-permute-start | bytes 884744 | tf_op jit(solution)/shard_map/ppermute | solution.py:255
  92.2 8.1 %collective-permute-start.15 = (bf16[128,2304]{1,0:T(8,128)(2,1)}, bf16[128,2304]{1,0:T(8,128)(2,1)}, u32[]{:S(2)}, u32[]{:S(2)}) collective-permute-start(bf16[128,2304]{1,0:T(8,128)(2,1)} %collective-permute-done.10.refs_4_), channel_id=1, source_target_pairs={{0,8},{8,0},{1,9},{9,1},{2,10},{10,2},{3,11},{11,3},{4,12},{12,4},... | collective-permute-start | bytes 1769480 | tf_op jit(solution)/shard_map/ppermute | solution.py:255
  96.7 21.3 %collective-permute-start.3 = (bf16[64,2304]{1,0:T(8,128)(2,1)}, bf16[64,2304]{1,0:T(8,128)(2,1)}, u32[]{:S(2)}, u32[]{:S(2)}) collective-permute-start(bf16[64,2304]{1,0:T(8,128)(2,1)} %pad_maximum_fusion.2), channel_id=1, source_target_pairs={{0,2},{2,4},{4,6},{6,0},{1,3},{3,5},{5,7},{7,1},{8,10},{10,12},{12... | collective-permute-start | bytes 884744 | tf_op jit(solution)/shard_map/ppermute | solution.py:255
  100.3 1.1 copy-start.1
  109.6 5.5 %copy-start.4 = (bf16[128,2304]{1,0:T(8,128)(2,1)S(1)}, bf16[128,2304]{1,0:T(8,128)(2,1)}, u32[]{:S(2)}) copy-start(bf16[128,2304]{1,0:T(8,128)(2,1)} %pad_maximum_fusion.1.refs_1_) | copy-start | bytes 1769476
  109.6 41.9 %all-to-all-start.3 = ((bf16[16,16,2304]{2,1,0:T(8,128)(2,1)}), bf16[16,16,2304]{2,1,0:T(8,128)(2,1)S(1)}, u32[]{:S(2)}, u32[]{:S(2)}) async-start(bf16[16,16,2304]{2,1,0:T(8,128)(2,1)} %gradient_rows.1), calls=%async_computation.3 | async-start | bytes 2359296 | tf_op jit(solution)/shard_map/all_to_all | solution.py:312
  115.1 14.5 %collective-permute-start.18 = (bf16[128,2304]{1,0:T(8,128)(2,1)S(1)}, bf16[128,2304]{1,0:T(8,128)(2,1)S(1)}, u32[]{:S(2)}, u32[]{:S(2)}) collective-permute-start(bf16[128,2304]{1,0:T(8,128)(2,1)S(1)} %copy-done.4), channel_id=1, source_target_pairs={{0,96},{32,0},{64,32},{96,64},{1,97},{33,1},{65,33},{97,65},{2,98}... | collective-permute-start | bytes 1769480 | tf_op jit(solution)/shard_map/ppermute | solution.py:255
  119.1 65.1 %copy-start.5 = (bf16[128,2304]{1,0:T(8,128)(2,1)}, bf16[128,2304]{1,0:T(8,128)(2,1)S(1)}, u32[]{:S(2)}) copy-start(bf16[128,2304]{1,0:T(8,128)(2,1)S(1)} %pad_maximum_fusion.refs_0_) | copy-start | bytes 1769476
  119.1 14.8 %collective-permute-start.6 = (bf16[128,2304]{1,0:T(8,128)(2,1)S(1)}, bf16[128,2304]{1,0:T(8,128)(2,1)S(1)}, u32[]{:S(2)}, u32[]{:S(2)}) collective-permute-start(bf16[128,2304]{1,0:T(8,128)(2,1)S(1)} %pad_maximum_fusion.refs_0_), channel_id=1, source_target_pairs={{0,32},{32,64},{64,96},{96,0},{1,33},{33,65},{65,97},{97,1},{2,34}... | collective-permute-start | bytes 1769480 | tf_op jit(solution)/shard_map/ppermute | solution.py:255
  119.2 23.0 %collective-permute-start.17 = (bf16[128,2304]{1,0:T(8,128)(2,1)S(1)}, bf16[128,2304]{1,0:T(8,128)(2,1)S(1)}, u32[]{:S(2)}, u32[]{:S(2)}) collective-permute-start(bf16[128,2304]{1,0:T(8,128)(2,1)S(1)} %pad_maximum_fusion.refs_0_), channel_id=1, source_target_pairs={{0,96},{32,0},{64,32},{96,64},{1,97},{33,1},{65,33},{97,65},{2,98}... | collective-permute-start | bytes 1769480 | tf_op jit(solution)/shard_map/ppermute | solution.py:255
  121.9 24.7 %collective-permute-start.16 = (bf16[128,2304]{1,0:T(8,128)(2,1)S(1)}, bf16[128,2304]{1,0:T(8,128)(2,1)S(1)}, u32[]{:S(2)}, u32[]{:S(2)}) collective-permute-start(bf16[128,2304]{1,0:T(8,128)(2,1)S(1)} %copy-done.4), channel_id=1, source_target_pairs={{0,32},{32,64},{64,96},{96,0},{1,33},{33,65},{65,97},{97,1},{2,34}... | collective-permute-start | bytes 1769480 | tf_op jit(solution)/shard_map/ppermute | solution.py:255
  129.6 54.6 %copy-start.6 = (bf16[128,2304]{1,0:T(8,128)(2,1)}, bf16[128,2304]{1,0:T(8,128)(2,1)S(1)}, u32[]{:S(2)}) copy-start(bf16[128,2304]{1,0:T(8,128)(2,1)S(1)} %collective-permute-done.18.refs_5_) | copy-start | bytes 1769476
  129.6 25.3 %collective-permute-start.20 = (bf16[128,2304]{1,0:T(8,128)(2,1)S(1)}, bf16[128,2304]{1,0:T(8,128)(2,1)}, u32[]{:S(2)}, u32[]{:S(2)}) collective-permute-start(bf16[128,2304]{1,0:T(8,128)(2,1)S(1)} %collective-permute-done.18.refs_5_), channel_id=1, source_target_pairs={{0,96},{32,0},{64,32},{96,64},{1,97},{33,1},{65,33},{97,65},{2,98}... | collective-permute-start | bytes 1769480 | tf_op jit(solution)/shard_map/ppermute | solution.py:255
  133.9 50.3 %copy-start.7 = (bf16[128,2304]{1,0:T(8,128)(2,1)}, bf16[128,2304]{1,0:T(8,128)(2,1)S(1)}, u32[]{:S(2)}) copy-start(bf16[128,2304]{1,0:T(8,128)(2,1)S(1)} %collective-permute-done.6.refs_2_) | copy-start | bytes 1769476
  133.9 45.9 %collective-permute-start.19 = (bf16[128,2304]{1,0:T(8,128)(2,1)S(1)}, bf16[128,2304]{1,0:T(8,128)(2,1)}, u32[]{:S(2)}, u32[]{:S(2)}) collective-permute-start(bf16[128,2304]{1,0:T(8,128)(2,1)S(1)} %collective-permute-done.6.refs_2_), channel_id=1, source_target_pairs={{0,32},{32,64},{64,96},{96,0},{1,33},{33,65},{65,97},{97,1},{2,34}... | collective-permute-start | bytes 1769480 | tf_op jit(solution)/shard_map/ppermute | solution.py:255
  133.9 46.3 %collective-permute-start.21 = (bf16[128,2304]{1,0:T(8,128)(2,1)S(1)}, bf16[128,2304]{1,0:T(8,128)(2,1)}, u32[]{:S(2)}, u32[]{:S(2)}) collective-permute-start(bf16[128,2304]{1,0:T(8,128)(2,1)S(1)} %pad_maximum_fusion.refs_0_), channel_id=1, source_target_pairs={{0,8},{8,0},{1,9},{9,1},{2,10},{10,2},{3,11},{11,3},{4,12},{12,4},... | collective-permute-start | bytes 1769480 | tf_op jit(solution)/shard_map/ppermute | solution.py:255
  142.2 4.3 %copy-start.8 = (bf16[128,2304]{1,0:T(8,128)(2,1)}, bf16[128,2304]{1,0:T(8,128)(2,1)S(1)}, u32[]{:S(2)}) copy-start(bf16[128,2304]{1,0:T(8,128)(2,1)S(1)} %collective-permute-done.17.refs_4_) | copy-start | bytes 1769476
  142.2 38.1 %collective-permute-start.22 = (bf16[128,2304]{1,0:T(8,128)(2,1)S(1)}, bf16[128,2304]{1,0:T(8,128)(2,1)}, u32[]{:S(2)}, u32[]{:S(2)}) collective-permute-start(bf16[128,2304]{1,0:T(8,128)(2,1)S(1)} %copy-done.4), channel_id=1, source_target_pairs={{0,8},{8,0},{1,9},{9,1},{2,10},{10,2},{3,11},{11,3},{4,12},{12,4},... | collective-permute-start | bytes 1769480 | tf_op jit(solution)/shard_map/ppermute | solution.py:255
  146.5 0.8 copy-start.9
  147.4 33.3 %collective-permute-start.26 = (bf16[128,2304]{1,0:T(8,128)(2,1)S(1)}, bf16[128,2304]{1,0:T(8,128)(2,1)}, u32[]{:S(2)}, u32[]{:S(2)}) collective-permute-start(bf16[128,2304]{1,0:T(8,128)(2,1)S(1)} %collective-permute-done.18.refs_5_), channel_id=1, source_target_pairs={{0,8},{8,0},{1,9},{9,1},{2,10},{10,2},{3,11},{11,3},{4,12},{12,4},... | collective-permute-start | bytes 1769480 | tf_op jit(solution)/shard_map/ppermute | solution.py:255
  151.5 1.0 copy-start
  154.9 25.9 %collective-permute-start.29 = (f32[16,2304]{1,0:T(8,128)}, f32[16,2304]{1,0:T(8,128)}, u32[]{:S(2)}, u32[]{:S(2)}) collective-permute-start(f32[16,2304]{1,0:T(8,128)} %get-tuple-element.48), channel_id=1, source_target_pairs={{0,0},{8,16},{16,8},{24,24},{1,1},{9,17},{17,9},{25,25},{2,2},{10,... | collective-permute-start | bytes 442376 | tf_op jit(solution)/shard_map/ppermute | solution.py:315
  160.0 19.1 %all-to-all-start.4 = ((f32[128,1,128]{2,1,0:T(1,128)}), f32[128,1,128]{2,1,0:T(1,128)S(1)}, u32[]{:S(2)}, u32[]{:S(2)}) async-start(f32[128,1,128]{2,1,0:T(1,128)} %get-tuple-element.42), calls=%async_computation.4 | async-start | bytes 131072 | tf_op jit(solution)/shard_map/all_to_all | solution.py:316
  179.1 0.6 copy-start.14
  179.8 4.5 %collective-permute-start.23 = (bf16[128,2304]{1,0:T(8,128)(2,1)S(1)}, bf16[128,2304]{1,0:T(8,128)(2,1)S(1)}, u32[]{:S(2)}, u32[]{:S(2)}) collective-permute-start(bf16[128,2304]{1,0:T(8,128)(2,1)S(1)} %collective-permute-done.6.refs_2_), channel_id=1, source_target_pairs={{0,8},{8,0},{1,9},{9,1},{2,10},{10,2},{3,11},{11,3},{4,12},{12,4},... | collective-permute-start | bytes 1769480 | tf_op jit(solution)/shard_map/ppermute | solution.py:255
  180.2 4.1 %collective-permute-start.25 = (bf16[128,2304]{1,0:T(8,128)(2,1)}, bf16[128,2304]{1,0:T(8,128)(2,1)S(1)}, u32[]{:S(2)}, u32[]{:S(2)}) collective-permute-start(bf16[128,2304]{1,0:T(8,128)(2,1)} %copy-done.8), channel_id=1, source_target_pairs={{0,8},{8,0},{1,9},{9,1},{2,10},{10,2},{3,11},{11,3},{4,12},{12,4},... | collective-permute-start | bytes 1769480 | tf_op jit(solution)/shard_map/ppermute | solution.py:255
  180.3 5.1 %collective-permute-start.24 = (bf16[128,2304]{1,0:T(8,128)(2,1)}, bf16[128,2304]{1,0:T(8,128)(2,1)S(1)}, u32[]{:S(2)}, u32[]{:S(2)}) collective-permute-start(bf16[128,2304]{1,0:T(8,128)(2,1)} %copy-done.9), channel_id=1, source_target_pairs={{0,8},{8,0},{1,9},{9,1},{2,10},{10,2},{3,11},{11,3},{4,12},{12,4},... | collective-permute-start | bytes 1769480 | tf_op jit(solution)/shard_map/ppermute | solution.py:255
  180.7 4.7 %collective-permute-start.28 = (bf16[128,2304]{1,0:T(8,128)(2,1)}, bf16[128,2304]{1,0:T(8,128)(2,1)}, u32[]{:S(2)}, u32[]{:S(2)}) collective-permute-start(bf16[128,2304]{1,0:T(8,128)(2,1)} %collective-permute-done.20.refs_7_), channel_id=1, source_target_pairs={{0,8},{8,0},{1,9},{9,1},{2,10},{10,2},{3,11},{11,3},{4,12},{12,4},... | collective-permute-start | bytes 1769480 | tf_op jit(solution)/shard_map/ppermute | solution.py:255
  180.8 4.7 %collective-permute-start.27 = (bf16[128,2304]{1,0:T(8,128)(2,1)}, bf16[128,2304]{1,0:T(8,128)(2,1)}, u32[]{:S(2)}, u32[]{:S(2)}) collective-permute-start(bf16[128,2304]{1,0:T(8,128)(2,1)} %collective-permute-done.19.refs_6_), channel_id=1, source_target_pairs={{0,8},{8,0},{1,9},{9,1},{2,10},{10,2},{3,11},{11,3},{4,12},{12,4},... | collective-permute-start | bytes 1769480 | tf_op jit(solution)/shard_map/ppermute | solution.py:255
  184.3 1.3 copy-start.10
  184.3 1.2 copy-start.11
  185.4 0.8 copy-start.12

commit v5 on v4

--- a/solution.py
+++ b/solution.py
@@ -137,7 +137,7 @@
 
 
 def project_kernel(me_ref, att_ref, *refs):
-    rows, out_ref, left = refs[:16], refs[16], refs[17]
+    rows, out_ref, left = refs[:10], refs[10], refs[11]
     x, c, z = me_ref[0], me_ref[2], me_ref[3]
     y = me_ref[4] * 2 + me_ref[1]
 
@@ -243,9 +243,6 @@
             jax.ShapeDtypeStruct(a.shape, a.dtype) for a in (weight, first, fscale, second, sscale)
         ),
         compiler_params=params(),
-        cost_estimate=pl.CostEstimate(
-            flops=30_000_000_000, bytes_accessed=1_000_000, transcendentals=0
-        ),
         name="adam",
     )(grad, squares, weight, first, fscale, second, sscale)
 
@@ -296,33 +293,27 @@
 
     columns = lax.all_to_all(own, ("dp_0", "dp_2"), 0, 0, tiled=True)
     rows = after(rows, own)
-    rows = [rows] + [shift(rows, "seq_0", k) for k in (1, 2, 3)]
-    top, bottom = jnp.concatenate(rows[:2], axis=0), jnp.concatenate(rows[2:], axis=0)
+    rows = jnp.concatenate([rows] + [shift(rows, "seq_0", k) for k in (1, 2, 3)], axis=0)
 
     partial = over_columns(
         gradient_kernel, me, [columns], cots, (16, 16, WIDE), (16, 16, DO), "gradient_rows",
         2 * 256 * 2048 * DO,
     )
-    top, bottom = after(top, columns), after(bottom, columns)
-    left_top, right_bottom = shift(top, "dp_0", 1), shift(bottom, "dp_0", -1)
-    far_top, far_bottom = shift(left_top, "dp_0", 1), shift(right_bottom, "dp_0", -1)
-    left_bottom = shift(after(bottom, partial), "dp_0", 1)
-    right_top = shift(after(top, partial), "dp_0", -1)
-    rows = [top, bottom, left_top, left_bottom, right_top, right_bottom, far_top, far_bottom]
+    rows = from_ring(after(rows, columns))
     parts = lax.all_to_all(partial, ("dp_1", "seq_0", "seq_1"), 0, 0, tiled=True)
 
     sums, squares = total_rows(parts)
     grad = lax.ppermute(sums, ("dp_1", "dp_2"), [(0, 0), (1, 2), (2, 1), (3, 3)])
     squares = lax.all_to_all(squares, DP_SEQ, 0, 0, tiled=True)
     rows = rows + from_partner(
-        [after(a, partial if k in (0, 1, 2, 5) else squares) for k, a in enumerate(rows)]
+        [after(a, partial) for a in rows[:3]] + [after(a, sums) for a in rows[3:]]
     )
     layer_out = over_columns(
         project_kernel, me, [own.reshape(8, 16, 16, TILE)], rows,
         (1, TILE, WIDE), (1, TILE, DO), "project", 1000,
     )
     new_weight, new_first, new_fscale, new_second, new_sscale = adam(
-        grad, squares, weight,
+        after(grad, layer_out), squares, weight,
         first_moment, first_scale, second_moment, second_scale,
     )
     return (layer_out, new_weight, new_first, new_fscale, new_second, new_sscale)

time: 195 us -> 174 us (0.89)
  starting transfers between devices: 79.6 us -> 59.5 us
  local copies, waits for them, and re-layouts: 5.78 us -> 10.8 us
  other arithmetic: 4.72 us -> 1.16 us
    ppermute x26 -> x21, starting transfers between devices: 35.3 us -> 24.5 us  [shift(): return lax.ppermute(x, axis, [(i, (i + by) % peers) for i in range(peers)])]
    all_to_all x1, waiting for transfers between devices: 9.81 us -> 0.28 us  [local(): squares = lax.all_to_all(squares, DP_SEQ, 0, 0, tiled=True)]
    ppermute x3, waiting for transfers between devices: 0.01 us -> 8.19 us  [shift_y(): return lax.ppermute(x, ('dp_1', 'seq_1'), pairs)]
    all_to_all x1, starting transfers between devices: 9.33 us -> 4.79 us  [local(): squares = lax.all_to_all(squares, DP_SEQ, 0, 0, tiled=True)]
    ppermute x1, starting transfers between devices: 5.11 us -> 2.18 us  [local(): lax.ppermute(sums, ('dp_1', 'dp_2'), [(0, 0), (1, 2), (2, 1), (3, 3)])]
    slice x1 -> x2, local copies, waits for them, and re-layouts: 0.91 us -> 3.84 us  [from_ring(): right[half:]]
    ppermute x26 -> x21, waiting for transfers between devices: 32 us -> 31.5 us  [shift(): return lax.ppermute(x, axis, [(i, (i + by) % peers) for i in range(peers)])]
    unnamed x30 -> x26, local copies, waits for them, and re-layouts: 4.26 us -> 4.43 us
  transfers between devices with their start and end apart: 35 -> 30, of which waited for: 12 -> 8; matrix products, arithmetic and copies ran while one was open for 3% -> 4% of each run, Pallas kernels for 12% -> 16%
where the time goes in v5:
time: 174 us; the launch traced here: 173 us
  waiting for transfers between devices  66.3 us (38%)
  starting transfers between devices  59.5 us (34%)
  Pallas kernels  34.8 us (20%)
  local copies, waits for them, and re-layouts  10.8 us (6%)
    ppermute x21, waiting for transfers between devices, shift(): return lax.ppermute(x, axis, [(i, (i + by) % peers) for i in range(peers)])  31.5 us
    all_to_all x1, waiting for transfers between devices, local(): arrived = lax.all_to_all(packed, SEQ, 0, 0, tiled=True)  26.3 us
    ppermute x21, starting transfers between devices, shift(): return lax.ppermute(x, axis, [(i, (i + by) % peers) for i in range(peers)])  24.5 us
    pallas_call x2, Pallas kernels, over_columns(): pl.pallas_call(kernel, grid_spec=pltpu.PrefetchScalarGridSpec(num_scalar_...  16.7 us
    pallas_call x1, Pallas kernels, attend(): pl.pallas_call(attend_kernel, out_shape=jax.ShapeDtypeStruct((BLOCKS, 256...  9.03 us
    all_to_all x1, starting transfers between devices, local(): arrived = lax.all_to_all(packed, SEQ, 0, 0, tiled=True)  8.49 us
    ppermute x3, waiting for transfers between devices, shift_y(): return lax.ppermute(x, ('dp_1', 'seq_1'), pairs)  8.19 us
    all_to_all x1, starting transfers between devices, local(): columns = lax.all_to_all(own, ('dp_0', 'dp_2'), 0, 0, tiled=True)  5.82 us
  transfers between devices with their start and end apart: 30, of which 8 were waited for; matrix products, arithmetic and copies ran while one was open for 4% of the time, Pallas kernels for 16%

profile of v5, /device:TPU:1, one launch (start us, length us, event | category | flops | bytes accessed | tf_op | source)
XLA Modules:
  0.0 173.4 jit_solution(3404199352418898118)
XLA Ops:
  0.6 3.8 %pack.1 = bf16[8,272,512]{2,1,0:T(8,128)(2,1)} custom-call(bf16[256,2048]{1,0:T(8,128)(2,1)} %bitcast.10, bf16[256,1024]{1,0:T(8,128)(2,1)} %bitcast.11, bf16[256,1024]{1,0:T(8,128)(2,1)} %bitcast.12, s32[1,256]{1,0:T(1,128)} %seg_ref.1), custom_call_target="tpu_custom_call" | custom-call | bytes 6000000 | tf_op jit(solution)/shard_map/pack/pallas_call | solution.py:63
  4.5 8.5 %all-to-all-start = ((bf16[8,272,512]{2,1,0:T(8,128)(2,1)}), bf16[8,272,512]{2,1,0:T(8,128)(2,1)S(1)}, u32[]{:S(2)}, u32[]{:S(2)}) async-start(bf16[8,272,512]{2,1,0:T(8,128)(2,1)} %pack.1), calls=%async_computation | async-start | bytes 4456448 | tf_op jit(solution)/shard_map/all_to_all | solution.py:285
  13.0 1.2 collective-permute-start.10
  14.2 1.5 collective-permute-start.11
  15.6 26.3 %all-to-all-done.in_ref = bf16[8,272,512]{2,1,0:T(8,128)(2,1)S(1)} async-done(((bf16[8,272,512]{2,1,0:T(8,128)(2,1)}), bf16[8,272,512]{2,1,0:T(8,128)(2,1)S(1)}, u32[]{:S(2)}, u32[]{:S(2)}) %all-to-all-start) | async-done | bytes 2228256 | tf_op jit(solution)/shard_map/all_to_all | solution.py:285
  41.9 1.4 copy-done.4
  43.3 9.0 %attend.1 = bf16[8,256,256]{2,1,0:T(8,128)(2,1)} custom-call(bf16[8,272,512]{2,1,0:T(8,128)(2,1)} %copy-done.4), custom_call_target="tpu_custom_call" | custom-call | flops 10000000000 | bytes 4000000 | tf_op jit(solution)/shard_map/attend/pallas_call | solution.py:109
  52.3 4.4 %all-to-all-start.1 = ((bf16[8,256,256]{2,1,0:T(8,128)(2,1)}), bf16[8,256,256]{2,1,0:T(8,128)(2,1)}, u32[]{:S(2)}, u32[]{:S(2)}) async-start(bf16[8,256,256]{2,1,0:T(8,128)(2,1)} %attend.1), calls=%async_computation.1 | async-start | bytes 2097152 | tf_op jit(solution)/shard_map/all_to_all | solution.py:289
  56.7 1.5 collective-permute-start
  58.2 3.4 %collective-permute-start.1 = (bf16[16,2304]{1,0:T(8,128)(2,1)S(1)}, bf16[16,2304]{1,0:T(8,128)(2,1)S(1)}, u32[]{:S(2)}, u32[]{:S(2)}) collective-permute-start(bf16[16,2304]{1,0:T(8,128)(2,1)S(1)} %convert_element_type.3), channel_id=1, source_target_pairs={{0,1},{16,17},{1,0},{17,16},{2,3},{18,19},{3,2},{19,18},{4,5},{20,... | collective-permute-start | bytes 221192 | tf_op jit(solution)/shard_map/ppermute | solution.py:275
  61.6 0.1 collective-permute-start.2
  61.7 0.0 collective-permute-done.10.refs_1_
  61.7 1.2 collective-permute-start.12
  62.9 0.0 collective-permute-done.11.refs_2_
  62.9 1.9 %slice.19 = bf16[128,2304]{1,0:T(8,128)(2,1)} slice(bf16[256,2304]{1,0:T(8,128)(2,1)} %collective-permute-done.11.refs_2_), slice={[128:256], [0:2304]} | slice | bytes 1179648 | tf_op jit(solution)/shard_map/slice | solution.py:262
  64.8 1.6 collective-permute-start.13
  66.4 8.2 %collective-permute-done = bf16[16,2304]{1,0:T(8,128)(2,1)S(1)} collective-permute-done((bf16[16,2304]{1,0:T(8,128)(2,1)S(1)}, bf16[16,2304]{1,0:T(8,128)(2,1)S(1)}, u32[]{:S(2)}, u32[]{:S(2)}) %collective-permute-start) | collective-permute-done | bytes 73760 | tf_op jit(solution)/shard_map/ppermute | solution.py:275
  74.6 0.0 collective-permute-done.1
  74.6 0.0 collective-permute-done.2
  74.7 1.3 collective-permute-start.3
  75.9 5.8 %all-to-all-start.2 = ((bf16[8,256,256]{2,1,0:T(8,128)(2,1)}), bf16[8,256,256]{2,1,0:T(8,128)(2,1)S(1)}, u32[]{:S(2)}, u32[]{:S(2)}) async-start(bf16[8,256,256]{2,1,0:T(8,128)(2,1)} %all-to-all-done.1), calls=%async_computation.2 | async-start | bytes 2097152 | tf_op jit(solution)/shard_map/all_to_all | solution.py:294
  81.7 2.4 %collective-permute-start.4 = (bf16[64,2304]{1,0:T(8,128)(2,1)S(1)}, bf16[64,2304]{1,0:T(8,128)(2,1)S(1)}, u32[]{:S(2)}, u32[]{:S(2)}) collective-permute-start(bf16[64,2304]{1,0:T(8,128)(2,1)S(1)} %pad_maximum_fusion.1), channel_id=1, source_target_pairs={{0,4},{2,6},{4,0},{6,2},{1,5},{3,7},{5,1},{7,3},{8,12},{10,14},{12... | collective-permute-start | bytes 884744 | tf_op jit(solution)/shard_map/ppermute | solution.py:252
  84.2 1.2 collective-permute-start.5
  85.3 0.0 collective-permute-done.12.refs_3_
  85.3 0.6 collective-permute-start.15
  85.9 0.0 collective-permute-done.13.refs_4_
  85.9 0.1 collective-permute-start.16
  86.0 0.0 collective-permute-done.3
  86.0 0.4 collective-permute-start.14
  86.4 5.5 %collective-permute-done.4 = bf16[64,2304]{1,0:T(8,128)(2,1)S(1)} collective-permute-done((bf16[64,2304]{1,0:T(8,128)(2,1)S(1)}, bf16[64,2304]{1,0:T(8,128)(2,1)S(1)}, u32[]{:S(2)}, u32[]{:S(2)}) %collective-permute-start.4) | collective-permute-done | bytes 294944 | tf_op jit(solution)/shard_map/ppermute | solution.py:252
  91.9 0.8 collective-permute-start.17
  92.7 5.3 %collective-permute-done.5 = bf16[64,2304]{1,0:T(8,128)(2,1)S(1)} collective-permute-done((bf16[64,2304]{1,0:T(8,128)(2,1)S(1)}, bf16[64,2304]{1,0:T(8,128)(2,1)S(1)}, u32[]{:S(2)}, u32[]{:S(2)}) %collective-permute-start.5) | collective-permute-done | bytes 294944 | tf_op jit(solution)/shard_map/ppermute | solution.py:252
  97.9 0.8 collective-permute-start.18
  98.7 1.1 pad_maximum_fusion.refs_0_
  99.9 0.0 all-to-all-done.2.att_ref
  99.9 2.7 %collective-permute-start.7 = (bf16[256,2304]{1,0:T(8,128)(2,1)S(1)}, bf16[256,2304]{1,0:T(8,128)(2,1)}, u32[]{:S(2)}, u32[]{:S(2)}) collective-permute-start(bf16[256,2304]{1,0:T(8,128)(2,1)S(1)} %pad_maximum_fusion.refs_0_), channel_id=1, source_target_pairs={{0,96},{32,0},{64,32},{96,64},{1,97},{33,1},{65,33},{97,65},{2,98}... | collective-permute-start | bytes 3538952 | tf_op jit(solution)/shard_map/ppermute | solution.py:252
  102.6 0.0 collective-permute-done.18.refs_9_
  102.6 0.0 collective-permute-start.6
  102.6 0.6 stack.23.me_ref
  103.2 0.0 collective-permute-done.15.refs_6_
  103.2 8.2 %gradient_rows.1 = bf16[16,16,2304]{2,1,0:T(8,128)(2,1)} custom-call(s32[5]{0:T(128)} %stack.23.me_ref, bf16[8,256,256]{2,1,0:T(8,128)(2,1)} %copy-done.2, bf16[256,2304]{1,0:T(8,128)(2,1)} %bitcast.9.refs_0_, bf16[256,2304]{1,0:T(8,128)(2,1)} %copy-done.3, bf16[256,2304]{1,0:T(8,128)(2,1)} %collective-permute-done.11.refs_2_, ...), custom_call_target="tpu_custom_call" | custom-call | flops 2415919104 | bytes 12079595 | tf_op jit(solution)/shard_map/gradient_rows/pallas_call | solution.py:165
  111.4 4.4 %all-to-all-start.3 = ((bf16[16,16,2304]{2,1,0:T(8,128)(2,1)}), bf16[16,16,2304]{2,1,0:T(8,128)(2,1)S(1)}, u32[]{:S(2)}, u32[]{:S(2)}) async-start(bf16[16,16,2304]{2,1,0:T(8,128)(2,1)} %gradient_rows.1), calls=%async_computation.3 | async-start | bytes 2359296 | tf_op jit(solution)/shard_map/all_to_all | solution.py:303
  115.8 0.6 collective-permute-start.19
  116.5 11.5 %collective-permute-done.7.refs_2_ = bf16[256,2304]{1,0:T(8,128)(2,1)} collective-permute-done((bf16[256,2304]{1,0:T(8,128)(2,1)S(1)}, bf16[256,2304]{1,0:T(8,128)(2,1)}, u32[]{:S(2)}, u32[]{:S(2)}) %collective-permute-start.7) | collective-permute-done | bytes 1179680 | tf_op jit(solution)/shard_map/ppermute | solution.py:252
  128.0 1.9 %slice.17 = bf16[128,2304]{1,0:T(8,128)(2,1)} slice(bf16[256,2304]{1,0:T(8,128)(2,1)} %collective-permute-done.7.refs_2_), slice={[128:256], [0:2304]} | slice | bytes 1179648 | tf_op jit(solution)/shard_map/slice | solution.py:262
  129.9 3.5 %collective-permute-start.9 = (bf16[128,2304]{1,0:T(8,128)(2,1)}, bf16[128,2304]{1,0:T(8,128)(2,1)}, u32[]{:S(2)}, u32[]{:S(2)}) collective-permute-start(bf16[128,2304]{1,0:T(8,128)(2,1)} %slice.17), channel_id=1, source_target_pairs={{0,96},{32,0},{64,32},{96,64},{1,97},{33,1},{65,33},{97,65},{2,98}... | collective-permute-start | bytes 1769480 | tf_op jit(solution)/shard_map/ppermute | solution.py:252
  133.4 1.9 %slice.16 = bf16[128,2304]{1,0:T(8,128)(2,1)} slice(bf16[256,2304]{1,0:T(8,128)(2,1)} %collective-permute-done.6.refs_1_), slice={[0:128], [0:2304]} | slice | bytes 1179648 | tf_op jit(solution)/shard_map/slice | solution.py:262
  135.3 1.1 collective-permute-start.21
  136.4 0.0 collective-permute-start.20
  136.4 1.0 copy-done.1
  137.4 2.2 %total_rows.1 = (f32[16,2304]{1,0:T(8,128)}, f32[128,1,128]{2,1,0:T(1,128)}) custom-call(bf16[16,16,2304]{2,1,0:T(8,128)(2,1)} %copy-done.1), custom_call_target="tpu_custom_call" | custom-call | tf_op jit(solution)/shard_map/total_rows/pallas_call | solution.py:192
  139.7 5.9 %collective-permute-done.9.refs_4_ = bf16[128,2304]{1,0:T(8,128)(2,1)} collective-permute-done((bf16[128,2304]{1,0:T(8,128)(2,1)}, bf16[128,2304]{1,0:T(8,128)(2,1)}, u32[]{:S(2)}, u32[]{:S(2)}) %collective-permute-start.9) | collective-permute-done | bytes 589856 | tf_op jit(solution)/shard_map/ppermute | solution.py:252
  145.6 1.7 collective-permute-start.23
  147.3 3.3 %collective-permute-done.8.refs_3_ = bf16[128,2304]{1,0:T(8,128)(2,1)} collective-permute-done((bf16[128,2304]{1,0:T(8,128)(2,1)}, bf16[128,2304]{1,0:T(8,128)(2,1)}, u32[]{:S(2)}, u32[]{:S(2)}) %collective-permute-start.8) | collective-permute-done | bytes 589856 | tf_op jit(solution)/shard_map/ppermute | solution.py:252
  150.6 2.0 %collective-permute-start.22 = (bf16[128,2304]{1,0:T(8,128)(2,1)}, bf16[128,2304]{1,0:T(8,128)(2,1)S(1)}, u32[]{:S(2)}, u32[]{:S(2)}) collective-permute-start(bf16[128,2304]{1,0:T(8,128)(2,1)} %collective-permute-done.8.refs_3_), channel_id=1, source_target_pairs={{0,8},{8,0},{1,9},{9,1},{2,10},{10,2},{3,11},{11,3},{4,12},{12,4},... | collective-permute-start | bytes 1769480 | tf_op jit(solution)/shard_map/ppermute | solution.py:252
  152.6 2.2 %collective-permute-start.24 = (f32[16,2304]{1,0:T(8,128)}, f32[16,2304]{1,0:T(8,128)S(1)}, u32[]{:S(2)}, u32[]{:S(2)}) collective-permute-start(f32[16,2304]{1,0:T(8,128)} %get-tuple-element.38), channel_id=1, source_target_pairs={{0,0},{8,16},{16,8},{24,24},{1,1},{9,17},{17,9},{25,25},{2,2},{10,... | collective-permute-start | bytes 442376 | tf_op jit(solution)/shard_map/ppermute | solution.py:306
  154.8 4.8 %all-to-all-start.4 = ((f32[128,1,128]{2,1,0:T(1,128)}), f32[128,1,128]{2,1,0:T(1,128)S(1)}, u32[]{:S(2)}, u32[]{:S(2)}) async-start(f32[128,1,128]{2,1,0:T(1,128)} %get-tuple-element.42), calls=%async_computation.4 | async-start | bytes 131072 | tf_op jit(solution)/shard_map/all_to_all | solution.py:307
  159.7 0.8 copy-done.7
  160.4 0.2 copy-done.8
  160.7 8.4 %project.1 = bf16[1,256,2304]{2,1,0:T(8,128)(2,1)} custom-call(s32[5]{0:T(128)} %stack.23.me_ref, bf16[8,16,16,256]{3,2,1,0:T(8,128)(2,1)} %bitcast.8.att_ref, bf16[256,2304]{1,0:T(8,128)(2,1)} %copy-done, bf16[256,2304]{1,0:T(8,128)(2,1)} %collective-permute-done.6.refs_1_, bf16[256,2304]{1,0:T(8,128)(2,1)} %collective-permute-done.7.refs_2_, ...), custom_call_target="tpu_custom_call" | custom-call | flops 1000 | bytes 5 | tf_op jit(solution)/shard_map/project/pallas_call | solution.py:165
  169.1 0.3 all-to-all-done.4.squares_ref
  169.4 0.4 copy-done.12
  169.8 0.6 copy-done.11
  170.4 3.0 %adam.1 = (f32[16,2304]{1,0:T(8,128)}, bf16[16,2304]{1,0:T(8,128)(2,1)}, f32[16,18]{1,0:T(8,128)}, bf16[16,2304]{1,0:T(8,128)(2,1)}, f32[16,18]{1,0:T(8,128)}) custom-call(f32[16,2304]{1,0:T(8,128)} %copy-done.12, f32[128,1,128]{2,1,0:T(1,128)} %copy-done.11, f32[16,2304]{1,0:T(8,128)} %weight_ref.1, bf16[16,2304]{1,0:T(8,128)(2,1)} %first_ref.1, ...), custom_call_target="tpu_custom_call" | custom-call | tf_op jit(solution)/shard_map/adam/pallas_call | solution.py:240
  (36 shorter events, 0.1 us)
Async XLA Ops:
  4.5 37.4 %all-to-all-start = ((bf16[8,272,512]{2,1,0:T(8,128)(2,1)}), bf16[8,272,512]{2,1,0:T(8,128)(2,1)S(1)}, u32[]{:S(2)}, u32[]{:S(2)}) async-start(bf16[8,272,512]{2,1,0:T(8,128)(2,1)} %pack.1), calls=%async_computation | async-start | bytes 4456448 | tf_op jit(solution)/shard_map/all_to_all | solution.py:285
  13.0 48.7 %collective-permute-start.10 = (bf16[256,2304]{1,0:T(8,128)(2,1)}, bf16[256,2304]{1,0:T(8,128)(2,1)S(1)}, u32[]{:S(2)}, u32[]{:S(2)}) collective-permute-start(bf16[256,2304]{1,0:T(8,128)(2,1)} %bitcast.9.refs_0_), channel_id=1, source_target_pairs={{0,32},{32,64},{64,96},{96,0},{1,33},{33,65},{65,97},{97,1},{2,34}... | collective-permute-start | bytes 3538952 | tf_op jit(solution)/shard_map/ppermute | solution.py:252
  14.2 48.8 %collective-permute-start.11 = (bf16[256,2304]{1,0:T(8,128)(2,1)}, bf16[256,2304]{1,0:T(8,128)(2,1)}, u32[]{:S(2)}, u32[]{:S(2)}) collective-permute-start(bf16[256,2304]{1,0:T(8,128)(2,1)} %bitcast.9.refs_0_), channel_id=1, source_target_pairs={{0,96},{32,0},{64,32},{96,64},{1,97},{33,1},{65,33},{97,65},{2,98}... | collective-permute-start | bytes 3538952 | tf_op jit(solution)/shard_map/ppermute | solution.py:252
  41.9 1.4 copy-start.4
  52.3 4.4 %copy-start.9 = (f32[16,2304]{1,0:T(8,128)S(1)}, f32[16,2304]{1,0:T(8,128)}, u32[]{:S(2)}) copy-start(f32[16,2304]{1,0:T(8,128)} %weight_ref.1) | copy-start | bytes 442372
  52.3 22.3 %all-to-all-start.1 = ((bf16[8,256,256]{2,1,0:T(8,128)(2,1)}), bf16[8,256,256]{2,1,0:T(8,128)(2,1)}, u32[]{:S(2)}, u32[]{:S(2)}) async-start(bf16[8,256,256]{2,1,0:T(8,128)(2,1)} %attend.1), calls=%async_computation.1 | async-start | bytes 2097152 | tf_op jit(solution)/shard_map/all_to_all | solution.py:289
  56.7 17.9 %collective-permute-start = (bf16[16,2304]{1,0:T(8,128)(2,1)S(1)}, bf16[16,2304]{1,0:T(8,128)(2,1)S(1)}, u32[]{:S(2)}, u32[]{:S(2)}) collective-permute-start(bf16[16,2304]{1,0:T(8,128)(2,1)S(1)} %convert_element_type.3), channel_id=1, source_target_pairs={{0,16},{16,1},{1,17},{17,0},{2,18},{18,3},{3,19},{19,2},{4,20},{20... | collective-permute-start | bytes 221192 | tf_op jit(solution)/shard_map/ppermute | solution.py:275
  58.2 16.4 %collective-permute-start.1 = (bf16[16,2304]{1,0:T(8,128)(2,1)S(1)}, bf16[16,2304]{1,0:T(8,128)(2,1)S(1)}, u32[]{:S(2)}, u32[]{:S(2)}) collective-permute-start(bf16[16,2304]{1,0:T(8,128)(2,1)S(1)} %convert_element_type.3), channel_id=1, source_target_pairs={{0,1},{16,17},{1,0},{17,16},{2,3},{18,19},{3,2},{19,18},{4,5},{20,... | collective-permute-start | bytes 221192 | tf_op jit(solution)/shard_map/ppermute | solution.py:275
  61.6 13.0 %collective-permute-start.2 = (bf16[16,2304]{1,0:T(8,128)(2,1)S(1)}, bf16[16,2304]{1,0:T(8,128)(2,1)S(1)}, u32[]{:S(2)}, u32[]{:S(2)}) collective-permute-start(bf16[16,2304]{1,0:T(8,128)(2,1)S(1)} %convert_element_type.3), channel_id=1, source_target_pairs={{0,17},{16,0},{1,16},{17,1},{2,19},{18,2},{3,18},{19,3},{4,21},{20... | collective-permute-start | bytes 221192 | tf_op jit(solution)/shard_map/ppermute | solution.py:275
  61.7 23.6 %copy-start.3 = (bf16[256,2304]{1,0:T(8,128)(2,1)}, bf16[256,2304]{1,0:T(8,128)(2,1)S(1)}, u32[]{:S(2)}) copy-start(bf16[256,2304]{1,0:T(8,128)(2,1)S(1)} %collective-permute-done.10.refs_1_) | copy-start | bytes 3538948
  61.7 23.6 %collective-permute-start.12 = (bf16[128,2304]{1,0:T(8,128)(2,1)S(1)}, bf16[128,2304]{1,0:T(8,128)(2,1)}, u32[]{:S(2)}, u32[]{:S(2)}) collective-permute-start(bf16[128,2304]{1,0:T(8,128)(2,1)S(1)} %slice.18), channel_id=1, source_target_pairs={{0,32},{32,64},{64,96},{96,0},{1,33},{33,65},{65,97},{97,1},{2,34}... | collective-permute-start | bytes 1769480 | tf_op jit(solution)/shard_map/ppermute | solution.py:252
  64.8 21.1 %collective-permute-start.13 = (bf16[128,2304]{1,0:T(8,128)(2,1)}, bf16[128,2304]{1,0:T(8,128)(2,1)}, u32[]{:S(2)}, u32[]{:S(2)}) collective-permute-start(bf16[128,2304]{1,0:T(8,128)(2,1)} %slice.19), channel_id=1, source_target_pairs={{0,96},{32,0},{64,32},{96,64},{1,97},{33,1},{65,33},{97,65},{2,98}... | collective-permute-start | bytes 1769480 | tf_op jit(solution)/shard_map/ppermute | solution.py:252
  74.6 23.3 %copy-start.6 = (bf16[64,2304]{1,0:T(8,128)(2,1)}, bf16[64,2304]{1,0:T(8,128)(2,1)S(1)}, u32[]{:S(2)}) copy-start(bf16[64,2304]{1,0:T(8,128)(2,1)S(1)} %pad_maximum_fusion.1) | copy-start | bytes 884740
  74.7 11.3 %collective-permute-start.3 = (bf16[64,2304]{1,0:T(8,128)(2,1)S(1)}, bf16[64,2304]{1,0:T(8,128)(2,1)S(1)}, u32[]{:S(2)}, u32[]{:S(2)}) collective-permute-start(bf16[64,2304]{1,0:T(8,128)(2,1)S(1)} %pad_maximum_fusion.1), channel_id=1, source_target_pairs={{0,2},{2,4},{4,6},{6,0},{1,3},{3,5},{5,7},{7,1},{8,10},{10,12},{12... | collective-permute-start | bytes 884744 | tf_op jit(solution)/shard_map/ppermute | solution.py:252
  75.9 24.0 %all-to-all-start.2 = ((bf16[8,256,256]{2,1,0:T(8,128)(2,1)}), bf16[8,256,256]{2,1,0:T(8,128)(2,1)S(1)}, u32[]{:S(2)}, u32[]{:S(2)}) async-start(bf16[8,256,256]{2,1,0:T(8,128)(2,1)} %all-to-all-done.1), calls=%async_computation.2 | async-start | bytes 2097152 | tf_op jit(solution)/shard_map/all_to_all | solution.py:294
  81.7 10.1 %collective-permute-start.4 = (bf16[64,2304]{1,0:T(8,128)(2,1)S(1)}, bf16[64,2304]{1,0:T(8,128)(2,1)S(1)}, u32[]{:S(2)}, u32[]{:S(2)}) collective-permute-start(bf16[64,2304]{1,0:T(8,128)(2,1)S(1)} %pad_maximum_fusion.1), channel_id=1, source_target_pairs={{0,4},{2,6},{4,0},{6,2},{1,5},{3,7},{5,1},{7,3},{8,12},{10,14},{12... | collective-permute-start | bytes 884744 | tf_op jit(solution)/shard_map/ppermute | solution.py:252
  84.2 13.8 %collective-permute-start.5 = (bf16[64,2304]{1,0:T(8,128)(2,1)S(1)}, bf16[64,2304]{1,0:T(8,128)(2,1)S(1)}, u32[]{:S(2)}, u32[]{:S(2)}) collective-permute-start(bf16[64,2304]{1,0:T(8,128)(2,1)S(1)} %pad_maximum_fusion.1), channel_id=1, source_target_pairs={{0,6},{2,0},{4,2},{6,4},{1,7},{3,1},{5,3},{7,5},{8,14},{10,8},{12,... | collective-permute-start | bytes 884744 | tf_op jit(solution)/shard_map/ppermute | solution.py:252
  85.3 17.9 %collective-permute-start.15 = (bf16[256,2304]{1,0:T(8,128)(2,1)S(1)}, bf16[256,2304]{1,0:T(8,128)(2,1)}, u32[]{:S(2)}, u32[]{:S(2)}) collective-permute-start(bf16[256,2304]{1,0:T(8,128)(2,1)S(1)} %collective-permute-done.10.refs_1_), channel_id=1, source_target_pairs={{0,8},{8,0},{1,9},{9,1},{2,10},{10,2},{3,11},{11,3},{4,12},{12,4},... | collective-permute-start | bytes 3538952 | tf_op jit(solution)/shard_map/ppermute | solution.py:252
  85.9 17.3 %collective-permute-start.16 = (bf16[256,2304]{1,0:T(8,128)(2,1)}, bf16[256,2304]{1,0:T(8,128)(2,1)}, u32[]{:S(2)}, u32[]{:S(2)}) collective-permute-start(bf16[256,2304]{1,0:T(8,128)(2,1)} %collective-permute-done.11.refs_2_), channel_id=1, source_target_pairs={{0,8},{8,0},{1,9},{9,1},{2,10},{10,2},{3,11},{11,3},{4,12},{12,4},... | collective-permute-start | bytes 3538952 | tf_op jit(solution)/shard_map/ppermute | solution.py:252
  86.0 12.0 %copy-start.10 = (bf16[64,2304]{1,0:T(8,128)(2,1)}, bf16[64,2304]{1,0:T(8,128)(2,1)S(1)}, u32[]{:S(2)}) copy-start(bf16[64,2304]{1,0:T(8,128)(2,1)S(1)} %collective-permute-done.3) | copy-start | bytes 884740
  86.0 17.2 %collective-permute-start.14 = (bf16[256,2304]{1,0:T(8,128)(2,1)}, bf16[256,2304]{1,0:T(8,128)(2,1)}, u32[]{:S(2)}, u32[]{:S(2)}) collective-permute-start(bf16[256,2304]{1,0:T(8,128)(2,1)} %bitcast.9.refs_0_), channel_id=1, source_target_pairs={{0,8},{8,0},{1,9},{9,1},{2,10},{10,2},{3,11},{11,3},{4,12},{12,4},... | collective-permute-start | bytes 3538952 | tf_op jit(solution)/shard_map/ppermute | solution.py:252
  91.9 8.0 %collective-permute-start.17 = (bf16[128,2304]{1,0:T(8,128)(2,1)}, bf16[128,2304]{1,0:T(8,128)(2,1)}, u32[]{:S(2)}, u32[]{:S(2)}) collective-permute-start(bf16[128,2304]{1,0:T(8,128)(2,1)} %collective-permute-done.12.refs_3_), channel_id=1, source_target_pairs={{0,8},{8,0},{1,9},{9,1},{2,10},{10,2},{3,11},{11,3},{4,12},{12,4},... | collective-permute-start | bytes 1769480 | tf_op jit(solution)/shard_map/ppermute | solution.py:252
  97.9 4.6 %collective-permute-start.18 = (bf16[128,2304]{1,0:T(8,128)(2,1)}, bf16[128,2304]{1,0:T(8,128)(2,1)}, u32[]{:S(2)}, u32[]{:S(2)}) collective-permute-start(bf16[128,2304]{1,0:T(8,128)(2,1)} %collective-permute-done.13.refs_4_), channel_id=1, source_target_pairs={{0,8},{8,0},{1,9},{9,1},{2,10},{10,2},{3,11},{11,3},{4,12},{12,4},... | collective-permute-start | bytes 1769480 | tf_op jit(solution)/shard_map/ppermute | solution.py:252
  99.9 16.0 %copy-start = (bf16[256,2304]{1,0:T(8,128)(2,1)}, bf16[256,2304]{1,0:T(8,128)(2,1)S(1)}, u32[]{:S(2)}) copy-start(bf16[256,2304]{1,0:T(8,128)(2,1)S(1)} %pad_maximum_fusion.refs_0_) | copy-start | bytes 3538948
  99.9 3.3 %copy-start.2 = (bf16[8,256,256]{2,1,0:T(8,128)(2,1)}, bf16[8,256,256]{2,1,0:T(8,128)(2,1)S(1)}, u32[]{:S(2)}) copy-start(bf16[8,256,256]{2,1,0:T(8,128)(2,1)S(1)} %all-to-all-done.2.att_ref) | copy-start | bytes 3145732
  99.9 28.1 %collective-permute-start.7 = (bf16[256,2304]{1,0:T(8,128)(2,1)S(1)}, bf16[256,2304]{1,0:T(8,128)(2,1)}, u32[]{:S(2)}, u32[]{:S(2)}) collective-permute-start(bf16[256,2304]{1,0:T(8,128)(2,1)S(1)} %pad_maximum_fusion.refs_0_), channel_id=1, source_target_pairs={{0,96},{32,0},{64,32},{96,64},{1,97},{33,1},{65,33},{97,65},{2,98}... | collective-permute-start | bytes 3538952 | tf_op jit(solution)/shard_map/ppermute | solution.py:252
  102.6 30.8 %collective-permute-start.6 = (bf16[256,2304]{1,0:T(8,128)(2,1)S(1)}, bf16[256,2304]{1,0:T(8,128)(2,1)}, u32[]{:S(2)}, u32[]{:S(2)}) collective-permute-start(bf16[256,2304]{1,0:T(8,128)(2,1)S(1)} %pad_maximum_fusion.refs_0_), channel_id=1, source_target_pairs={{0,32},{32,64},{64,96},{96,0},{1,33},{33,65},{65,97},{97,1},{2,34}... | collective-permute-start | bytes 3538952 | tf_op jit(solution)/shard_map/ppermute | solution.py:252
  111.4 25.0 %all-to-all-start.3 = ((bf16[16,16,2304]{2,1,0:T(8,128)(2,1)}), bf16[16,16,2304]{2,1,0:T(8,128)(2,1)S(1)}, u32[]{:S(2)}, u32[]{:S(2)}) async-start(bf16[16,16,2304]{2,1,0:T(8,128)(2,1)} %gradient_rows.1), calls=%async_computation.3 | async-start | bytes 2359296 | tf_op jit(solution)/shard_map/all_to_all | solution.py:303
  115.8 36.8 %collective-permute-start.19 = (bf16[256,2304]{1,0:T(8,128)(2,1)S(1)}, bf16[256,2304]{1,0:T(8,128)(2,1)S(1)}, u32[]{:S(2)}, u32[]{:S(2)}) collective-permute-start(bf16[256,2304]{1,0:T(8,128)(2,1)S(1)} %pad_maximum_fusion.refs_0_), channel_id=1, source_target_pairs={{0,8},{8,0},{1,9},{9,1},{2,10},{10,2},{3,11},{11,3},{4,12},{12,4},... | collective-permute-start | bytes 3538952 | tf_op jit(solution)/shard_map/ppermute | solution.py:252
  129.9 15.7 %collective-permute-start.9 = (bf16[128,2304]{1,0:T(8,128)(2,1)}, bf16[128,2304]{1,0:T(8,128)(2,1)}, u32[]{:S(2)}, u32[]{:S(2)}) collective-permute-start(bf16[128,2304]{1,0:T(8,128)(2,1)} %slice.17), channel_id=1, source_target_pairs={{0,96},{32,0},{64,32},{96,64},{1,97},{33,1},{65,33},{97,65},{2,98}... | collective-permute-start | bytes 1769480 | tf_op jit(solution)/shard_map/ppermute | solution.py:252
  135.3 15.3 %collective-permute-start.8 = (bf16[128,2304]{1,0:T(8,128)(2,1)}, bf16[128,2304]{1,0:T(8,128)(2,1)}, u32[]{:S(2)}, u32[]{:S(2)}) collective-permute-start(bf16[128,2304]{1,0:T(8,128)(2,1)} %slice.16), channel_id=1, source_target_pairs={{0,32},{32,64},{64,96},{96,0},{1,33},{33,65},{65,97},{97,1},{2,34}... | collective-permute-start | bytes 1769480 | tf_op jit(solution)/shard_map/ppermute | solution.py:252
  135.3 24.3 %collective-permute-start.21 = (bf16[256,2304]{1,0:T(8,128)(2,1)}, bf16[256,2304]{1,0:T(8,128)(2,1)}, u32[]{:S(2)}, u32[]{:S(2)}) collective-permute-start(bf16[256,2304]{1,0:T(8,128)(2,1)} %collective-permute-done.7.refs_2_), channel_id=1, source_target_pairs={{0,8},{8,0},{1,9},{9,1},{2,10},{10,2},{3,11},{11,3},{4,12},{12,4},... | collective-permute-start | bytes 3538952 | tf_op jit(solution)/shard_map/ppermute | solution.py:252
  136.4 23.2 %collective-permute-start.20 = (bf16[256,2304]{1,0:T(8,128)(2,1)}, bf16[256,2304]{1,0:T(8,128)(2,1)}, u32[]{:S(2)}, u32[]{:S(2)}) collective-permute-start(bf16[256,2304]{1,0:T(8,128)(2,1)} %collective-permute-done.6.refs_1_), channel_id=1, source_target_pairs={{0,8},{8,0},{1,9},{9,1},{2,10},{10,2},{3,11},{11,3},{4,12},{12,4},... | collective-permute-start | bytes 3538952 | tf_op jit(solution)/shard_map/ppermute | solution.py:252
  136.4 1.0 copy-start.1
  145.6 14.0 %collective-permute-start.23 = (bf16[128,2304]{1,0:T(8,128)(2,1)}, bf16[128,2304]{1,0:T(8,128)(2,1)S(1)}, u32[]{:S(2)}, u32[]{:S(2)}) collective-permute-start(bf16[128,2304]{1,0:T(8,128)(2,1)} %collective-permute-done.9.refs_4_), channel_id=1, source_target_pairs={{0,8},{8,0},{1,9},{9,1},{2,10},{10,2},{3,11},{11,3},{4,12},{12,4},... | collective-permute-start | bytes 1769480 | tf_op jit(solution)/shard_map/ppermute | solution.py:252
  150.6 9.0 %collective-permute-start.22 = (bf16[128,2304]{1,0:T(8,128)(2,1)}, bf16[128,2304]{1,0:T(8,128)(2,1)S(1)}, u32[]{:S(2)}, u32[]{:S(2)}) collective-permute-start(bf16[128,2304]{1,0:T(8,128)(2,1)} %collective-permute-done.8.refs_3_), channel_id=1, source_target_pairs={{0,8},{8,0},{1,9},{9,1},{2,10},{10,2},{3,11},{11,3},{4,12},{12,4},... | collective-permute-start | bytes 1769480 | tf_op jit(solution)/shard_map/ppermute | solution.py:252
  152.6 7.0 %copy-start.5 = (bf16[256,2304]{1,0:T(8,128)(2,1)}, bf16[256,2304]{1,0:T(8,128)(2,1)S(1)}, u32[]{:S(2)}) copy-start(bf16[256,2304]{1,0:T(8,128)(2,1)S(1)} %collective-permute-done.19.refs_5_) | copy-start | bytes 3538948
  152.6 16.5 %collective-permute-start.24 = (f32[16,2304]{1,0:T(8,128)}, f32[16,2304]{1,0:T(8,128)S(1)}, u32[]{:S(2)}, u32[]{:S(2)}) collective-permute-start(f32[16,2304]{1,0:T(8,128)} %get-tuple-element.38), channel_id=1, source_target_pairs={{0,0},{8,16},{16,8},{24,24},{1,1},{9,17},{17,9},{25,25},{2,2},{10,... | collective-permute-start | bytes 442376 | tf_op jit(solution)/shard_map/ppermute | solution.py:306
  154.8 14.6 %all-to-all-start.4 = ((f32[128,1,128]{2,1,0:T(1,128)}), f32[128,1,128]{2,1,0:T(1,128)S(1)}, u32[]{:S(2)}, u32[]{:S(2)}) async-start(f32[128,1,128]{2,1,0:T(1,128)} %get-tuple-element.42), calls=%async_computation.4 | async-start | bytes 131072 | tf_op jit(solution)/shard_map/all_to_all | solution.py:307
  159.6 0.8 copy-start.7
  159.6 1.1 copy-start.8
  169.1 0.7 copy-start.12
  169.8 0.6 copy-start.11

commit v6 on v5

--- a/solution.py
+++ b/solution.py
@@ -243,6 +243,9 @@
             jax.ShapeDtypeStruct(a.shape, a.dtype) for a in (weight, first, fscale, second, sscale)
         ),
         compiler_params=params(),
+        cost_estimate=pl.CostEstimate(
+            flops=30_000_000_000, bytes_accessed=1_000_000, transcendentals=0
+        ),
         name="adam",
     )(grad, squares, weight, first, fscale, second, sscale)
 
@@ -306,14 +309,14 @@
     grad = lax.ppermute(sums, ("dp_1", "dp_2"), [(0, 0), (1, 2), (2, 1), (3, 3)])
     squares = lax.all_to_all(squares, DP_SEQ, 0, 0, tiled=True)
     rows = rows + from_partner(
-        [after(a, partial) for a in rows[:3]] + [after(a, sums) for a in rows[3:]]
+        [after(a, partial) for a in rows[:3]] + [after(a, squares) for a in rows[3:]]
     )
     layer_out = over_columns(
         project_kernel, me, [own.reshape(8, 16, 16, TILE)], rows,
         (1, TILE, WIDE), (1, TILE, DO), "project", 1000,
     )
     new_weight, new_first, new_fscale, new_second, new_sscale = adam(
-        after(grad, layer_out), squares, weight,
+        grad, squares, weight,
         first_moment, first_scale, second_moment, second_scale,
     )
     return (layer_out, new_weight, new_first, new_fscale, new_second, new_sscale)

time: 174 us -> 174 us (level)
  starting transfers between devices: 59.5 us -> 61.7 us
    ppermute x21, waiting for transfers between devices: 31.5 us -> 22.9 us  [shift(): return lax.ppermute(x, axis, [(i, (i + by) % peers) for i in range(peers)])]
    all_to_all x1, waiting for transfers between devices: 0.28 us -> 7.99 us  [local(): squares = lax.all_to_all(squares, DP_SEQ, 0, 0, tiled=True)]
    all_to_all x1, starting transfers between devices: 4.79 us -> 7.73 us  [local(): squares = lax.all_to_all(squares, DP_SEQ, 0, 0, tiled=True)]
    ppermute x21, starting transfers between devices: 24.5 us -> 22.1 us  [shift(): return lax.ppermute(x, axis, [(i, (i + by) % peers) for i in range(peers)])]
    unnamed x26 -> x20, local copies, waits for them, and re-layouts: 4.43 us -> 3.79 us
  transfers between devices with their start and end apart: 30 -> 30, of which waited for: 8 -> 6; matrix products, arithmetic and copies ran while one was open for 4% -> 4% of each run, Pallas kernels for 16% -> 13%
where the time goes in v6:
time: 174 us
  waiting for transfers between devices  65.2 us (37%)
  starting transfers between devices  61.7 us (35%)
  Pallas kernels  34.6 us (20%)
  local copies, waits for them, and re-layouts  10.2 us (6%)
    all_to_all x1, waiting for transfers between devices, local(): arrived = lax.all_to_all(packed, SEQ, 0, 0, tiled=True)  26.3 us
    ppermute x21, waiting for transfers between devices, shift(): return lax.ppermute(x, axis, [(i, (i + by) % peers) for i in range(peers)])  22.9 us
    ppermute x21, starting transfers between devices, shift(): return lax.ppermute(x, axis, [(i, (i + by) % peers) for i in range(peers)])  22.1 us
    pallas_call x2, Pallas kernels, over_columns(): pl.pallas_call(kernel, grid_spec=pltpu.PrefetchScalarGridSpec(num_scalar_...  16.6 us
    pallas_call x1, Pallas kernels, attend(): pl.pallas_call(attend_kernel, out_shape=jax.ShapeDtypeStruct((BLOCKS, 256...  8.89 us
    all_to_all x1, starting transfers between devices, local(): arrived = lax.all_to_all(packed, SEQ, 0, 0, tiled=True)  8.49 us
    ppermute x3, waiting for transfers between devices, shift_y(): return lax.ppermute(x, ('dp_1', 'seq_1'), pairs)  8.1 us
    all_to_all x1, waiting for transfers between devices, local(): squares = lax.all_to_all(squares, DP_SEQ, 0, 0, tiled=True)  7.99 us
  transfers between devices with their start and end apart: 30, of which 6 were waited for; matrix products, arithmetic and copies ran while one was open for 4% of the time, Pallas kernels for 13%

profile of v6, /device:TPU:1, one launch (start us, length us, event | category | flops | bytes accessed | tf_op | source)
XLA Modules:
  0.0 173.8 jit_solution(15575348583621723823)
XLA Ops:
  0.6 3.8 %pack.1 = bf16[8,272,512]{2,1,0:T(8,128)(2,1)} custom-call(bf16[256,2048]{1,0:T(8,128)(2,1)} %bitcast.10, bf16[256,1024]{1,0:T(8,128)(2,1)} %bitcast.11, bf16[256,1024]{1,0:T(8,128)(2,1)} %bitcast.12, s32[1,256]{1,0:T(1,128)} %seg_ref.1), custom_call_target="tpu_custom_call" | custom-call | bytes 6000000 | tf_op jit(solution)/shard_map/pack/pallas_call | solution.py:63
  4.5 8.5 %all-to-all-start = ((bf16[8,272,512]{2,1,0:T(8,128)(2,1)}), bf16[8,272,512]{2,1,0:T(8,128)(2,1)S(1)}, u32[]{:S(2)}, u32[]{:S(2)}) async-start(bf16[8,272,512]{2,1,0:T(8,128)(2,1)} %pack.1), calls=%async_computation | async-start | bytes 4456448 | tf_op jit(solution)/shard_map/all_to_all | solution.py:288
  13.0 1.2 collective-permute-start.10
  14.2 1.5 collective-permute-start.11
  15.6 26.3 %all-to-all-done.in_ref = bf16[8,272,512]{2,1,0:T(8,128)(2,1)S(1)} async-done(((bf16[8,272,512]{2,1,0:T(8,128)(2,1)}), bf16[8,272,512]{2,1,0:T(8,128)(2,1)S(1)}, u32[]{:S(2)}, u32[]{:S(2)}) %all-to-all-start) | async-done | bytes 2228256 | tf_op jit(solution)/shard_map/all_to_all | solution.py:288
  41.9 1.4 copy-done.4
  43.3 8.9 %attend.1 = bf16[8,256,256]{2,1,0:T(8,128)(2,1)} custom-call(bf16[8,272,512]{2,1,0:T(8,128)(2,1)} %copy-done.4), custom_call_target="tpu_custom_call" | custom-call | flops 10000000000 | bytes 4000000 | tf_op jit(solution)/shard_map/attend/pallas_call | solution.py:109
  52.2 4.4 %all-to-all-start.1 = ((bf16[8,256,256]{2,1,0:T(8,128)(2,1)}), bf16[8,256,256]{2,1,0:T(8,128)(2,1)}, u32[]{:S(2)}, u32[]{:S(2)}) async-start(bf16[8,256,256]{2,1,0:T(8,128)(2,1)} %attend.1), calls=%async_computation.1 | async-start | bytes 2097152 | tf_op jit(solution)/shard_map/all_to_all | solution.py:292
  56.6 1.6 collective-permute-start
  58.2 3.4 %collective-permute-start.1 = (bf16[16,2304]{1,0:T(8,128)(2,1)S(1)}, bf16[16,2304]{1,0:T(8,128)(2,1)S(1)}, u32[]{:S(2)}, u32[]{:S(2)}) collective-permute-start(bf16[16,2304]{1,0:T(8,128)(2,1)S(1)} %convert_element_type.3), channel_id=1, source_target_pairs={{0,1},{16,17},{1,0},{17,16},{2,3},{18,19},{3,2},{19,18},{4,5},{20,... | collective-permute-start | bytes 221192 | tf_op jit(solution)/shard_map/ppermute | solution.py:278
  61.6 0.0 collective-permute-start.2
  61.6 0.0 collective-permute-done.10.refs_1_
  61.7 1.2 collective-permute-start.12
  62.9 0.0 collective-permute-done.11.refs_2_
  62.9 1.9 %slice.19 = bf16[128,2304]{1,0:T(8,128)(2,1)} slice(bf16[256,2304]{1,0:T(8,128)(2,1)} %collective-permute-done.11.refs_2_), slice={[128:256], [0:2304]} | slice | bytes 1179648 | tf_op jit(solution)/shard_map/slice | solution.py:265
  64.8 1.5 collective-permute-start.13
  66.4 8.1 %collective-permute-done = bf16[16,2304]{1,0:T(8,128)(2,1)S(1)} collective-permute-done((bf16[16,2304]{1,0:T(8,128)(2,1)S(1)}, bf16[16,2304]{1,0:T(8,128)(2,1)S(1)}, u32[]{:S(2)}, u32[]{:S(2)}) %collective-permute-start) | collective-permute-done | bytes 73760 | tf_op jit(solution)/shard_map/ppermute | solution.py:278
  74.4 0.0 collective-permute-done.1
  74.5 0.0 all-to-all-done.1
  74.5 1.3 collective-permute-start.3
  75.8 5.8 %all-to-all-start.2 = ((bf16[8,256,256]{2,1,0:T(8,128)(2,1)}), bf16[8,256,256]{2,1,0:T(8,128)(2,1)S(1)}, u32[]{:S(2)}, u32[]{:S(2)}) async-start(bf16[8,256,256]{2,1,0:T(8,128)(2,1)} %all-to-all-done.1), calls=%async_computation.2 | async-start | bytes 2097152 | tf_op jit(solution)/shard_map/all_to_all | solution.py:297
  81.6 0.1 collective-permute-start.15
  81.6 0.4 collective-permute-start.16
  82.1 0.1 collective-permute-start.14
  82.2 0.0 collective-permute-done.13.refs_4_
  82.2 2.4 %collective-permute-start.4 = (bf16[64,2304]{1,0:T(8,128)(2,1)S(1)}, bf16[64,2304]{1,0:T(8,128)(2,1)S(1)}, u32[]{:S(2)}, u32[]{:S(2)}) collective-permute-start(bf16[64,2304]{1,0:T(8,128)(2,1)S(1)} %pad_maximum_fusion.1), channel_id=1, source_target_pairs={{0,4},{2,6},{4,0},{6,2},{1,5},{3,7},{5,1},{7,3},{8,12},{10,14},{12... | collective-permute-start | bytes 884744 | tf_op jit(solution)/shard_map/ppermute | solution.py:255
  84.6 1.2 collective-permute-start.5
  85.8 6.1 %collective-permute-done.4 = bf16[64,2304]{1,0:T(8,128)(2,1)S(1)} collective-permute-done((bf16[64,2304]{1,0:T(8,128)(2,1)S(1)}, bf16[64,2304]{1,0:T(8,128)(2,1)S(1)}, u32[]{:S(2)}, u32[]{:S(2)}) %collective-permute-start.4) | collective-permute-done | bytes 294944 | tf_op jit(solution)/shard_map/ppermute | solution.py:255
  91.8 1.3 collective-permute-start.17
  93.1 4.8 %collective-permute-done.5 = bf16[64,2304]{1,0:T(8,128)(2,1)S(1)} collective-permute-done((bf16[64,2304]{1,0:T(8,128)(2,1)S(1)}, bf16[64,2304]{1,0:T(8,128)(2,1)S(1)}, u32[]{:S(2)}, u32[]{:S(2)}) %collective-permute-start.5) | collective-permute-done | bytes 294944 | tf_op jit(solution)/shard_map/ppermute | solution.py:255
  97.9 1.3 collective-permute-start.18
  99.2 1.1 pad_maximum_fusion.refs_0_
  100.3 0.0 collective-permute-done.17.refs_8_
  100.3 2.9 %collective-permute-start.7 = (bf16[256,2304]{1,0:T(8,128)(2,1)S(1)}, bf16[256,2304]{1,0:T(8,128)(2,1)}, u32[]{:S(2)}, u32[]{:S(2)}) collective-permute-start(bf16[256,2304]{1,0:T(8,128)(2,1)S(1)} %pad_maximum_fusion.refs_0_), channel_id=1, source_target_pairs={{0,96},{32,0},{64,32},{96,64},{1,97},{33,1},{65,33},{97,65},{2,98}... | collective-permute-start | bytes 3538952 | tf_op jit(solution)/shard_map/ppermute | solution.py:255
  103.3 0.0 collective-permute-done.18.refs_9_
  103.3 0.0 collective-permute-start.6
  103.3 0.6 stack.23.me_ref
  103.9 0.0 collective-permute-done.15.refs_6_
  103.9 8.2 %gradient_rows.1 = bf16[16,16,2304]{2,1,0:T(8,128)(2,1)} custom-call(s32[5]{0:T(128)} %stack.23.me_ref, bf16[8,256,256]{2,1,0:T(8,128)(2,1)} %copy-done.2, bf16[256,2304]{1,0:T(8,128)(2,1)} %bitcast.9.refs_0_, bf16[256,2304]{1,0:T(8,128)(2,1)} %copy-done.3, bf16[256,2304]{1,0:T(8,128)(2,1)} %collective-permute-done.11.refs_2_, ...), custom_call_target="tpu_custom_call" | custom-call | flops 2415919104 | bytes 12079595 | tf_op jit(solution)/shard_map/gradient_rows/pallas_call | solution.py:165
  112.1 4.6 %all-to-all-start.3 = ((bf16[16,16,2304]{2,1,0:T(8,128)(2,1)}), bf16[16,16,2304]{2,1,0:T(8,128)(2,1)S(1)}, u32[]{:S(2)}, u32[]{:S(2)}) async-start(bf16[16,16,2304]{2,1,0:T(8,128)(2,1)} %gradient_rows.1), calls=%async_computation.3 | async-start | bytes 2359296 | tf_op jit(solution)/shard_map/all_to_all | solution.py:306
  116.7 12.0 %collective-permute-done.7.refs_2_ = bf16[256,2304]{1,0:T(8,128)(2,1)} collective-permute-done((bf16[256,2304]{1,0:T(8,128)(2,1)S(1)}, bf16[256,2304]{1,0:T(8,128)(2,1)}, u32[]{:S(2)}, u32[]{:S(2)}) %collective-permute-start.7) | collective-permute-done | bytes 1179680 | tf_op jit(solution)/shard_map/ppermute | solution.py:255
  128.7 1.9 %slice.17 = bf16[128,2304]{1,0:T(8,128)(2,1)} slice(bf16[256,2304]{1,0:T(8,128)(2,1)} %collective-permute-done.7.refs_2_), slice={[128:256], [0:2304]} | slice | bytes 1179648 | tf_op jit(solution)/shard_map/slice | solution.py:265
  130.6 3.5 %collective-permute-start.9 = (bf16[128,2304]{1,0:T(8,128)(2,1)}, bf16[128,2304]{1,0:T(8,128)(2,1)}, u32[]{:S(2)}, u32[]{:S(2)}) collective-permute-start(bf16[128,2304]{1,0:T(8,128)(2,1)} %slice.17), channel_id=1, source_target_pairs={{0,96},{32,0},{64,32},{96,64},{1,97},{33,1},{65,33},{97,65},{2,98}... | collective-permute-start | bytes 1769480 | tf_op jit(solution)/shard_map/ppermute | solution.py:255
  134.1 0.0 collective-permute-done.6.refs_1_
  134.1 2.0 %slice.16 = bf16[128,2304]{1,0:T(8,128)(2,1)} slice(bf16[256,2304]{1,0:T(8,128)(2,1)} %collective-permute-done.6.refs_1_), slice={[0:128], [0:2304]} | slice | bytes 1179648 | tf_op jit(solution)/shard_map/slice | solution.py:265
  136.1 0.0 collective-permute-start.8
  136.1 1.0 copy-done.1
  137.1 2.2 %total_rows.1 = (f32[16,2304]{1,0:T(8,128)}, f32[128,1,128]{2,1,0:T(1,128)}) custom-call(bf16[16,16,2304]{2,1,0:T(8,128)(2,1)} %copy-done.1), custom_call_target="tpu_custom_call" | custom-call | tf_op jit(solution)/shard_map/total_rows/pallas_call | solution.py:192
  139.3 3.6 %collective-permute-start.24 = (f32[16,2304]{1,0:T(8,128)}, f32[16,2304]{1,0:T(8,128)}, u32[]{:S(2)}, u32[]{:S(2)}) collective-permute-start(f32[16,2304]{1,0:T(8,128)} %get-tuple-element.40), channel_id=1, source_target_pairs={{0,0},{8,16},{16,8},{24,24},{1,1},{9,17},{17,9},{25,25},{2,2},{10,... | collective-permute-start | bytes 442376 | tf_op jit(solution)/shard_map/ppermute | solution.py:309
  142.9 7.7 %all-to-all-start.4 = ((f32[128,1,128]{2,1,0:T(1,128)}), f32[128,1,128]{2,1,0:T(1,128)}, u32[]{:S(2)}, u32[]{:S(2)}) async-start(f32[128,1,128]{2,1,0:T(1,128)} %get-tuple-element.37), calls=%async_computation.4 | async-start | bytes 131072 | tf_op jit(solution)/shard_map/all_to_all | solution.py:310
  150.7 1.2 collective-permute-start.19
  151.9 0.1 collective-permute-start.21
  152.0 0.4 collective-permute-start.20
  152.4 8.0 %all-to-all-done.4.squares_ref = f32[128,1,128]{2,1,0:T(1,128)} async-done(((f32[128,1,128]{2,1,0:T(1,128)}), f32[128,1,128]{2,1,0:T(1,128)}, u32[]{:S(2)}, u32[]{:S(2)}) %all-to-all-start.4) | async-done | bytes 65568 | tf_op jit(solution)/shard_map/all_to_all | solution.py:310
  160.4 0.0 collective-permute-done.8.refs_3_
  160.4 0.4 collective-permute-start.23
  160.8 0.1 collective-permute-start.22
  160.9 3.0 %adam.1 = (f32[16,2304]{1,0:T(8,128)}, bf16[16,2304]{1,0:T(8,128)(2,1)}, f32[16,18]{1,0:T(8,128)}, bf16[16,2304]{1,0:T(8,128)(2,1)}, f32[16,18]{1,0:T(8,128)}) custom-call(f32[16,2304]{1,0:T(8,128)} %collective-permute-done.24.grad_ref, f32[128,1,128]{2,1,0:T(1,128)} %all-to-all-done.4.squares_ref, f32[16,2304]{1,0:T(8,128)} %weight_ref.1, ...), custom_call_target="tpu_custom_call" | custom-call | flops 30000001024 | bytes 1000000 | tf_op jit(solution)/shard_map/adam/pallas_call | solution.py:240
  164.0 0.0 collective-permute-done.23.refs_9_
  164.0 0.0 collective-permute-done.21.refs_7_
  164.0 0.0 collective-permute-done.20.refs_6_
  164.0 1.0 copy-done.5
  165.0 0.4 copy-done.6
  165.4 8.4 %project.1 = bf16[1,256,2304]{2,1,0:T(8,128)(2,1)} custom-call(s32[5]{0:T(128)} %stack.23.me_ref, bf16[8,16,16,256]{3,2,1,0:T(8,128)(2,1)} %bitcast.8.att_ref, bf16[256,2304]{1,0:T(8,128)(2,1)} %copy-done, bf16[256,2304]{1,0:T(8,128)(2,1)} %collective-permute-done.6.refs_1_, bf16[256,2304]{1,0:T(8,128)(2,1)} %collective-permute-done.7.refs_2_, ...), custom_call_target="tpu_custom_call" | custom-call | flops 1000 | bytes 5 | tf_op jit(solution)/shard_map/project/pallas_call | solution.py:165
  (30 shorter events, 0.1 us)
Async XLA Ops:
  4.5 37.4 %all-to-all-start = ((bf16[8,272,512]{2,1,0:T(8,128)(2,1)}), bf16[8,272,512]{2,1,0:T(8,128)(2,1)S(1)}, u32[]{:S(2)}, u32[]{:S(2)}) async-start(bf16[8,272,512]{2,1,0:T(8,128)(2,1)} %pack.1), calls=%async_computation | async-start | bytes 4456448 | tf_op jit(solution)/shard_map/all_to_all | solution.py:288
  13.0 48.7 %collective-permute-start.10 = (bf16[256,2304]{1,0:T(8,128)(2,1)}, bf16[256,2304]{1,0:T(8,128)(2,1)S(1)}, u32[]{:S(2)}, u32[]{:S(2)}) collective-permute-start(bf16[256,2304]{1,0:T(8,128)(2,1)} %bitcast.9.refs_0_), channel_id=1, source_target_pairs={{0,32},{32,64},{64,96},{96,0},{1,33},{33,65},{65,97},{97,1},{2,34}... | collective-permute-start | bytes 3538952 | tf_op jit(solution)/shard_map/ppermute | solution.py:255
  14.2 48.7 %collective-permute-start.11 = (bf16[256,2304]{1,0:T(8,128)(2,1)}, bf16[256,2304]{1,0:T(8,128)(2,1)}, u32[]{:S(2)}, u32[]{:S(2)}) collective-permute-start(bf16[256,2304]{1,0:T(8,128)(2,1)} %bitcast.9.refs_0_), channel_id=1, source_target_pairs={{0,96},{32,0},{64,32},{96,64},{1,97},{33,1},{65,33},{97,65},{2,98}... | collective-permute-start | bytes 3538952 | tf_op jit(solution)/shard_map/ppermute | solution.py:255
  41.9 1.4 copy-start.4
  52.2 4.4 %copy-start.9 = (f32[16,2304]{1,0:T(8,128)S(1)}, f32[16,2304]{1,0:T(8,128)}, u32[]{:S(2)}) copy-start(f32[16,2304]{1,0:T(8,128)} %weight_ref.1) | copy-start | bytes 442372
  52.2 22.3 %all-to-all-start.1 = ((bf16[8,256,256]{2,1,0:T(8,128)(2,1)}), bf16[8,256,256]{2,1,0:T(8,128)(2,1)}, u32[]{:S(2)}, u32[]{:S(2)}) async-start(bf16[8,256,256]{2,1,0:T(8,128)(2,1)} %attend.1), calls=%async_computation.1 | async-start | bytes 2097152 | tf_op jit(solution)/shard_map/all_to_all | solution.py:292
  56.6 17.9 %collective-permute-start = (bf16[16,2304]{1,0:T(8,128)(2,1)S(1)}, bf16[16,2304]{1,0:T(8,128)(2,1)S(1)}, u32[]{:S(2)}, u32[]{:S(2)}) collective-permute-start(bf16[16,2304]{1,0:T(8,128)(2,1)S(1)} %convert_element_type.3), channel_id=1, source_target_pairs={{0,16},{16,1},{1,17},{17,0},{2,18},{18,3},{3,19},{19,2},{4,20},{20... | collective-permute-start | bytes 221192 | tf_op jit(solution)/shard_map/ppermute | solution.py:278
  58.2 16.3 %collective-permute-start.1 = (bf16[16,2304]{1,0:T(8,128)(2,1)S(1)}, bf16[16,2304]{1,0:T(8,128)(2,1)S(1)}, u32[]{:S(2)}, u32[]{:S(2)}) collective-permute-start(bf16[16,2304]{1,0:T(8,128)(2,1)S(1)} %convert_element_type.3), channel_id=1, source_target_pairs={{0,1},{16,17},{1,0},{17,16},{2,3},{18,19},{3,2},{19,18},{4,5},{20,... | collective-permute-start | bytes 221192 | tf_op jit(solution)/shard_map/ppermute | solution.py:278
  61.6 12.8 %collective-permute-start.2 = (bf16[16,2304]{1,0:T(8,128)(2,1)S(1)}, bf16[16,2304]{1,0:T(8,128)(2,1)S(1)}, u32[]{:S(2)}, u32[]{:S(2)}) collective-permute-start(bf16[16,2304]{1,0:T(8,128)(2,1)S(1)} %convert_element_type.3), channel_id=1, source_target_pairs={{0,17},{16,0},{1,16},{17,1},{2,19},{18,2},{3,18},{19,3},{4,21},{20... | collective-permute-start | bytes 221192 | tf_op jit(solution)/shard_map/ppermute | solution.py:278
  61.6 19.9 %copy-start.3 = (bf16[256,2304]{1,0:T(8,128)(2,1)}, bf16[256,2304]{1,0:T(8,128)(2,1)S(1)}, u32[]{:S(2)}) copy-start(bf16[256,2304]{1,0:T(8,128)(2,1)S(1)} %collective-permute-done.10.refs_1_) | copy-start | bytes 3538948
  61.7 20.4 %collective-permute-start.12 = (bf16[128,2304]{1,0:T(8,128)(2,1)S(1)}, bf16[128,2304]{1,0:T(8,128)(2,1)}, u32[]{:S(2)}, u32[]{:S(2)}) collective-permute-start(bf16[128,2304]{1,0:T(8,128)(2,1)S(1)} %slice.18), channel_id=1, source_target_pairs={{0,32},{32,64},{64,96},{96,0},{1,33},{33,65},{65,97},{97,1},{2,34}... | collective-permute-start | bytes 1769480 | tf_op jit(solution)/shard_map/ppermute | solution.py:255
  64.8 17.3 %collective-permute-start.13 = (bf16[128,2304]{1,0:T(8,128)(2,1)}, bf16[128,2304]{1,0:T(8,128)(2,1)}, u32[]{:S(2)}, u32[]{:S(2)}) collective-permute-start(bf16[128,2304]{1,0:T(8,128)(2,1)} %slice.19), channel_id=1, source_target_pairs={{0,96},{32,0},{64,32},{96,64},{1,97},{33,1},{65,33},{97,65},{2,98}... | collective-permute-start | bytes 1769480 | tf_op jit(solution)/shard_map/ppermute | solution.py:255
  74.5 23.4 %copy-start.7 = (bf16[64,2304]{1,0:T(8,128)(2,1)}, bf16[64,2304]{1,0:T(8,128)(2,1)S(1)}, u32[]{:S(2)}) copy-start(bf16[64,2304]{1,0:T(8,128)(2,1)S(1)} %pad_maximum_fusion.1) | copy-start | bytes 884740
  74.5 10.1 %collective-permute-start.3 = (bf16[64,2304]{1,0:T(8,128)(2,1)S(1)}, bf16[64,2304]{1,0:T(8,128)(2,1)S(1)}, u32[]{:S(2)}, u32[]{:S(2)}) collective-permute-start(bf16[64,2304]{1,0:T(8,128)(2,1)S(1)} %pad_maximum_fusion.1), channel_id=1, source_target_pairs={{0,2},{2,4},{4,6},{6,0},{1,3},{3,5},{5,7},{7,1},{8,10},{10,12},{12... | collective-permute-start | bytes 884744 | tf_op jit(solution)/shard_map/ppermute | solution.py:255
  75.8 24.5 %all-to-all-start.2 = ((bf16[8,256,256]{2,1,0:T(8,128)(2,1)}), bf16[8,256,256]{2,1,0:T(8,128)(2,1)S(1)}, u32[]{:S(2)}, u32[]{:S(2)}) async-start(bf16[8,256,256]{2,1,0:T(8,128)(2,1)} %all-to-all-done.1), calls=%async_computation.2 | async-start | bytes 2097152 | tf_op jit(solution)/shard_map/all_to_all | solution.py:297
  81.6 22.4 %collective-permute-start.15 = (bf16[256,2304]{1,0:T(8,128)(2,1)S(1)}, bf16[256,2304]{1,0:T(8,128)(2,1)}, u32[]{:S(2)}, u32[]{:S(2)}) collective-permute-start(bf16[256,2304]{1,0:T(8,128)(2,1)S(1)} %collective-permute-done.10.refs_1_), channel_id=1, source_target_pairs={{0,8},{8,0},{1,9},{9,1},{2,10},{10,2},{3,11},{11,3},{4,12},{12,4},... | collective-permute-start | bytes 3538952 | tf_op jit(solution)/shard_map/ppermute | solution.py:255
  81.6 22.3 %collective-permute-start.16 = (bf16[256,2304]{1,0:T(8,128)(2,1)}, bf16[256,2304]{1,0:T(8,128)(2,1)}, u32[]{:S(2)}, u32[]{:S(2)}) collective-permute-start(bf16[256,2304]{1,0:T(8,128)(2,1)} %collective-permute-done.11.refs_2_), channel_id=1, source_target_pairs={{0,8},{8,0},{1,9},{9,1},{2,10},{10,2},{3,11},{11,3},{4,12},{12,4},... | collective-permute-start | bytes 3538952 | tf_op jit(solution)/shard_map/ppermute | solution.py:255
  82.1 21.8 %collective-permute-start.14 = (bf16[256,2304]{1,0:T(8,128)(2,1)}, bf16[256,2304]{1,0:T(8,128)(2,1)}, u32[]{:S(2)}, u32[]{:S(2)}) collective-permute-start(bf16[256,2304]{1,0:T(8,128)(2,1)} %bitcast.9.refs_0_), channel_id=1, source_target_pairs={{0,8},{8,0},{1,9},{9,1},{2,10},{10,2},{3,11},{11,3},{4,12},{12,4},... | collective-permute-start | bytes 3538952 | tf_op jit(solution)/shard_map/ppermute | solution.py:255
  82.2 9.7 %collective-permute-start.4 = (bf16[64,2304]{1,0:T(8,128)(2,1)S(1)}, bf16[64,2304]{1,0:T(8,128)(2,1)S(1)}, u32[]{:S(2)}, u32[]{:S(2)}) collective-permute-start(bf16[64,2304]{1,0:T(8,128)(2,1)S(1)} %pad_maximum_fusion.1), channel_id=1, source_target_pairs={{0,4},{2,6},{4,0},{6,2},{1,5},{3,7},{5,1},{7,3},{8,12},{10,14},{12... | collective-permute-start | bytes 884744 | tf_op jit(solution)/shard_map/ppermute | solution.py:255
  84.6 13.3 %copy-start.8 = (bf16[64,2304]{1,0:T(8,128)(2,1)}, bf16[64,2304]{1,0:T(8,128)(2,1)S(1)}, u32[]{:S(2)}) copy-start(bf16[64,2304]{1,0:T(8,128)(2,1)S(1)} %collective-permute-done.3) | copy-start | bytes 884740
  84.6 13.3 %collective-permute-start.5 = (bf16[64,2304]{1,0:T(8,128)(2,1)S(1)}, bf16[64,2304]{1,0:T(8,128)(2,1)S(1)}, u32[]{:S(2)}, u32[]{:S(2)}) collective-permute-start(bf16[64,2304]{1,0:T(8,128)(2,1)S(1)} %pad_maximum_fusion.1), channel_id=1, source_target_pairs={{0,6},{2,0},{4,2},{6,4},{1,7},{3,1},{5,3},{7,5},{8,14},{10,8},{12,... | collective-permute-start | bytes 884744 | tf_op jit(solution)/shard_map/ppermute | solution.py:255
  91.8 8.5 %collective-permute-start.17 = (bf16[128,2304]{1,0:T(8,128)(2,1)}, bf16[128,2304]{1,0:T(8,128)(2,1)}, u32[]{:S(2)}, u32[]{:S(2)}) collective-permute-start(bf16[128,2304]{1,0:T(8,128)(2,1)} %collective-permute-done.12.refs_3_), channel_id=1, source_target_pairs={{0,8},{8,0},{1,9},{9,1},{2,10},{10,2},{3,11},{11,3},{4,12},{12,4},... | collective-permute-start | bytes 1769480 | tf_op jit(solution)/shard_map/ppermute | solution.py:255
  97.9 5.4 %collective-permute-start.18 = (bf16[128,2304]{1,0:T(8,128)(2,1)}, bf16[128,2304]{1,0:T(8,128)(2,1)}, u32[]{:S(2)}, u32[]{:S(2)}) collective-permute-start(bf16[128,2304]{1,0:T(8,128)(2,1)} %collective-permute-done.13.refs_4_), channel_id=1, source_target_pairs={{0,8},{8,0},{1,9},{9,1},{2,10},{10,2},{3,11},{11,3},{4,12},{12,4},... | collective-permute-start | bytes 1769480 | tf_op jit(solution)/shard_map/ppermute | solution.py:255
  100.3 50.4 %copy-start = (bf16[256,2304]{1,0:T(8,128)(2,1)}, bf16[256,2304]{1,0:T(8,128)(2,1)S(1)}, u32[]{:S(2)}) copy-start(bf16[256,2304]{1,0:T(8,128)(2,1)S(1)} %pad_maximum_fusion.refs_0_) | copy-start | bytes 3538948
  100.3 3.6 %copy-start.2 = (bf16[8,256,256]{2,1,0:T(8,128)(2,1)}, bf16[8,256,256]{2,1,0:T(8,128)(2,1)S(1)}, u32[]{:S(2)}) copy-start(bf16[8,256,256]{2,1,0:T(8,128)(2,1)S(1)} %all-to-all-done.2.att_ref) | copy-start | bytes 3145732
  100.3 28.3 %collective-permute-start.7 = (bf16[256,2304]{1,0:T(8,128)(2,1)S(1)}, bf16[256,2304]{1,0:T(8,128)(2,1)}, u32[]{:S(2)}, u32[]{:S(2)}) collective-permute-start(bf16[256,2304]{1,0:T(8,128)(2,1)S(1)} %pad_maximum_fusion.refs_0_), channel_id=1, source_target_pairs={{0,96},{32,0},{64,32},{96,64},{1,97},{33,1},{65,33},{97,65},{2,98}... | collective-permute-start | bytes 3538952 | tf_op jit(solution)/shard_map/ppermute | solution.py:255
  103.3 30.8 %collective-permute-start.6 = (bf16[256,2304]{1,0:T(8,128)(2,1)S(1)}, bf16[256,2304]{1,0:T(8,128)(2,1)}, u32[]{:S(2)}, u32[]{:S(2)}) collective-permute-start(bf16[256,2304]{1,0:T(8,128)(2,1)S(1)} %pad_maximum_fusion.refs_0_), channel_id=1, source_target_pairs={{0,32},{32,64},{64,96},{96,0},{1,33},{33,65},{65,97},{97,1},{2,34}... | collective-permute-start | bytes 3538952 | tf_op jit(solution)/shard_map/ppermute | solution.py:255
  112.1 23.9 %all-to-all-start.3 = ((bf16[16,16,2304]{2,1,0:T(8,128)(2,1)}), bf16[16,16,2304]{2,1,0:T(8,128)(2,1)S(1)}, u32[]{:S(2)}, u32[]{:S(2)}) async-start(bf16[16,16,2304]{2,1,0:T(8,128)(2,1)} %gradient_rows.1), calls=%async_computation.3 | async-start | bytes 2359296 | tf_op jit(solution)/shard_map/all_to_all | solution.py:306
  130.6 21.4 %collective-permute-start.9 = (bf16[128,2304]{1,0:T(8,128)(2,1)}, bf16[128,2304]{1,0:T(8,128)(2,1)}, u32[]{:S(2)}, u32[]{:S(2)}) collective-permute-start(bf16[128,2304]{1,0:T(8,128)(2,1)} %slice.17), channel_id=1, source_target_pairs={{0,96},{32,0},{64,32},{96,64},{1,97},{33,1},{65,33},{97,65},{2,98}... | collective-permute-start | bytes 1769480 | tf_op jit(solution)/shard_map/ppermute | solution.py:255
  136.1 24.4 %collective-permute-start.8 = (bf16[128,2304]{1,0:T(8,128)(2,1)}, bf16[128,2304]{1,0:T(8,128)(2,1)}, u32[]{:S(2)}, u32[]{:S(2)}) collective-permute-start(bf16[128,2304]{1,0:T(8,128)(2,1)} %slice.16), channel_id=1, source_target_pairs={{0,32},{32,64},{64,96},{96,0},{1,33},{33,65},{65,97},{97,1},{2,34}... | collective-permute-start | bytes 1769480 | tf_op jit(solution)/shard_map/ppermute | solution.py:255
  136.1 1.0 copy-start.1
  139.3 21.5 %collective-permute-start.24 = (f32[16,2304]{1,0:T(8,128)}, f32[16,2304]{1,0:T(8,128)}, u32[]{:S(2)}, u32[]{:S(2)}) collective-permute-start(f32[16,2304]{1,0:T(8,128)} %get-tuple-element.40), channel_id=1, source_target_pairs={{0,0},{8,16},{16,8},{24,24},{1,1},{9,17},{17,9},{25,25},{2,2},{10,... | collective-permute-start | bytes 442376 | tf_op jit(solution)/shard_map/ppermute | solution.py:309
  142.9 17.5 %all-to-all-start.4 = ((f32[128,1,128]{2,1,0:T(1,128)}), f32[128,1,128]{2,1,0:T(1,128)}, u32[]{:S(2)}, u32[]{:S(2)}) async-start(f32[128,1,128]{2,1,0:T(1,128)} %get-tuple-element.37), calls=%async_computation.4 | async-start | bytes 131072 | tf_op jit(solution)/shard_map/all_to_all | solution.py:310
  150.7 13.3 %collective-permute-start.19 = (bf16[256,2304]{1,0:T(8,128)(2,1)S(1)}, bf16[256,2304]{1,0:T(8,128)(2,1)S(1)}, u32[]{:S(2)}, u32[]{:S(2)}) collective-permute-start(bf16[256,2304]{1,0:T(8,128)(2,1)S(1)} %pad_maximum_fusion.refs_0_), channel_id=1, source_target_pairs={{0,8},{8,0},{1,9},{9,1},{2,10},{10,2},{3,11},{11,3},{4,12},{12,4},... | collective-permute-start | bytes 3538952 | tf_op jit(solution)/shard_map/ppermute | solution.py:255
  151.9 12.1 %collective-permute-start.21 = (bf16[256,2304]{1,0:T(8,128)(2,1)}, bf16[256,2304]{1,0:T(8,128)(2,1)S(1)}, u32[]{:S(2)}, u32[]{:S(2)}) collective-permute-start(bf16[256,2304]{1,0:T(8,128)(2,1)} %collective-permute-done.7.refs_2_), channel_id=1, source_target_pairs={{0,8},{8,0},{1,9},{9,1},{2,10},{10,2},{3,11},{11,3},{4,12},{12,4},... | collective-permute-start | bytes 3538952 | tf_op jit(solution)/shard_map/ppermute | solution.py:255
  152.0 12.0 %collective-permute-start.20 = (bf16[256,2304]{1,0:T(8,128)(2,1)}, bf16[256,2304]{1,0:T(8,128)(2,1)}, u32[]{:S(2)}, u32[]{:S(2)}) collective-permute-start(bf16[256,2304]{1,0:T(8,128)(2,1)} %collective-permute-done.6.refs_1_), channel_id=1, source_target_pairs={{0,8},{8,0},{1,9},{9,1},{2,10},{10,2},{3,11},{11,3},{4,12},{12,4},... | collective-permute-start | bytes 3538952 | tf_op jit(solution)/shard_map/ppermute | solution.py:255
  160.4 3.6 %collective-permute-start.23 = (bf16[128,2304]{1,0:T(8,128)(2,1)}, bf16[128,2304]{1,0:T(8,128)(2,1)}, u32[]{:S(2)}, u32[]{:S(2)}) collective-permute-start(bf16[128,2304]{1,0:T(8,128)(2,1)} %collective-permute-done.9.refs_4_), channel_id=1, source_target_pairs={{0,8},{8,0},{1,9},{9,1},{2,10},{10,2},{3,11},{11,3},{4,12},{12,4},... | collective-permute-start | bytes 1769480 | tf_op jit(solution)/shard_map/ppermute | solution.py:255
  160.8 3.2 %collective-permute-start.22 = (bf16[128,2304]{1,0:T(8,128)(2,1)}, bf16[128,2304]{1,0:T(8,128)(2,1)}, u32[]{:S(2)}, u32[]{:S(2)}) collective-permute-start(bf16[128,2304]{1,0:T(8,128)(2,1)} %collective-permute-done.8.refs_3_), channel_id=1, source_target_pairs={{0,8},{8,0},{1,9},{9,1},{2,10},{10,2},{3,11},{11,3},{4,12},{12,4},... | collective-permute-start | bytes 1769480 | tf_op jit(solution)/shard_map/ppermute | solution.py:255
  164.0 1.1 copy-start.5
  164.0 1.4 copy-start.6
